TPU v7x, 512 devices: a whole 4x4x16 slice. The times are simulated.
512 devices in a mesh: pb: 16 (over y, x_hi, core), ma: 32 (over z, x_lo).
Axes of the slice: x: 4 (x_hi: 2, x_lo: 2; x = x_hi * 2 + x_lo), y: 4, z: 16, core: 2. Of those that a mesh axis runs over, the one named last changes fastest.
Arguments:
- queries: bfloat16 [1, 4096, 2048], P(None, ('pb', 'ma')), may hold values from -6 to 6
- map_descriptors: bfloat16 [32768, 2048], P('ma', 'pb'), may hold values from -0.125 to 0.125
- slopes: int32 [8], replicated, may hold values from 0 to 15, as said below
Outputs:
- best: float32 [1, 4096, 32768], P(None, 'pb', 'ma')
Inputs may be any that keep to these rules, and one draw needn't show every extreme that they name: `slopes`: 8 distinct velocities; the largest is exactly 15.
All inputs are finite; a program needn't handle non-finite values.
Results may differ from a plain program's by a relative error of at most 0.0003.
Values may be sent and summed in bfloat16 or wider, within the bound.
No kernel may reach another device: no remote copies, remote signals or barrier semaphores. Data moves between devices by JAX's collectives and lax.ppermute only.
A program may use at most 64 MiB of HBM per device.

v0:
```python
import math

import jax
import jax.numpy as jnp
from jax import lax
from jax.sharding import PartitionSpec as P

SEQ = 20
RAD = 10
SPAN = 285


def padded(value, sides, width):
    for axis, dim in sides:
        peers, length = (lax.axis_size(axis), value.shape[dim])
        up = [(i, (i + 1) % peers) for i in range(peers - 1)]
        down = [(j, i) for i, j in up]
        last = lax.slice_in_dim(value, length - width, length, axis=dim)
        leading = lax.slice_in_dim(value, 0, width, axis=dim)
        before = lax.ppermute(last, axis, up)
        after = lax.ppermute(leading, axis, down)
        value = jnp.concatenate([before, value, after], axis=dim)
    return value


def passed_along(value, axis, by):
    peers = lax.axis_size(axis)
    pairs = [(i, i + by) for i in range(peers) if 0 <= i + by < peers]
    return lax.ppermute(value, axis, pairs)


def score_tile(queries, map_descriptors):
    query_full = lax.all_gather(queries, "ma", axis=1, tiled=True)
    return jnp.einsum(
        "sqd,md->sqm",
        query_full,
        lax.all_gather(map_descriptors, "pb", axis=1, tiled=True),
        preferred_element_type=jnp.float32,
    )


def contrast(extended, columns):
    shape_out = (extended.shape[0], extended.shape[1], columns)
    running = jnp.zeros(shape_out, jnp.float32)
    squares = jnp.zeros(shape_out, jnp.float32)
    for offset in range(2 * RAD + 1):
        window = extended[:, :, offset : offset + columns]
        running = running + window
        squares = squares + window * window
    average = running / (2 * RAD + 1)
    spread = squares / (2 * RAD + 1) - average * average
    centre = extended[:, :, RAD : RAD + columns]
    return (centre - average) / jnp.sqrt(spread + 1.0)


def sequence_best(normal_ext, slopes, q_count, m_count):
    sessions = normal_ext.shape[0]
    best_val = None
    for slope_index in range(slopes.shape[0]):
        velocity = slopes[slope_index]
        summed = jnp.zeros((sessions, q_count, m_count), jnp.float32)
        for lag_step in range(SEQ):
            row_at = jnp.asarray(SEQ - 1 - lag_step, jnp.int32)
            col_at = SPAN - lag_step * velocity
            zero_at = jnp.asarray(0, jnp.int32)
            summed = summed + lax.dynamic_slice(
                normal_ext, (zero_at, row_at, col_at), (sessions, q_count, m_count)
            )
        best_val = summed if best_val is None else jnp.maximum(best_val, summed)
    return best_val / math.sqrt(SEQ)


def local(queries, map_descriptors, slopes):
    m_count = map_descriptors.shape[0]
    lead_rows = SEQ - 1
    scores = score_tile(queries, map_descriptors)
    q_count = scores.shape[1]
    widened = padded(scores, (("ma", 2),), RAD)
    normal = contrast(widened, m_count)
    before = passed_along(normal[:, :, m_count - SPAN :], "ma", 1)
    normal_ext = jnp.concatenate([before, normal], axis=2)
    above = passed_along(normal_ext[:, q_count - lead_rows :], "pb", 1)
    normal_ext = jnp.concatenate([above, normal_ext], axis=1)
    return sequence_best(normal_ext, slopes, q_count, m_count)


def solution(mesh):
    return jax.shard_map(
        local,
        mesh=mesh,
        in_specs=(P(None, ("pb", "ma"), None), P("ma", "pb"), P()),
        out_specs=P(None, "pb", "ma"),
        check_vma=False,
    )
```

profile of v0, /device:TPU:104, one launch (start us, length us, event | category | flops | bytes accessed | tf_op | source)
XLA Modules:
  0.0 506.0 jit_solution(8209121053983662750)
XLA Ops:
  6.5 0.0 all-gather.3.cloned.1.call-start
  6.5 0.7 all-gather.3.cloned.1.call-update
  7.3 0.0 all-gather.5.cloned.1.call-start
  7.3 0.7 all-gather.5.cloned.1.call-update
  8.0 134.3 %all-gather.3.cloned.1.call-done = bf16[1,256,2048]{2,1,0:T(8,128)(2,1)} async-done(((bf16[1,8,2048]{2,1,0:T(8,128)(2,1)}), bf16[1,256,2048]{2,1,0:T(8,128)(2,1)}) %all-gather.3.cloned.1.call-update) | async-done | bytes 1048592 | tf_op jit(solution)/shard_map/all_gather | solution.py:33
  142.3 74.3 %all-gather.5.cloned.1.call-done = bf16[1024,2048]{1,0:T(8,128)(2,1)} async-done(((bf16[1024,128]{1,0:T(8,128)(2,1)}), bf16[1024,2048]{1,0:T(8,128)(2,1)}) %all-gather.5.cloned.1.call-update) | async-done | bytes 4194320 | tf_op jit(solution)/shard_map/all_gather | solution.py:37
  216.5 3.8 fusion.345
  220.3 0.1 fusion.348
  220.4 2.5 collective-permute-start
  222.9 0.0 copy-start
  222.9 4.3 collective-permute-start.1
  227.2 1.7 collective-permute-done
  228.9 3.2 collective-permute-done.1
  232.1 7.6 %fusion.344 = f32[1,256,1024]{2,1,0:T(8,128)S(1)} fusion(f32[256,1024]{1,0:T(8,128)S(1)} %fusion.345, f32[1,256,1024]{2,1,0:T(8,128)S(1)} %bitcast.342, f32[1,256,10]{2,1,0:T(8,128)S(1)} %collective-permute-done.1, f32[1,256,10]{2,1,0:T(8,128)S(1)} %collective-permute-done), kind=kLoop, calls=%fused_computation.538 | loop fusion | flops 23068672 | bytes 3166208 | tf_op jit(solution)/shard_map/div | solution.py:53
  239.7 0.2 slice.186
  239.9 5.8 %collective-permute-start.2 = (f32[1,256,285]{2,1,0:T(8,128)S(1)}, f32[1,256,285]{2,1,0:T(8,128)S(1)}, u32[]{:S(2)}, u32[]{:S(2)}) collective-permute-start(f32[1,256,285]{2,1,0:T(8,128)S(1)} %slice.186), channel_id=1, source_target_pairs={{0,1},{1,2},{2,3},{3,4},{4,5},{5,6},{6,7},{7,8},{8,9},{9,10},{10,1... | collective-permute-start | bytes 875528 | tf_op jit(solution)/shard_map/ppermute | solution.py:29
  245.6 0.0 copy-done
  245.6 0.7 fusion.349
  349.1 0.0 collective-permute-done.2
  349.1 0.1 fusion.347
  349.2 1.9 collective-permute-start.3
  351.1 0.4 pad_maximum_fusion
  351.5 6.4 %collective-permute-done.3 = f32[1,19,1309]{2,1,0:T(8,128)S(1)} collective-permute-done((f32[1,19,1309]{2,1,0:T(8,128)S(1)}, f32[1,19,1309]{2,1,0:T(8,128)S(1)}, u32[]{:S(2)}, u32[]{:S(2)}) %collective-permute-start.3) | collective-permute-done | bytes 99516 | tf_op jit(solution)/shard_map/ppermute | solution.py:29
  357.9 141.2 %fusion.21 = f32[1,256,1024]{2,1,0:T(8,128)} fusion(s32[]{:T(128)S(6)} %select_n.607, f32[1,19,1309]{2,1,0:T(8,128)S(1)} %collective-permute-done.3, f32[1,256,1024]{2,1,0:T(8,128)S(1)} %fusion.344, s32[]{:T(128)S(6)} %select_n.532, s32[]{:T(128)S(6)} %select_n.533, s32[]{:T(128)S(6)} %select_n.534, s32[]{:T(128)S(6)} %select_n.535, s32[]{:T(128)S(6)} %select_n.536, ...), kind=kLoop, calls=%fused_computation.212 | loop fusion | flops 81788928 | bytes 3537660 | tf_op jit(solution)/shard_map/div | solution.py:70
Async XLA Ops:
  6.5 135.7 %all-gather.3.cloned.1.call-start = ((), (), s32[]{:S(2)}) async-start(), calls=%async_computation | async-start | bytes 1081344 | tf_op jit(solution)/shard_map/all_gather | solution.py:33
  7.3 209.3 %all-gather.5.cloned.1.call-start = ((), (), s32[]{:S(2)}) async-start(), calls=%async_computation.1 | async-start | bytes 4456448 | tf_op jit(solution)/shard_map/all_gather | solution.py:37
  220.4 8.5 %collective-permute-start = (f32[1,256,10]{2,1,0:T(8,128)S(1)}, f32[1,256,10]{2,1,0:T(8,128)S(1)}, u32[]{:S(2)}, u32[]{:S(2)}) collective-permute-start(f32[1,256,10]{2,1,0:T(8,128)S(1)} %get-tuple-element.5), channel_id=1, source_target_pairs={{0,1},{1,2},{2,3},{3,4},{4,5},{5,6},{6,7},{7,8},{8,9},{9,10},{10,1... | collective-permute-start | bytes 30728 | tf_op jit(solution)/shard_map/ppermute | solution.py:20
  222.9 22.7 %copy-start = (s32[8]{0:T(128)S(1)}, s32[8]{0:T(128)}, u32[]{:S(2)}) copy-start(s32[8]{0:T(128)} %param.5) | copy-start | bytes 100
  222.9 9.2 %collective-permute-start.1 = (f32[1,256,10]{2,1,0:T(8,128)S(1)}, f32[1,256,10]{2,1,0:T(8,128)S(1)}, u32[]{:S(2)}, u32[]{:S(2)}) collective-permute-start(f32[1,256,10]{2,1,0:T(8,128)S(1)} %get-tuple-element.6), channel_id=1, source_target_pairs={{1,0},{2,1},{3,2},{4,3},{5,4},{6,5},{7,6},{8,7},{9,8},{10,9},{11,1... | collective-permute-start | bytes 30728 | tf_op jit(solution)/shard_map/ppermute | solution.py:21
  239.9 109.2 %collective-permute-start.2 = (f32[1,256,285]{2,1,0:T(8,128)S(1)}, f32[1,256,285]{2,1,0:T(8,128)S(1)}, u32[]{:S(2)}, u32[]{:S(2)}) collective-permute-start(f32[1,256,285]{2,1,0:T(8,128)S(1)} %slice.186), channel_id=1, source_target_pairs={{0,1},{1,2},{2,3},{3,4},{4,5},{5,6},{6,7},{7,8},{8,9},{9,10},{10,1... | collective-permute-start | bytes 875528 | tf_op jit(solution)/shard_map/ppermute | solution.py:29
  349.2 8.7 %collective-permute-start.3 = (f32[1,19,1309]{2,1,0:T(8,128)S(1)}, f32[1,19,1309]{2,1,0:T(8,128)S(1)}, u32[]{:S(2)}, u32[]{:S(2)}) collective-permute-start(f32[1,19,1309]{2,1,0:T(8,128)S(1)} %fusion.347), channel_id=1, source_target_pairs={{0,32},{32,64},{64,96},{96,128},{128,160},{160,192},{192,224},{224... | collective-permute-start | bytes 298460 | tf_op jit(solution)/shard_map/ppermute | solution.py:29
Sparse Core Ops, SparseCore 0:
  9.4 132.7 all-gather.2
  145.5 71.0 all-gather.4
where the time goes:
time: 508 us; the launch traced here: 506 us
  waiting for transfers between devices  221 us (44%)
  other arithmetic  149 us (29%)
  between operations  116 us (23%)
  starting transfers between devices  14.5 us (3%)
    div x1, other arithmetic, sequence_best(): return best_val / math.sqrt(SEQ)  141 us
    all_gather x1, waiting for transfers between devices, score_tile(): query_full = lax.all_gather(queries, 'ma', axis=1, tiled=True)  134 us
    all_gather x1, waiting for transfers between devices, score_tile(): lax.all_gather(map_descriptors, 'pb', axis=1, tiled=True)  74.3 us
  transfers between devices with their start and end apart: 6, of which 5 were waited for; matrix products, arithmetic and copies ran while one was open for 0% of the time, Pallas kernels for 0%

commit v1 on v0

v1 whole, which is shorter than its diff:
```python
import functools
import math

import jax
import jax.numpy as jnp
from jax import lax
from jax.experimental import pallas as pl
from jax.experimental.pallas import tpu as pltpu
from jax.sharding import PartitionSpec as P

SEQ = 20
RAD = 10
TOP = 32
LEFT = 384
RIGHT = 128
LANES = 128
CHIPS = 8

FAR = (4, 12, 8)
NEAR = (1, 15, 2)


def along_z(step, cross=0):
    return [
        (z * 2 + side, ((z + step) % 16) * 2 + (side ^ cross))
        for z in range(16)
        for side in range(2)
    ]


def gather_queries(queries):
    depth = queries.shape[-1]
    far = jnp.concatenate(
        [queries[None]] + [lax.ppermute(queries[None], "ma", along_z(k)) for k in FAR]
    )
    other = lax.ppermute(far, "ma", along_z(0, 1))
    side = lax.axis_index("ma") % 2
    first = jnp.where(side == 0, far, other)
    second = jnp.where(side == 0, other, far)
    pairs = jnp.concatenate([first, second], axis=1)
    parts = [pairs] + [lax.ppermute(pairs, "ma", along_z(k)) for k in NEAR]
    held = jnp.stack(parts)
    here = lax.axis_index("ma") // 2
    tail = []
    for z in (14, 15):
        near, far_at = place(z, here)
        tail.append(lax.dynamic_slice(held, (near, far_at, 0, 0), (1, 1, 16, depth)))
    tail = jnp.concatenate(tail).reshape(TOP, depth)
    above = lax.ppermute(tail, "pb", [(i, i + 1) for i in range(15)])
    return held, above


def place(z, here):
    delta = (z - here + 16) % 16
    low = delta % 4
    near = jnp.where(low == 0, 0, jnp.where(low == 3, 1, jnp.where(low == 1, 2, 3)))
    back = jnp.where(low == 0, 0, jnp.where(low == 3, -1, jnp.where(low == 1, 1, -2)))
    rest = ((delta - back + 16) % 16) // 4
    far = jnp.where(rest == 0, 0, jnp.where(rest == 3, 1, jnp.where(rest == 1, 2, 3)))
    return near.astype(jnp.int32), far.astype(jnp.int32)


def gather_map(frames):
    groups = [[2 * i + c for i in range(CHIPS)] for c in range(2)]
    copies = jnp.broadcast_to(frames[None], (CHIPS,) + frames.shape)
    own = lax.all_to_all(copies, "pb", 0, 0, axis_index_groups=groups)
    other = lax.ppermute(own, "pb", [(i, i ^ 1) for i in range(16)])
    return own, other


def score_kernel(at_ref, held_ref, above_ref, own_ref, other_ref, out_ref, left_ref, right_ref, rows_ref):
    rows_ref[:TOP] = above_ref[...]
    for z in range(16):
        rows_ref[TOP + 16 * z : TOP + 16 * z + 16] = held_ref[at_ref[2 * z], at_ref[2 * z + 1]]
    core = at_ref[32]
    columns = own_ref.shape[1]
    width = 256

    def block(n, carry):
        begin = pl.multiple_of(n * width, width)
        total = None
        for g in range(CHIPS):
            one = pl.multiple_of((2 * g + core) * LANES, LANES)
            two = pl.multiple_of((2 * g + 1 - core) * LANES, LANES)
            lhs = jnp.concatenate([rows_ref[:, pl.ds(one, LANES)], rows_ref[:, pl.ds(two, LANES)]], axis=1)
            rhs = jnp.concatenate([own_ref[g, pl.ds(begin, width)], other_ref[g, pl.ds(begin, width)]], axis=1)
            part = lax.dot_general(lhs, rhs, (((1,), (1,)), ((), ())), preferred_element_type=jnp.float32)
            total = part if total is None else total + part
        out_ref[:, pl.ds(begin, width)] = total
        return carry

    lax.fori_loop(0, columns // width, block, 0)
    left_ref[...] = out_ref[:, columns - LEFT :]
    right_ref[...] = out_ref[:, :RIGHT]


def score_tile(at, held, above, own, other):
    rows = TOP + 256
    columns = own.shape[1]
    return pl.pallas_call(
        score_kernel,
        name="scores",
        out_shape=(
            jax.ShapeDtypeStruct((rows, columns), jnp.float32),
            jax.ShapeDtypeStruct((rows, LEFT), jnp.float32),
            jax.ShapeDtypeStruct((rows, RIGHT), jnp.float32),
        ),
        in_specs=[pl.BlockSpec(memory_space=pltpu.SMEM)] + [pl.BlockSpec(memory_space=pltpu.VMEM)] * 4,
        out_specs=(pl.BlockSpec(memory_space=pltpu.VMEM),) * 3,
        scratch_shapes=[pltpu.VMEM((rows, 2048), jnp.bfloat16)],
        compiler_params=pltpu.CompilerParams(vmem_limit_bytes=32 << 20),
        cost_estimate=pl.CostEstimate(flops=2 * rows * columns * 2048, bytes_accessed=8 << 20, transcendentals=0),
    )(at, held, above, own, other)


def tile(c):
    return slice(c * LANES, (c + 1) * LANES)


def best_kernel(slopes_ref, left_ref, mid_ref, right_ref, out_ref, x_ref, two_ref, four_ref, eight_ref):
    rows = mid_ref.shape[0]
    columns = mid_ref.shape[1]
    halo = LEFT // LANES
    tiles = halo + columns // LANES
    first_map = slopes_ref[8] == 0
    step_rows = 96

    def source(c):
        if c < halo:
            return left_ref, c
        if c < tiles:
            return mid_ref, c - halo
        return right_ref, c - tiles

    def up(prev, cur, by, lane):
        return jnp.where(lane < LANES - by, pltpu.roll(prev, LANES - by, 1), pltpu.roll(cur, LANES - by, 1))

    def normalise(block, carry):
        begin = pl.multiple_of(block * 32, 32)
        take = pl.ds(begin, 32)
        lane = lax.broadcasted_iota(jnp.int32, (32, LANES), 1)

        def raw(c):
            ref, at = source(c)
            return ref[take, tile(at)]

        def chain(values):
            one = values
            two = [v + up(v, w, 1, lane) for v, w in zip(one, one[1:] + one[-1:])]
            four = [v + up(v, w, 2, lane) for v, w in zip(two, two[1:] + two[-1:])]
            eight = [v + up(v, w, 4, lane) for v, w in zip(four, four[1:] + four[-1:])]
            ten = [e + up(v, w, 8, lane) for e, v, w in zip(eight, two, two[1:] + two[-1:])]
            twenty = [v + up(v, w, 10, lane) for v, w in zip(ten, ten[1:] + ten[-1:])]
            return [t + up(v, w, 20, lane) for t, v, w in zip(twenty, one, one[1:] + one[-1:])]

        for c in range(tiles):
            near = [raw(max(c - 1, 0)), raw(c), raw(c + 1)]
            sums = chain(near)
            squares = chain([v * v for v in near])
            back = lambda v: jnp.where(lane < RAD, pltpu.roll(v[0], RAD, 1), pltpu.roll(v[1], RAD, 1))
            mean = back(sums) * (1.0 / (2 * RAD + 1))
            square = back(squares) * (1.0 / (2 * RAD + 1))
            value = (near[1] - mean) * lax.rsqrt(square - mean * mean + 1.0)
            if c < halo:
                value = jnp.where(first_map, 0.0, value)
            x_ref[take, tile(c)] = value
        return carry

    lax.fori_loop(0, rows // 32, normalise, 0)

    def shifted(ref, take, c, by, whole, lane, prev):
        at = c if whole is None else pl.multiple_of((c - whole) * LANES, LANES)
        cols = tile(c) if whole is None else pl.ds(at, LANES)
        cur = pltpu.roll(ref[take, cols], by, 1)
        return cur if prev is None else jnp.where(lane < by, prev, cur), cur

    def blocks(start):
        at = start
        while at < rows:
            size = min(64, rows - at)
            yield at, size
            at += size

    def stage(src, dst, lag, by, row0, col0):
        for at, size in blocks(row0):
            lane = lax.broadcasted_iota(jnp.int32, (size, LANES), 1)
            prev = None
            if col0 > 0:
                _, prev = shifted(src, slice(at - lag, at - lag + size), col0 - 1, by, None, lane, None)
            for c in range(col0, tiles):
                moved, prev = shifted(src, slice(at - lag, at - lag + size), c, by, None, lane, prev)
                dst[at : at + size, tile(c)] = src[at : at + size, tile(c)] + moved

    def per_slope(index, carry):
        v = slopes_ref[index]
        stage(x_ref, two_ref, 1, v, 8, 0)
        stage(two_ref, four_ref, 2, 2 * v, 16, 1)
        stage(four_ref, eight_ref, 4, 4 * v, 24, 2)
        by8 = 8 * v
        by16 = 16 * v
        whole = by16 // LANES
        by16 = by16 % LANES
        for at, size in blocks(TOP):
            lane = lax.broadcasted_iota(jnp.int32, (size, LANES), 1)
            take8 = slice(at - 8, at - 8 + size)
            take16 = slice(at - 16, at - 16 + size)
            _, prev8 = shifted(eight_ref, take8, halo - 1, by8, None, lane, None)
            _, prev16 = shifted(four_ref, take16, halo - 1, by16, whole, lane, None)
            for c in range(halo, tiles):
                moved8, prev8 = shifted(eight_ref, take8, c, by8, None, lane, prev8)
                moved16, prev16 = shifted(four_ref, take16, c, by16, whole, lane, prev16)
                total = (eight_ref[at : at + size, tile(c)] + moved8) + moved16
                out_rows = slice(at - TOP, at - TOP + size)
                kept = jnp.where(index == 0, total, jnp.maximum(out_ref[out_rows, tile(c - halo)], total))
                out_ref[out_rows, tile(c - halo)] = kept
        return carry

    lax.fori_loop(0, 8, per_slope, 0)
    out_ref[...] = out_ref[...] * (1.0 / math.sqrt(SEQ))


def best_of(slopes_and_place, left, mid, right):
    rows, columns = mid.shape
    scratch = pltpu.VMEM((rows, LEFT + columns), jnp.float32)
    return pl.pallas_call(
        best_kernel,
        name="best",
        out_shape=jax.ShapeDtypeStruct((rows - TOP, columns), jnp.float32),
        in_specs=[pl.BlockSpec(memory_space=pltpu.SMEM)] + [pl.BlockSpec(memory_space=pltpu.VMEM)] * 3,
        out_specs=pl.BlockSpec(memory_space=pltpu.VMEM),
        scratch_shapes=[scratch] * 4,
        compiler_params=pltpu.CompilerParams(vmem_limit_bytes=32 << 20),
        cost_estimate=pl.CostEstimate(flops=60 << 20, bytes_accessed=4 << 20, transcendentals=0),
    )(slopes_and_place, left, mid, right)


def local(queries, map_descriptors, slopes):
    ma = lax.axis_index("ma")
    pb = lax.axis_index("pb")
    held, above = gather_queries(queries[0])
    own, other = gather_map(map_descriptors)
    at = []
    for z in range(16):
        at.extend(place(z, ma // 2))
    at.append(pb % 2)
    at = jnp.stack([jnp.asarray(v, jnp.int32) for v in at])
    mid, last, lead = score_tile(at, held, above, own, other)
    left = lax.ppermute(last, "ma", [(i, i + 1) for i in range(31)])
    right = lax.ppermute(lead, "ma", [(i + 1, i) for i in range(31)])
    marks = jnp.concatenate([slopes, ma[None].astype(jnp.int32)])
    return best_of(marks, left, mid, right)[None]


def solution(mesh):
    return jax.shard_map(
        local,
        mesh=mesh,
        in_specs=(P(None, ("pb", "ma"), None), P("ma", "pb"), P()),
        out_specs=P(None, "pb", "ma"),
        check_vma=False,
    )
```

time: 508 us -> 178 us (0.35)
  the two profiles are of different devices: /device:TPU:104 before, /device:TPU:33 now
where the time goes in v1:
time: 178 us; the launch traced here: 177 us
  Pallas kernels  72.3 us (41%)
  starting transfers between devices  58.6 us (33%)
  waiting for transfers between devices  39.7 us (22%)
  local copies, waits for them, and re-layouts  3.45 us (2%)
  between operations  1.89 us (1%)
    pallas_call x1, Pallas kernels, best_of(): pl.pallas_call(best_kernel, name='best', out_shape=jax.ShapeDtypeStruct((...  68.5 us
    ppermute x3, starting transfers between devices, gather_queries(): lax.ppermute(queries[None], 'ma', along_z(k))  23.7 us
    ppermute x3, waiting for transfers between devices, gather_queries(): parts = [pairs] + [lax.ppermute(pairs, 'ma', along_z(k)) for k in NEAR]  19.9 us
    ppermute x3, starting transfers between devices, gather_queries(): parts = [pairs] + [lax.ppermute(pairs, 'ma', along_z(k)) for k in NEAR]  11.6 us
    ppermute x1, waiting for transfers between devices, local(): right = lax.ppermute(lead, 'ma', [(i + 1, i) for i in range(31)])  10.9 us
    all_to_all x1, starting transfers between devices, gather_map(): own = lax.all_to_all(copies, 'pb', 0, 0, axis_index_groups=groups)  6.78 us
    ppermute x1, waiting for transfers between devices, gather_queries(): other = lax.ppermute(far, 'ma', along_z(0, 1))  4.77 us
    ppermute x1, starting transfers between devices, gather_queries(): above = lax.ppermute(tail, 'pb', [(i, i + 1) for i in range(15)])  4.33 us
  transfers between devices with their start and end apart: 12, of which 6 were waited for; matrix products, arithmetic and copies ran while one was open for 1% of the time, Pallas kernels for 0%

profile of v1, /device:TPU:33, one launch (start us, length us, event | category | flops | bytes accessed | tf_op | source)
XLA Modules:
  0.0 177.3 jit_solution(16824989439491470091)
XLA Ops:
  0.0 2.6 %broadcast_in_dim.13 = bf16[8,1024,128]{2,1,0:T(8,128)(2,1)} broadcast(bf16[1024,128]{1,0:T(8,128)(2,1)} %param.4), dimensions={1,2} | broadcast | bytes 2359296 | tf_op jit(solution)/shard_map/broadcast_in_dim | solution.py:65
  2.6 0.0 copy-start.3
  2.6 6.8 %all-to-all-start = ((bf16[8,1024,128]{2,1,0:T(8,128)(2,1)}), bf16[8,1024,128]{2,1,0:T(8,128)(2,1)S(1)}, u32[]{:S(2)}, u32[]{:S(2)}) async-start(bf16[8,1024,128]{2,1,0:T(8,128)(2,1)} %broadcast_in_dim.13), calls=%async_computation | async-start | bytes 4194304 | tf_op jit(solution)/shard_map/all_to_all | solution.py:66
  9.3 0.0 copy-done.3
  9.3 11.6 %collective-permute-start.1 = (bf16[1,8,2048]{2,1,0:T(8,128)(2,1)S(1)}, bf16[1,8,2048]{2,1,0:T(8,128)(2,1)S(1)}, u32[]{:S(2)}, u32[]{:S(2)}) collective-permute-start(bf16[1,8,2048]{2,1,0:T(8,128)(2,1)S(1)} %copy-done.3), channel_id=1, source_target_pairs={{0,24},{1,25},{2,26},{3,27},{4,28},{5,29},{6,30},{7,31},{8,0},{9,1... | collective-permute-start | bytes 98312 | tf_op jit(solution)/shard_map/ppermute | solution.py:34
  20.9 1.9 %collective-permute-start = (bf16[1,8,2048]{2,1,0:T(8,128)(2,1)S(1)}, bf16[1,8,2048]{2,1,0:T(8,128)(2,1)S(1)}, u32[]{:S(2)}, u32[]{:S(2)}) collective-permute-start(bf16[1,8,2048]{2,1,0:T(8,128)(2,1)S(1)} %copy-done.3), channel_id=1, source_target_pairs={{0,8},{1,9},{2,10},{3,11},{4,12},{5,13},{6,14},{7,15},{8,16},{9,17... | collective-permute-start | bytes 98312 | tf_op jit(solution)/shard_map/ppermute | solution.py:34
  22.8 10.3 %collective-permute-start.2 = (bf16[1,8,2048]{2,1,0:T(8,128)(2,1)S(1)}, bf16[1,8,2048]{2,1,0:T(8,128)(2,1)S(1)}, u32[]{:S(2)}, u32[]{:S(2)}) collective-permute-start(bf16[1,8,2048]{2,1,0:T(8,128)(2,1)S(1)} %copy-done.3), channel_id=1, source_target_pairs={{0,16},{1,17},{2,18},{3,19},{4,20},{5,21},{6,22},{7,23},{8,24},{9,... | collective-permute-start | bytes 98312 | tf_op jit(solution)/shard_map/ppermute | solution.py:34
  33.1 0.0 collective-permute-done
  33.1 0.0 collective-permute-done.1
  33.2 3.7 %all-to-all-done.own_ref = bf16[8,1024,128]{2,1,0:T(8,128)(2,1)S(1)} async-done(((bf16[8,1024,128]{2,1,0:T(8,128)(2,1)}), bf16[8,1024,128]{2,1,0:T(8,128)(2,1)S(1)}, u32[]{:S(2)}, u32[]{:S(2)}) %all-to-all-start) | async-done | bytes 2097184 | tf_op jit(solution)/shard_map/all_to_all | solution.py:66
  36.9 3.8 %collective-permute-start.8 = (bf16[8,1024,128]{2,1,0:T(8,128)(2,1)S(1)}, bf16[8,1024,128]{2,1,0:T(8,128)(2,1)}, u32[]{:S(2)}, u32[]{:S(2)}) collective-permute-start(bf16[8,1024,128]{2,1,0:T(8,128)(2,1)S(1)} %all-to-all-done.own_ref), channel_id=1, source_target_pairs={{0,32},{32,0},{64,96},{96,64},{128,160},{160,128},{192,224},{224,1... | collective-permute-start | bytes 6291464 | tf_op jit(solution)/shard_map/ppermute | solution.py:67
  40.7 0.0 collective-permute-done.2
  40.7 2.2 %collective-permute-start.3 = (bf16[4,8,2048]{2,1,0:T(8,128)(2,1)S(1)}, bf16[4,8,2048]{2,1,0:T(8,128)(2,1)S(1)}, u32[]{:S(2)}, u32[]{:S(2)}) collective-permute-start(bf16[4,8,2048]{2,1,0:T(8,128)(2,1)S(1)} %constant_dynamic-update-slice_fusion), channel_id=1, source_target_pairs={{0,1},{1,0},{2,3},{3,2},{4,5},{5,4},{6,7},{7,6},{8,9},{9,8},{10,11... | collective-permute-start | bytes 393224 | tf_op jit(solution)/shard_map/ppermute | solution.py:36
  42.9 4.8 %collective-permute-done.3 = bf16[4,8,2048]{2,1,0:T(8,128)(2,1)S(1)} collective-permute-done((bf16[4,8,2048]{2,1,0:T(8,128)(2,1)S(1)}, bf16[4,8,2048]{2,1,0:T(8,128)(2,1)S(1)}, u32[]{:S(2)}, u32[]{:S(2)}) %collective-permute-start.3) | collective-permute-done | bytes 131104 | tf_op jit(solution)/shard_map/ppermute | solution.py:36
  47.8 1.9 %collective-permute-start.5 = (bf16[4,16,2048]{2,1,0:T(8,128)(2,1)S(1)}, bf16[4,16,2048]{2,1,0:T(8,128)(2,1)S(1)}, u32[]{:S(2)}, u32[]{:S(2)}) collective-permute-start(bf16[4,16,2048]{2,1,0:T(8,128)(2,1)S(1)} %get-tuple-element.14), channel_id=1, source_target_pairs={{0,30},{1,31},{2,0},{3,1},{4,2},{5,3},{6,4},{7,5},{8,6},{9,7},{10,... | collective-permute-start | bytes 786440 | tf_op jit(solution)/shard_map/ppermute | solution.py:41
  49.7 3.5 %collective-permute-start.4 = (bf16[4,16,2048]{2,1,0:T(8,128)(2,1)S(1)}, bf16[4,16,2048]{2,1,0:T(8,128)(2,1)S(1)}, u32[]{:S(2)}, u32[]{:S(2)}) collective-permute-start(bf16[4,16,2048]{2,1,0:T(8,128)(2,1)S(1)} %get-tuple-element.14), channel_id=1, source_target_pairs={{0,2},{1,3},{2,4},{3,5},{4,6},{5,7},{6,8},{7,9},{8,10},{9,11},{10,... | collective-permute-start | bytes 786440 | tf_op jit(solution)/shard_map/ppermute | solution.py:41
  53.3 6.1 %collective-permute-start.6 = (bf16[4,16,2048]{2,1,0:T(8,128)(2,1)S(1)}, bf16[4,16,2048]{2,1,0:T(8,128)(2,1)S(1)}, u32[]{:S(2)}, u32[]{:S(2)}) collective-permute-start(bf16[4,16,2048]{2,1,0:T(8,128)(2,1)S(1)} %get-tuple-element.14), channel_id=1, source_target_pairs={{0,4},{1,5},{2,6},{3,7},{4,8},{5,9},{6,10},{7,11},{8,12},{9,13},{1... | collective-permute-start | bytes 786440 | tf_op jit(solution)/shard_map/ppermute | solution.py:41
  59.6 0.0 collective-permute-done.5
  59.6 0.0 copy-start
  59.6 6.6 %collective-permute-done.4 = bf16[4,16,2048]{2,1,0:T(8,128)(2,1)S(1)} collective-permute-done((bf16[4,16,2048]{2,1,0:T(8,128)(2,1)S(1)}, bf16[4,16,2048]{2,1,0:T(8,128)(2,1)S(1)}, u32[]{:S(2)}, u32[]{:S(2)}) %collective-permute-start.4) | collective-permute-done | bytes 262176 | tf_op jit(solution)/shard_map/ppermute | solution.py:41
  66.2 0.0 copy-start.1
  66.2 13.3 %collective-permute-done.6 = bf16[4,16,2048]{2,1,0:T(8,128)(2,1)S(1)} collective-permute-done((bf16[4,16,2048]{2,1,0:T(8,128)(2,1)S(1)}, bf16[4,16,2048]{2,1,0:T(8,128)(2,1)S(1)}, u32[]{:S(2)}, u32[]{:S(2)}) %collective-permute-start.6) | collective-permute-done | bytes 262176 | tf_op jit(solution)/shard_map/ppermute | solution.py:41
  79.5 0.0 copy-start.2
  79.5 0.0 copy-done
  79.5 0.0 copy-done.1
  79.5 0.7 copy-done.2
  80.2 1.2 pad_maximum_fusion.held_ref
  81.5 4.3 %collective-permute-start.7 = (bf16[32,2048]{1,0:T(8,128)(2,1)S(1)}, bf16[32,2048]{1,0:T(8,128)(2,1)S(1)}, u32[]{:S(2)}, u32[]{:S(2)}) collective-permute-start(bf16[32,2048]{1,0:T(8,128)(2,1)S(1)} %bitcast.44), channel_id=1, source_target_pairs={{0,32},{32,64},{64,96},{96,128},{128,160},{160,192},{192,224},{224... | collective-permute-start | bytes 393224 | tf_op jit(solution)/shard_map/ppermute | solution.py:49
  87.3 0.1 stack.150.at_ref
  87.5 0.0 copy-start.4
  87.5 0.3 collective-permute-done.7.above_ref
  87.8 0.0 collective-permute-done.8.other_ref
  87.8 3.8 %scores.1 = (f32[288,1024]{1,0:T(8,128)S(1)}, f32[288,384]{1,0:T(8,128)S(1)}, f32[288,128]{1,0:T(8,128)S(1)}) custom-call(s32[33]{0:T(128)S(1)} %stack.150.at_ref, bf16[4,4,16,2048]{3,2,1,0:T(8,128)(2,1)S(1)} %pad_maximum_fusion.held_ref, bf16[32,2048]{1,0:T(8,128)(2,1)S(1)} %collective-permute-done.7.above_ref, ...), custom_call_target="tpu_custom_call" | custom-call | flops 1207959552 | bytes 8388608 | tf_op jit(solution)/shard_map/scores/pallas_call | solution.py:100
  91.6 2.2 %collective-permute-start.9 = (f32[288,384]{1,0:T(8,128)S(1)}, f32[288,384]{1,0:T(8,128)S(1)}, u32[]{:S(2)}, u32[]{:S(2)}) collective-permute-start(f32[288,384]{1,0:T(8,128)S(1)} %get-tuple-element.8), channel_id=1, source_target_pairs={{0,1},{1,2},{2,3},{3,4},{4,5},{5,6},{6,7},{7,8},{8,9},{9,10},{10,1... | collective-permute-start | bytes 1327112 | tf_op jit(solution)/shard_map/ppermute | solution.py:248
  93.9 4.0 %collective-permute-start.10 = (f32[288,128]{1,0:T(8,128)S(1)}, f32[288,128]{1,0:T(8,128)S(1)}, u32[]{:S(2)}, u32[]{:S(2)}) collective-permute-start(f32[288,128]{1,0:T(8,128)S(1)} %get-tuple-element.10), channel_id=1, source_target_pairs={{1,0},{2,1},{3,2},{4,3},{5,4},{6,5},{7,6},{8,7},{9,8},{10,9},{11,1... | collective-permute-start | bytes 442376 | tf_op jit(solution)/shard_map/ppermute | solution.py:249
  97.8 0.0 copy-done.4
  97.8 0.1 pad_add_fusion.slopes_ref
  97.9 10.9 %collective-permute-done.10.right_ref = f32[288,128]{1,0:T(8,128)S(1)} collective-permute-done((f32[288,128]{1,0:T(8,128)S(1)}, f32[288,128]{1,0:T(8,128)S(1)}, u32[]{:S(2)}, u32[]{:S(2)}) %collective-permute-start.10) | collective-permute-done | bytes 147488 | tf_op jit(solution)/shard_map/ppermute | solution.py:249
  108.8 0.0 collective-permute-done.9.left_ref
  108.8 68.5 %best.1 = f32[256,1024]{1,0:T(8,128)} custom-call(s32[9]{0:T(128)S(1)} %pad_add_fusion.slopes_ref, f32[288,384]{1,0:T(8,128)S(1)} %collective-permute-done.9.left_ref, f32[288,1024]{1,0:T(8,128)S(1)} %get-tuple-element.9.mid_ref, f32[288,128]{1,0:T(8,128)S(1)} %collective-permute-done.10.right_ref), custom_call_target="tpu_custom_call" | custom-call | flops 62914560 | bytes 4194304 | tf_op jit(solution)/shard_map/best/pallas_call | solution.py:225
  (8 shorter events, 0.1 us)
Async XLA Ops:
  2.6 6.8 %copy-start.3 = (bf16[1,8,2048]{2,1,0:T(8,128)(2,1)S(1)}, bf16[1,8,2048]{2,1,0:T(8,128)(2,1)}, u32[]{:S(2)}) copy-start(bf16[1,8,2048]{2,1,0:T(8,128)(2,1)} %param.3) | copy-start | bytes 98308
  2.6 34.3 %all-to-all-start = ((bf16[8,1024,128]{2,1,0:T(8,128)(2,1)}), bf16[8,1024,128]{2,1,0:T(8,128)(2,1)S(1)}, u32[]{:S(2)}, u32[]{:S(2)}) async-start(bf16[8,1024,128]{2,1,0:T(8,128)(2,1)} %broadcast_in_dim.13), calls=%async_computation | async-start | bytes 4194304 | tf_op jit(solution)/shard_map/all_to_all | solution.py:66
  9.3 23.8 %collective-permute-start.1 = (bf16[1,8,2048]{2,1,0:T(8,128)(2,1)S(1)}, bf16[1,8,2048]{2,1,0:T(8,128)(2,1)S(1)}, u32[]{:S(2)}, u32[]{:S(2)}) collective-permute-start(bf16[1,8,2048]{2,1,0:T(8,128)(2,1)S(1)} %copy-done.3), channel_id=1, source_target_pairs={{0,24},{1,25},{2,26},{3,27},{4,28},{5,29},{6,30},{7,31},{8,0},{9,1... | collective-permute-start | bytes 98312 | tf_op jit(solution)/shard_map/ppermute | solution.py:34
  20.9 12.2 %collective-permute-start = (bf16[1,8,2048]{2,1,0:T(8,128)(2,1)S(1)}, bf16[1,8,2048]{2,1,0:T(8,128)(2,1)S(1)}, u32[]{:S(2)}, u32[]{:S(2)}) collective-permute-start(bf16[1,8,2048]{2,1,0:T(8,128)(2,1)S(1)} %copy-done.3), channel_id=1, source_target_pairs={{0,8},{1,9},{2,10},{3,11},{4,12},{5,13},{6,14},{7,15},{8,16},{9,17... | collective-permute-start | bytes 98312 | tf_op jit(solution)/shard_map/ppermute | solution.py:34
  22.8 17.8 %collective-permute-start.2 = (bf16[1,8,2048]{2,1,0:T(8,128)(2,1)S(1)}, bf16[1,8,2048]{2,1,0:T(8,128)(2,1)S(1)}, u32[]{:S(2)}, u32[]{:S(2)}) collective-permute-start(bf16[1,8,2048]{2,1,0:T(8,128)(2,1)S(1)} %copy-done.3), channel_id=1, source_target_pairs={{0,16},{1,17},{2,18},{3,19},{4,20},{5,21},{6,22},{7,23},{8,24},{9,... | collective-permute-start | bytes 98312 | tf_op jit(solution)/shard_map/ppermute | solution.py:34
  36.9 50.9 %collective-permute-start.8 = (bf16[8,1024,128]{2,1,0:T(8,128)(2,1)S(1)}, bf16[8,1024,128]{2,1,0:T(8,128)(2,1)}, u32[]{:S(2)}, u32[]{:S(2)}) collective-permute-start(bf16[8,1024,128]{2,1,0:T(8,128)(2,1)S(1)} %all-to-all-done.own_ref), channel_id=1, source_target_pairs={{0,32},{32,0},{64,96},{96,64},{128,160},{160,128},{192,224},{224,1... | collective-permute-start | bytes 6291464 | tf_op jit(solution)/shard_map/ppermute | solution.py:67
  40.7 7.0 %collective-permute-start.3 = (bf16[4,8,2048]{2,1,0:T(8,128)(2,1)S(1)}, bf16[4,8,2048]{2,1,0:T(8,128)(2,1)S(1)}, u32[]{:S(2)}, u32[]{:S(2)}) collective-permute-start(bf16[4,8,2048]{2,1,0:T(8,128)(2,1)S(1)} %constant_dynamic-update-slice_fusion), channel_id=1, source_target_pairs={{0,1},{1,0},{2,3},{3,2},{4,5},{5,4},{6,7},{7,6},{8,9},{9,8},{10,11... | collective-permute-start | bytes 393224 | tf_op jit(solution)/shard_map/ppermute | solution.py:36
  47.8 11.8 %collective-permute-start.5 = (bf16[4,16,2048]{2,1,0:T(8,128)(2,1)S(1)}, bf16[4,16,2048]{2,1,0:T(8,128)(2,1)S(1)}, u32[]{:S(2)}, u32[]{:S(2)}) collective-permute-start(bf16[4,16,2048]{2,1,0:T(8,128)(2,1)S(1)} %get-tuple-element.14), channel_id=1, source_target_pairs={{0,30},{1,31},{2,0},{3,1},{4,2},{5,3},{6,4},{7,5},{8,6},{9,7},{10,... | collective-permute-start | bytes 786440 | tf_op jit(solution)/shard_map/ppermute | solution.py:41
  49.7 16.5 %collective-permute-start.4 = (bf16[4,16,2048]{2,1,0:T(8,128)(2,1)S(1)}, bf16[4,16,2048]{2,1,0:T(8,128)(2,1)S(1)}, u32[]{:S(2)}, u32[]{:S(2)}) collective-permute-start(bf16[4,16,2048]{2,1,0:T(8,128)(2,1)S(1)} %get-tuple-element.14), channel_id=1, source_target_pairs={{0,2},{1,3},{2,4},{3,5},{4,6},{5,7},{6,8},{7,9},{8,10},{9,11},{10,... | collective-permute-start | bytes 786440 | tf_op jit(solution)/shard_map/ppermute | solution.py:41
  53.3 26.3 %collective-permute-start.6 = (bf16[4,16,2048]{2,1,0:T(8,128)(2,1)S(1)}, bf16[4,16,2048]{2,1,0:T(8,128)(2,1)S(1)}, u32[]{:S(2)}, u32[]{:S(2)}) collective-permute-start(bf16[4,16,2048]{2,1,0:T(8,128)(2,1)S(1)} %get-tuple-element.14), channel_id=1, source_target_pairs={{0,4},{1,5},{2,6},{3,7},{4,8},{5,9},{6,10},{7,11},{8,12},{9,13},{1... | collective-permute-start | bytes 786440 | tf_op jit(solution)/shard_map/ppermute | solution.py:41
  59.6 19.9 %copy-start = (bf16[4,16,2048]{2,1,0:T(8,128)(2,1)}, bf16[4,16,2048]{2,1,0:T(8,128)(2,1)S(1)}, u32[]{:S(2)}) copy-start(bf16[4,16,2048]{2,1,0:T(8,128)(2,1)S(1)} %collective-permute-done.5) | copy-start | bytes 786436
  66.2 13.3 %copy-start.1 = (bf16[4,16,2048]{2,1,0:T(8,128)(2,1)}, bf16[4,16,2048]{2,1,0:T(8,128)(2,1)S(1)}, u32[]{:S(2)}) copy-start(bf16[4,16,2048]{2,1,0:T(8,128)(2,1)S(1)} %collective-permute-done.4) | copy-start | bytes 786436
  79.5 0.7 copy-start.2
  81.5 6.3 %collective-permute-start.7 = (bf16[32,2048]{1,0:T(8,128)(2,1)S(1)}, bf16[32,2048]{1,0:T(8,128)(2,1)S(1)}, u32[]{:S(2)}, u32[]{:S(2)}) collective-permute-start(bf16[32,2048]{1,0:T(8,128)(2,1)S(1)} %bitcast.44), channel_id=1, source_target_pairs={{0,32},{32,64},{64,96},{96,128},{128,160},{160,192},{192,224},{224... | collective-permute-start | bytes 393224 | tf_op jit(solution)/shard_map/ppermute | solution.py:49
  87.5 10.4 %copy-start.4 = (s32[8]{0:T(128)S(1)}, s32[8]{0:T(128)}, u32[]{:S(2)}) copy-start(s32[8]{0:T(128)} %param.5) | copy-start | bytes 100
  91.6 17.2 %collective-permute-start.9 = (f32[288,384]{1,0:T(8,128)S(1)}, f32[288,384]{1,0:T(8,128)S(1)}, u32[]{:S(2)}, u32[]{:S(2)}) collective-permute-start(f32[288,384]{1,0:T(8,128)S(1)} %get-tuple-element.8), channel_id=1, source_target_pairs={{0,1},{1,2},{2,3},{3,4},{4,5},{5,6},{6,7},{7,8},{8,9},{9,10},{10,1... | collective-permute-start | bytes 1327112 | tf_op jit(solution)/shard_map/ppermute | solution.py:248
  93.9 15.0 %collective-permute-start.10 = (f32[288,128]{1,0:T(8,128)S(1)}, f32[288,128]{1,0:T(8,128)S(1)}, u32[]{:S(2)}, u32[]{:S(2)}) collective-permute-start(f32[288,128]{1,0:T(8,128)S(1)} %get-tuple-element.10), channel_id=1, source_target_pairs={{1,0},{2,1},{3,2},{4,3},{5,4},{6,5},{7,6},{8,7},{9,8},{10,9},{11,1... | collective-permute-start | bytes 442376 | tf_op jit(solution)/shard_map/ppermute | solution.py:249

commit v2 on v1

--- a/solution.py
+++ b/solution.py
@@ -117,13 +117,12 @@
     return slice(c * LANES, (c + 1) * LANES)
 
 
-def best_kernel(slopes_ref, left_ref, mid_ref, right_ref, out_ref, x_ref, two_ref, four_ref, eight_ref):
+def best_kernel(slopes_ref, left_ref, mid_ref, right_ref, out_ref, split_ref, x_ref, lag_ref, sum_ref, best_ref):
     rows = mid_ref.shape[0]
     columns = mid_ref.shape[1]
     halo = LEFT // LANES
     tiles = halo + columns // LANES
     first_map = slopes_ref[8] == 0
-    step_rows = 96
 
     def source(c):
         if c < halo:
@@ -132,103 +131,128 @@
             return mid_ref, c - halo
         return right_ref, c - tiles
 
-    def up(prev, cur, by, lane):
-        return jnp.where(lane < LANES - by, pltpu.roll(prev, LANES - by, 1), pltpu.roll(cur, LANES - by, 1))
+    for part in range(6):
+        for c in (0, tiles + 2):
+            split_ref[part, :, tile(c)] = jnp.zeros((rows, LANES), jnp.bfloat16)
+
+    def split(block, carry):
+        take = pl.ds(pl.multiple_of(block * 96, 96), 96)
+        for c in range(tiles + 1):
+            ref, at = source(c)
+            value = ref[take, tile(at)]
+            for kind, rest in enumerate((value, value * value)):
+                for part in range(3):
+                    piece = rest.astype(jnp.bfloat16)
+                    split_ref[3 * kind + part, take, tile(c + 1)] = piece
+                    rest = rest - piece.astype(jnp.float32)
+        return carry
+
+    lax.fori_loop(0, rows // 96, split, 0)
+    at_in = lax.broadcasted_iota(jnp.int32, (4 * LANES, 2 * LANES), 0)
+    at_out = lax.broadcasted_iota(jnp.int32, (4 * LANES, 2 * LANES), 1) + LANES
+    band = jnp.where(jnp.abs(at_in - at_out) <= RAD, 1.0, 0.0).astype(jnp.bfloat16)
 
     def normalise(block, carry):
-        begin = pl.multiple_of(block * 32, 32)
-        take = pl.ds(begin, 32)
-        lane = lax.broadcasted_iota(jnp.int32, (32, LANES), 1)
-
-        def raw(c):
-            ref, at = source(c)
-            return ref[take, tile(at)]
-
-        def chain(values):
-            one = values
-            two = [v + up(v, w, 1, lane) for v, w in zip(one, one[1:] + one[-1:])]
-            four = [v + up(v, w, 2, lane) for v, w in zip(two, two[1:] + two[-1:])]
-            eight = [v + up(v, w, 4, lane) for v, w in zip(four, four[1:] + four[-1:])]
-            ten = [e + up(v, w, 8, lane) for e, v, w in zip(eight, two, two[1:] + two[-1:])]
-            twenty = [v + up(v, w, 10, lane) for v, w in zip(ten, ten[1:] + ten[-1:])]
-            return [t + up(v, w, 20, lane) for t, v, w in zip(twenty, one, one[1:] + one[-1:])]
-
+        take = pl.ds(pl.multiple_of(block * 96, 96), 96)
+        for c in range(0, tiles, 2):
+            found = []
+            for kind in range(2):
+                total = None
+                for part in range(3):
+                    lhs = split_ref[3 * kind + part, take, c * LANES : (c + 4) * LANES]
+                    term = jnp.dot(lhs, band, preferred_element_type=jnp.float32)
+                    total = term if total is None else total + term
+                found.append(total * (1.0 / (2 * RAD + 1)))
+            mean, square = found
+            scale = lax.rsqrt(square - mean * mean + 1.0)
+            for half in range(2):
+                if c + half >= tiles:
+                    continue
+                ref, at = source(c + half)
+                value = (ref[take, tile(at)] - mean[:, tile(half)]) * scale[:, tile(half)]
+                if c + half < halo:
+                    value = jnp.where(first_map, 0.0, value)
+                x_ref[c + half, take] = value
+        return carry
+
+    lax.fori_loop(0, rows // 96, normalise, 0)
+
+    steps = SEQ - 1 + 32
+    zero = jnp.zeros((8, LANES), jnp.float32)
+    for t in range(steps):
+        for c in range(halo):
+            lag_ref[t, c] = zero
         for c in range(tiles):
-            near = [raw(max(c - 1, 0)), raw(c), raw(c + 1)]
-            sums = chain(near)
-            squares = chain([v * v for v in near])
-            back = lambda v: jnp.where(lane < RAD, pltpu.roll(v[0], RAD, 1), pltpu.roll(v[1], RAD, 1))
-            mean = back(sums) * (1.0 / (2 * RAD + 1))
-            square = back(squares) * (1.0 / (2 * RAD + 1))
-            value = (near[1] - mean) * lax.rsqrt(square - mean * mean + 1.0)
-            if c < halo:
-                value = jnp.where(first_map, 0.0, value)
-            x_ref[take, tile(c)] = value
-        return carry
-
-    lax.fori_loop(0, rows // 32, normalise, 0)
-
-    def shifted(ref, take, c, by, whole, lane, prev):
-        at = c if whole is None else pl.multiple_of((c - whole) * LANES, LANES)
-        cols = tile(c) if whole is None else pl.ds(at, LANES)
-        cur = pltpu.roll(ref[take, cols], by, 1)
-        return cur if prev is None else jnp.where(lane < by, prev, cur), cur
-
-    def blocks(start):
-        at = start
-        while at < rows:
-            size = min(64, rows - at)
-            yield at, size
-            at += size
-
-    def stage(src, dst, lag, by, row0, col0):
-        for at, size in blocks(row0):
-            lane = lax.broadcasted_iota(jnp.int32, (size, LANES), 1)
-            prev = None
-            if col0 > 0:
-                _, prev = shifted(src, slice(at - lag, at - lag + size), col0 - 1, by, None, lane, None)
-            for c in range(col0, tiles):
-                moved, prev = shifted(src, slice(at - lag, at - lag + size), c, by, None, lane, prev)
-                dst[at : at + size, tile(c)] = src[at : at + size, tile(c)] + moved
-
-    def per_slope(index, carry):
-        v = slopes_ref[index]
-        stage(x_ref, two_ref, 1, v, 8, 0)
-        stage(two_ref, four_ref, 2, 2 * v, 16, 1)
-        stage(four_ref, eight_ref, 4, 4 * v, 24, 2)
-        by8 = 8 * v
-        by16 = 16 * v
-        whole = by16 // LANES
-        by16 = by16 % LANES
-        for at, size in blocks(TOP):
-            lane = lax.broadcasted_iota(jnp.int32, (size, LANES), 1)
-            take8 = slice(at - 8, at - 8 + size)
-            take16 = slice(at - 16, at - 16 + size)
-            _, prev8 = shifted(eight_ref, take8, halo - 1, by8, None, lane, None)
-            _, prev16 = shifted(four_ref, take16, halo - 1, by16, whole, lane, None)
+            lag_ref[t, c + halo] = x_ref[c, pl.ds(t + TOP - SEQ + 1, 8, stride=32)]
+    for index in range(8):
+        for c in range(tiles):
+            sum_ref[index, c] = zero
+
+    lane = lax.broadcasted_iota(jnp.int32, (8, LANES), 1)
+
+    def step(t, begin, drop, emit):
+        best = [None] * tiles
+        for index in range(8):
+            v = slopes_ref[index]
+            by = v
+            far = SEQ * v
+            whole = far // LANES
+            far = far % LANES
+            before = zero
+            old = None
+
+            def dropped(c):
+                return pltpu.roll(lag_ref[t - SEQ, c + halo - whole], far, 1)
+
+            if drop:
+                old = dropped(begin - 1)
+            for c in range(begin, tiles):
+                moved = pltpu.roll(sum_ref[index, c], by, 1)
+                total = jnp.where(lane < by, before, moved) + lag_ref[t, c + halo]
+                before = moved
+                if drop:
+                    gone = dropped(c)
+                    total = total - jnp.where(lane < far, old, gone)
+                    old = gone
+                sum_ref[index, c] = total
+                if emit and c >= halo:
+                    best[c] = total if best[c] is None else jnp.maximum(best[c], total)
+        if emit:
             for c in range(halo, tiles):
-                moved8, prev8 = shifted(eight_ref, take8, c, by8, None, lane, prev8)
-                moved16, prev16 = shifted(four_ref, take16, c, by16, whole, lane, prev16)
-                total = (eight_ref[at : at + size, tile(c)] + moved8) + moved16
-                out_rows = slice(at - TOP, at - TOP + size)
-                kept = jnp.where(index == 0, total, jnp.maximum(out_ref[out_rows, tile(c - halo)], total))
-                out_ref[out_rows, tile(c - halo)] = kept
-        return carry
-
-    lax.fori_loop(0, 8, per_slope, 0)
-    out_ref[...] = out_ref[...] * (1.0 / math.sqrt(SEQ))
+                best_ref[c - halo, pl.ds(t - SEQ + 1, 8, stride=32)] = best[c] * (1.0 / math.sqrt(SEQ))
+
+    def phase(first, last, begin, drop, emit):
+        def body(t, carry):
+            step(t, begin, drop, emit)
+            return carry
+
+        lax.fori_loop(first, last, body, 0)
+
+    phase(0, SEQ - 1, 0, False, False)
+    step(SEQ - 1, 0, False, True)
+    phase(SEQ, 34, 0, True, True)
+    phase(34, 43, 1, True, True)
+    phase(43, steps, 2, True, True)
+    for c in range(columns // LANES):
+        out_ref[:, tile(c)] = best_ref[c]
 
 
 def best_of(slopes_and_place, left, mid, right):
     rows, columns = mid.shape
-    scratch = pltpu.VMEM((rows, LEFT + columns), jnp.float32)
+    tiles = (LEFT + columns) // LANES
     return pl.pallas_call(
         best_kernel,
         name="best",
         out_shape=jax.ShapeDtypeStruct((rows - TOP, columns), jnp.float32),
         in_specs=[pl.BlockSpec(memory_space=pltpu.SMEM)] + [pl.BlockSpec(memory_space=pltpu.VMEM)] * 3,
         out_specs=pl.BlockSpec(memory_space=pltpu.VMEM),
-        scratch_shapes=[scratch] * 4,
+        scratch_shapes=[
+            pltpu.VMEM((6, rows, (tiles + 3) * LANES), jnp.bfloat16),
+            pltpu.VMEM((tiles, rows, LANES), jnp.float32),
+            pltpu.VMEM((SEQ + 31, tiles + LEFT // LANES, 8, LANES), jnp.float32),
+            pltpu.VMEM((8, tiles, 8, LANES), jnp.float32),
+            pltpu.VMEM((columns // LANES, rows - TOP, LANES), jnp.float32),
+        ],
         compiler_params=pltpu.CompilerParams(vmem_limit_bytes=32 << 20),
         cost_estimate=pl.CostEstimate(flops=60 << 20, bytes_accessed=4 << 20, transcendentals=0),
     )(slopes_and_place, left, mid, right)

time: 178 us -> 130 us (0.73)
  Pallas kernels: 72.3 us -> 24.6 us
    pallas_call x1, Pallas kernels: 68.5 us -> 20.8 us  [best_of(): pl.pallas_call(best_kernel, name='best', out_shape=jax.ShapeDtypeStruct((...]
where the time goes in v2:
time: 130 us
  starting transfers between devices  58.6 us (45%)
  waiting for transfers between devices  39.7 us (31%)
  Pallas kernels  24.6 us (19%)
  local copies, waits for them, and re-layouts  3.45 us (3%)
  between operations  1.89 us (1%)
  other arithmetic  1.4 us (1%)
    ppermute x3, starting transfers between devices, gather_queries(): lax.ppermute(queries[None], 'ma', along_z(k))  23.7 us
    pallas_call x1, Pallas kernels, best_of(): pl.pallas_call(best_kernel, name='best', out_shape=jax.ShapeDtypeStruct((...  20.8 us
    ppermute x3, waiting for transfers between devices, gather_queries(): parts = [pairs] + [lax.ppermute(pairs, 'ma', along_z(k)) for k in NEAR]  19.9 us
    ppermute x3, starting transfers between devices, gather_queries(): parts = [pairs] + [lax.ppermute(pairs, 'ma', along_z(k)) for k in NEAR]  11.6 us
    ppermute x1, waiting for transfers between devices, local(): right = lax.ppermute(lead, 'ma', [(i + 1, i) for i in range(31)])  10.9 us
    all_to_all x1, starting transfers between devices, gather_map(): own = lax.all_to_all(copies, 'pb', 0, 0, axis_index_groups=groups)  6.78 us
    ppermute x1, waiting for transfers between devices, gather_queries(): other = lax.ppermute(far, 'ma', along_z(0, 1))  4.77 us
    ppermute x1, starting transfers between devices, gather_queries(): above = lax.ppermute(tail, 'pb', [(i, i + 1) for i in range(15)])  4.33 us
  transfers between devices with their start and end apart: 12, of which 6 were waited for; matrix products, arithmetic and copies ran while one was open for 1% of the time, Pallas kernels for 0%

profile of v2, /device:TPU:33, one launch (start us, length us, event | category | flops | bytes accessed | tf_op | source)
XLA Modules:
  0.0 129.6 jit_solution(17950012602569402433)
XLA Ops:
  0.0 2.6 %broadcast_in_dim.13 = bf16[8,1024,128]{2,1,0:T(8,128)(2,1)} broadcast(bf16[1024,128]{1,0:T(8,128)(2,1)} %param.4), dimensions={1,2} | broadcast | bytes 2359296 | tf_op jit(solution)/shard_map/broadcast_in_dim | solution.py:65
  2.6 0.0 copy-start.3
  2.6 6.8 %all-to-all-start = ((bf16[8,1024,128]{2,1,0:T(8,128)(2,1)}), bf16[8,1024,128]{2,1,0:T(8,128)(2,1)S(1)}, u32[]{:S(2)}, u32[]{:S(2)}) async-start(bf16[8,1024,128]{2,1,0:T(8,128)(2,1)} %broadcast_in_dim.13), calls=%async_computation | async-start | bytes 4194304 | tf_op jit(solution)/shard_map/all_to_all | solution.py:66
  9.3 0.0 copy-done.3
  9.3 11.6 %collective-permute-start.1 = (bf16[1,8,2048]{2,1,0:T(8,128)(2,1)S(1)}, bf16[1,8,2048]{2,1,0:T(8,128)(2,1)S(1)}, u32[]{:S(2)}, u32[]{:S(2)}) collective-permute-start(bf16[1,8,2048]{2,1,0:T(8,128)(2,1)S(1)} %copy-done.3), channel_id=1, source_target_pairs={{0,24},{1,25},{2,26},{3,27},{4,28},{5,29},{6,30},{7,31},{8,0},{9,1... | collective-permute-start | bytes 98312 | tf_op jit(solution)/shard_map/ppermute | solution.py:34
  20.9 1.9 %collective-permute-start = (bf16[1,8,2048]{2,1,0:T(8,128)(2,1)S(1)}, bf16[1,8,2048]{2,1,0:T(8,128)(2,1)S(1)}, u32[]{:S(2)}, u32[]{:S(2)}) collective-permute-start(bf16[1,8,2048]{2,1,0:T(8,128)(2,1)S(1)} %copy-done.3), channel_id=1, source_target_pairs={{0,8},{1,9},{2,10},{3,11},{4,12},{5,13},{6,14},{7,15},{8,16},{9,17... | collective-permute-start | bytes 98312 | tf_op jit(solution)/shard_map/ppermute | solution.py:34
  22.8 10.3 %collective-permute-start.2 = (bf16[1,8,2048]{2,1,0:T(8,128)(2,1)S(1)}, bf16[1,8,2048]{2,1,0:T(8,128)(2,1)S(1)}, u32[]{:S(2)}, u32[]{:S(2)}) collective-permute-start(bf16[1,8,2048]{2,1,0:T(8,128)(2,1)S(1)} %copy-done.3), channel_id=1, source_target_pairs={{0,16},{1,17},{2,18},{3,19},{4,20},{5,21},{6,22},{7,23},{8,24},{9,... | collective-permute-start | bytes 98312 | tf_op jit(solution)/shard_map/ppermute | solution.py:34
  33.1 0.0 collective-permute-done
  33.1 0.0 collective-permute-done.1
  33.2 3.7 %all-to-all-done.own_ref = bf16[8,1024,128]{2,1,0:T(8,128)(2,1)S(1)} async-done(((bf16[8,1024,128]{2,1,0:T(8,128)(2,1)}), bf16[8,1024,128]{2,1,0:T(8,128)(2,1)S(1)}, u32[]{:S(2)}, u32[]{:S(2)}) %all-to-all-start) | async-done | bytes 2097184 | tf_op jit(solution)/shard_map/all_to_all | solution.py:66
  36.9 3.8 %collective-permute-start.8 = (bf16[8,1024,128]{2,1,0:T(8,128)(2,1)S(1)}, bf16[8,1024,128]{2,1,0:T(8,128)(2,1)}, u32[]{:S(2)}, u32[]{:S(2)}) collective-permute-start(bf16[8,1024,128]{2,1,0:T(8,128)(2,1)S(1)} %all-to-all-done.own_ref), channel_id=1, source_target_pairs={{0,32},{32,0},{64,96},{96,64},{128,160},{160,128},{192,224},{224,1... | collective-permute-start | bytes 6291464 | tf_op jit(solution)/shard_map/ppermute | solution.py:67
  40.7 0.0 collective-permute-done.2
  40.7 2.2 %collective-permute-start.3 = (bf16[4,8,2048]{2,1,0:T(8,128)(2,1)S(1)}, bf16[4,8,2048]{2,1,0:T(8,128)(2,1)S(1)}, u32[]{:S(2)}, u32[]{:S(2)}) collective-permute-start(bf16[4,8,2048]{2,1,0:T(8,128)(2,1)S(1)} %constant_dynamic-update-slice_fusion), channel_id=1, source_target_pairs={{0,1},{1,0},{2,3},{3,2},{4,5},{5,4},{6,7},{7,6},{8,9},{9,8},{10,11... | collective-permute-start | bytes 393224 | tf_op jit(solution)/shard_map/ppermute | solution.py:36
  42.9 4.8 %collective-permute-done.3 = bf16[4,8,2048]{2,1,0:T(8,128)(2,1)S(1)} collective-permute-done((bf16[4,8,2048]{2,1,0:T(8,128)(2,1)S(1)}, bf16[4,8,2048]{2,1,0:T(8,128)(2,1)S(1)}, u32[]{:S(2)}, u32[]{:S(2)}) %collective-permute-start.3) | collective-permute-done | bytes 131104 | tf_op jit(solution)/shard_map/ppermute | solution.py:36
  47.8 1.9 %collective-permute-start.5 = (bf16[4,16,2048]{2,1,0:T(8,128)(2,1)S(1)}, bf16[4,16,2048]{2,1,0:T(8,128)(2,1)S(1)}, u32[]{:S(2)}, u32[]{:S(2)}) collective-permute-start(bf16[4,16,2048]{2,1,0:T(8,128)(2,1)S(1)} %get-tuple-element.14), channel_id=1, source_target_pairs={{0,30},{1,31},{2,0},{3,1},{4,2},{5,3},{6,4},{7,5},{8,6},{9,7},{10,... | collective-permute-start | bytes 786440 | tf_op jit(solution)/shard_map/ppermute | solution.py:41
  49.7 3.5 %collective-permute-start.4 = (bf16[4,16,2048]{2,1,0:T(8,128)(2,1)S(1)}, bf16[4,16,2048]{2,1,0:T(8,128)(2,1)S(1)}, u32[]{:S(2)}, u32[]{:S(2)}) collective-permute-start(bf16[4,16,2048]{2,1,0:T(8,128)(2,1)S(1)} %get-tuple-element.14), channel_id=1, source_target_pairs={{0,2},{1,3},{2,4},{3,5},{4,6},{5,7},{6,8},{7,9},{8,10},{9,11},{10,... | collective-permute-start | bytes 786440 | tf_op jit(solution)/shard_map/ppermute | solution.py:41
  53.3 6.1 %collective-permute-start.6 = (bf16[4,16,2048]{2,1,0:T(8,128)(2,1)S(1)}, bf16[4,16,2048]{2,1,0:T(8,128)(2,1)S(1)}, u32[]{:S(2)}, u32[]{:S(2)}) collective-permute-start(bf16[4,16,2048]{2,1,0:T(8,128)(2,1)S(1)} %get-tuple-element.14), channel_id=1, source_target_pairs={{0,4},{1,5},{2,6},{3,7},{4,8},{5,9},{6,10},{7,11},{8,12},{9,13},{1... | collective-permute-start | bytes 786440 | tf_op jit(solution)/shard_map/ppermute | solution.py:41
  59.6 0.0 collective-permute-done.5
  59.6 0.0 copy-start
  59.6 6.6 %collective-permute-done.4 = bf16[4,16,2048]{2,1,0:T(8,128)(2,1)S(1)} collective-permute-done((bf16[4,16,2048]{2,1,0:T(8,128)(2,1)S(1)}, bf16[4,16,2048]{2,1,0:T(8,128)(2,1)S(1)}, u32[]{:S(2)}, u32[]{:S(2)}) %collective-permute-start.4) | collective-permute-done | bytes 262176 | tf_op jit(solution)/shard_map/ppermute | solution.py:41
  66.2 0.0 copy-start.1
  66.2 13.3 %collective-permute-done.6 = bf16[4,16,2048]{2,1,0:T(8,128)(2,1)S(1)} collective-permute-done((bf16[4,16,2048]{2,1,0:T(8,128)(2,1)S(1)}, bf16[4,16,2048]{2,1,0:T(8,128)(2,1)S(1)}, u32[]{:S(2)}, u32[]{:S(2)}) %collective-permute-start.6) | collective-permute-done | bytes 262176 | tf_op jit(solution)/shard_map/ppermute | solution.py:41
  79.5 0.0 copy-start.2
  79.5 0.0 copy-done
  79.5 0.0 copy-done.1
  79.5 0.7 copy-done.2
  80.2 1.2 pad_maximum_fusion.held_ref
  81.5 4.3 %collective-permute-start.7 = (bf16[32,2048]{1,0:T(8,128)(2,1)S(1)}, bf16[32,2048]{1,0:T(8,128)(2,1)S(1)}, u32[]{:S(2)}, u32[]{:S(2)}) collective-permute-start(bf16[32,2048]{1,0:T(8,128)(2,1)S(1)} %bitcast.44), channel_id=1, source_target_pairs={{0,32},{32,64},{64,96},{96,128},{128,160},{160,192},{192,224},{224... | collective-permute-start | bytes 393224 | tf_op jit(solution)/shard_map/ppermute | solution.py:49
  87.3 0.1 stack.150.at_ref
  87.5 0.0 copy-start.4
  87.5 0.3 collective-permute-done.7.above_ref
  87.8 0.0 collective-permute-done.8.other_ref
  87.8 3.8 %scores.1 = (f32[288,1024]{1,0:T(8,128)S(1)}, f32[288,384]{1,0:T(8,128)S(1)}, f32[288,128]{1,0:T(8,128)S(1)}) custom-call(s32[33]{0:T(128)S(1)} %stack.150.at_ref, bf16[4,4,16,2048]{3,2,1,0:T(8,128)(2,1)S(1)} %pad_maximum_fusion.held_ref, bf16[32,2048]{1,0:T(8,128)(2,1)S(1)} %collective-permute-done.7.above_ref, ...), custom_call_target="tpu_custom_call" | custom-call | flops 1207959552 | bytes 8388608 | tf_op jit(solution)/shard_map/scores/pallas_call | solution.py:100
  91.6 2.2 %collective-permute-start.9 = (f32[288,384]{1,0:T(8,128)S(1)}, f32[288,384]{1,0:T(8,128)S(1)}, u32[]{:S(2)}, u32[]{:S(2)}) collective-permute-start(f32[288,384]{1,0:T(8,128)S(1)} %get-tuple-element.8), channel_id=1, source_target_pairs={{0,1},{1,2},{2,3},{3,4},{4,5},{5,6},{6,7},{7,8},{8,9},{9,10},{10,1... | collective-permute-start | bytes 1327112 | tf_op jit(solution)/shard_map/ppermute | solution.py:272
  93.9 4.0 %collective-permute-start.10 = (f32[288,128]{1,0:T(8,128)S(1)}, f32[288,128]{1,0:T(8,128)S(1)}, u32[]{:S(2)}, u32[]{:S(2)}) collective-permute-start(f32[288,128]{1,0:T(8,128)S(1)} %get-tuple-element.10), channel_id=1, source_target_pairs={{1,0},{2,1},{3,2},{4,3},{5,4},{6,5},{7,6},{8,7},{9,8},{10,9},{11,1... | collective-permute-start | bytes 442376 | tf_op jit(solution)/shard_map/ppermute | solution.py:273
  97.8 0.0 copy-done.4
  97.8 0.1 pad_add_fusion.slopes_ref
  97.9 10.9 %collective-permute-done.10.right_ref = f32[288,128]{1,0:T(8,128)S(1)} collective-permute-done((f32[288,128]{1,0:T(8,128)S(1)}, f32[288,128]{1,0:T(8,128)S(1)}, u32[]{:S(2)}, u32[]{:S(2)}) %collective-permute-start.10) | collective-permute-done | bytes 147488 | tf_op jit(solution)/shard_map/ppermute | solution.py:273
  108.8 0.0 collective-permute-done.9.left_ref
  108.8 20.8 %best.1 = f32[256,1024]{1,0:T(8,128)} custom-call(s32[9]{0:T(128)S(1)} %pad_add_fusion.slopes_ref, f32[288,384]{1,0:T(8,128)S(1)} %collective-permute-done.9.left_ref, f32[288,1024]{1,0:T(8,128)S(1)} %get-tuple-element.9.mid_ref, f32[288,128]{1,0:T(8,128)S(1)} %collective-permute-done.10.right_ref), custom_call_target="tpu_custom_call" | custom-call | flops 62914560 | bytes 4194304 | tf_op jit(solution)/shard_map/best/pallas_call | solution.py:243
  (8 shorter events, 0.1 us)
Async XLA Ops:
  2.6 6.8 %copy-start.3 = (bf16[1,8,2048]{2,1,0:T(8,128)(2,1)S(1)}, bf16[1,8,2048]{2,1,0:T(8,128)(2,1)}, u32[]{:S(2)}) copy-start(bf16[1,8,2048]{2,1,0:T(8,128)(2,1)} %param.3) | copy-start | bytes 98308
  2.6 34.3 %all-to-all-start = ((bf16[8,1024,128]{2,1,0:T(8,128)(2,1)}), bf16[8,1024,128]{2,1,0:T(8,128)(2,1)S(1)}, u32[]{:S(2)}, u32[]{:S(2)}) async-start(bf16[8,1024,128]{2,1,0:T(8,128)(2,1)} %broadcast_in_dim.13), calls=%async_computation | async-start | bytes 4194304 | tf_op jit(solution)/shard_map/all_to_all | solution.py:66
  9.3 23.8 %collective-permute-start.1 = (bf16[1,8,2048]{2,1,0:T(8,128)(2,1)S(1)}, bf16[1,8,2048]{2,1,0:T(8,128)(2,1)S(1)}, u32[]{:S(2)}, u32[]{:S(2)}) collective-permute-start(bf16[1,8,2048]{2,1,0:T(8,128)(2,1)S(1)} %copy-done.3), channel_id=1, source_target_pairs={{0,24},{1,25},{2,26},{3,27},{4,28},{5,29},{6,30},{7,31},{8,0},{9,1... | collective-permute-start | bytes 98312 | tf_op jit(solution)/shard_map/ppermute | solution.py:34
  20.9 12.2 %collective-permute-start = (bf16[1,8,2048]{2,1,0:T(8,128)(2,1)S(1)}, bf16[1,8,2048]{2,1,0:T(8,128)(2,1)S(1)}, u32[]{:S(2)}, u32[]{:S(2)}) collective-permute-start(bf16[1,8,2048]{2,1,0:T(8,128)(2,1)S(1)} %copy-done.3), channel_id=1, source_target_pairs={{0,8},{1,9},{2,10},{3,11},{4,12},{5,13},{6,14},{7,15},{8,16},{9,17... | collective-permute-start | bytes 98312 | tf_op jit(solution)/shard_map/ppermute | solution.py:34
  22.8 17.8 %collective-permute-start.2 = (bf16[1,8,2048]{2,1,0:T(8,128)(2,1)S(1)}, bf16[1,8,2048]{2,1,0:T(8,128)(2,1)S(1)}, u32[]{:S(2)}, u32[]{:S(2)}) collective-permute-start(bf16[1,8,2048]{2,1,0:T(8,128)(2,1)S(1)} %copy-done.3), channel_id=1, source_target_pairs={{0,16},{1,17},{2,18},{3,19},{4,20},{5,21},{6,22},{7,23},{8,24},{9,... | collective-permute-start | bytes 98312 | tf_op jit(solution)/shard_map/ppermute | solution.py:34
  36.9 50.9 %collective-permute-start.8 = (bf16[8,1024,128]{2,1,0:T(8,128)(2,1)S(1)}, bf16[8,1024,128]{2,1,0:T(8,128)(2,1)}, u32[]{:S(2)}, u32[]{:S(2)}) collective-permute-start(bf16[8,1024,128]{2,1,0:T(8,128)(2,1)S(1)} %all-to-all-done.own_ref), channel_id=1, source_target_pairs={{0,32},{32,0},{64,96},{96,64},{128,160},{160,128},{192,224},{224,1... | collective-permute-start | bytes 6291464 | tf_op jit(solution)/shard_map/ppermute | solution.py:67
  40.7 7.0 %collective-permute-start.3 = (bf16[4,8,2048]{2,1,0:T(8,128)(2,1)S(1)}, bf16[4,8,2048]{2,1,0:T(8,128)(2,1)S(1)}, u32[]{:S(2)}, u32[]{:S(2)}) collective-permute-start(bf16[4,8,2048]{2,1,0:T(8,128)(2,1)S(1)} %constant_dynamic-update-slice_fusion), channel_id=1, source_target_pairs={{0,1},{1,0},{2,3},{3,2},{4,5},{5,4},{6,7},{7,6},{8,9},{9,8},{10,11... | collective-permute-start | bytes 393224 | tf_op jit(solution)/shard_map/ppermute | solution.py:36
  47.8 11.8 %collective-permute-start.5 = (bf16[4,16,2048]{2,1,0:T(8,128)(2,1)S(1)}, bf16[4,16,2048]{2,1,0:T(8,128)(2,1)S(1)}, u32[]{:S(2)}, u32[]{:S(2)}) collective-permute-start(bf16[4,16,2048]{2,1,0:T(8,128)(2,1)S(1)} %get-tuple-element.14), channel_id=1, source_target_pairs={{0,30},{1,31},{2,0},{3,1},{4,2},{5,3},{6,4},{7,5},{8,6},{9,7},{10,... | collective-permute-start | bytes 786440 | tf_op jit(solution)/shard_map/ppermute | solution.py:41
  49.7 16.5 %collective-permute-start.4 = (bf16[4,16,2048]{2,1,0:T(8,128)(2,1)S(1)}, bf16[4,16,2048]{2,1,0:T(8,128)(2,1)S(1)}, u32[]{:S(2)}, u32[]{:S(2)}) collective-permute-start(bf16[4,16,2048]{2,1,0:T(8,128)(2,1)S(1)} %get-tuple-element.14), channel_id=1, source_target_pairs={{0,2},{1,3},{2,4},{3,5},{4,6},{5,7},{6,8},{7,9},{8,10},{9,11},{10,... | collective-permute-start | bytes 786440 | tf_op jit(solution)/shard_map/ppermute | solution.py:41
  53.3 26.3 %collective-permute-start.6 = (bf16[4,16,2048]{2,1,0:T(8,128)(2,1)S(1)}, bf16[4,16,2048]{2,1,0:T(8,128)(2,1)S(1)}, u32[]{:S(2)}, u32[]{:S(2)}) collective-permute-start(bf16[4,16,2048]{2,1,0:T(8,128)(2,1)S(1)} %get-tuple-element.14), channel_id=1, source_target_pairs={{0,4},{1,5},{2,6},{3,7},{4,8},{5,9},{6,10},{7,11},{8,12},{9,13},{1... | collective-permute-start | bytes 786440 | tf_op jit(solution)/shard_map/ppermute | solution.py:41
  59.6 19.9 %copy-start = (bf16[4,16,2048]{2,1,0:T(8,128)(2,1)}, bf16[4,16,2048]{2,1,0:T(8,128)(2,1)S(1)}, u32[]{:S(2)}) copy-start(bf16[4,16,2048]{2,1,0:T(8,128)(2,1)S(1)} %collective-permute-done.5) | copy-start | bytes 786436
  66.2 13.3 %copy-start.1 = (bf16[4,16,2048]{2,1,0:T(8,128)(2,1)}, bf16[4,16,2048]{2,1,0:T(8,128)(2,1)S(1)}, u32[]{:S(2)}) copy-start(bf16[4,16,2048]{2,1,0:T(8,128)(2,1)S(1)} %collective-permute-done.4) | copy-start | bytes 786436
  79.5 0.7 copy-start.2
  81.5 6.3 %collective-permute-start.7 = (bf16[32,2048]{1,0:T(8,128)(2,1)S(1)}, bf16[32,2048]{1,0:T(8,128)(2,1)S(1)}, u32[]{:S(2)}, u32[]{:S(2)}) collective-permute-start(bf16[32,2048]{1,0:T(8,128)(2,1)S(1)} %bitcast.44), channel_id=1, source_target_pairs={{0,32},{32,64},{64,96},{96,128},{128,160},{160,192},{192,224},{224... | collective-permute-start | bytes 393224 | tf_op jit(solution)/shard_map/ppermute | solution.py:49
  87.5 10.4 %copy-start.4 = (s32[8]{0:T(128)S(1)}, s32[8]{0:T(128)}, u32[]{:S(2)}) copy-start(s32[8]{0:T(128)} %param.5) | copy-start | bytes 100
  91.6 17.2 %collective-permute-start.9 = (f32[288,384]{1,0:T(8,128)S(1)}, f32[288,384]{1,0:T(8,128)S(1)}, u32[]{:S(2)}, u32[]{:S(2)}) collective-permute-start(f32[288,384]{1,0:T(8,128)S(1)} %get-tuple-element.8), channel_id=1, source_target_pairs={{0,1},{1,2},{2,3},{3,4},{4,5},{5,6},{6,7},{7,8},{8,9},{9,10},{10,1... | collective-permute-start | bytes 1327112 | tf_op jit(solution)/shard_map/ppermute | solution.py:272
  93.9 15.0 %collective-permute-start.10 = (f32[288,128]{1,0:T(8,128)S(1)}, f32[288,128]{1,0:T(8,128)S(1)}, u32[]{:S(2)}, u32[]{:S(2)}) collective-permute-start(f32[288,128]{1,0:T(8,128)S(1)} %get-tuple-element.10), channel_id=1, source_target_pairs={{1,0},{2,1},{3,2},{4,3},{5,4},{6,5},{7,6},{8,7},{9,8},{10,9},{11,1... | collective-permute-start | bytes 442376 | tf_op jit(solution)/shard_map/ppermute | solution.py:273

commit v3 on v0

v3 whole, which is shorter than its diff:
```python
import functools
import math

import jax
import jax.numpy as jnp
from jax import lax
from jax.experimental import pallas as pl
from jax.experimental.pallas import tpu as pltpu
from jax.sharding import PartitionSpec as P

SEQ = 20
RAD = 10
TOP = 32
LEFT = 384
LANES = 128
ROWS = TOP + 256
COLUMNS = 1024
HALO = LEFT // LANES
TILES = HALO + COLUMNS // LANES
FIRST, LAST = HALO + 1, TILES - 1
SHIFTS = ((1, 0), (3, 0), (0, 1), (1, 1), (3, 1), (2, 0), (2, 1))


def tile(c):
    return slice(c * LANES, (c + 1) * LANES)


def across(dy, dx, core):
    return [
        (y * 4 + x * 2 + c, (y + dy) % 4 * 4 + (x + dx) % 2 * 2 + (c ^ core))
        for y in range(4)
        for x in range(2)
        for c in range(2)
    ]


def gather(queries, frames):
    depth = queries.shape[-1]
    groups = [[z * 2 + side for z in range(16)] for side in range(2)]
    sides = [(i, i ^ 1) for i in range(32)]
    copies = jnp.broadcast_to(queries[None], (16,) + queries.shape)
    copies, frames = lax.optimization_barrier((copies, frames))
    near = lax.all_to_all(copies, "ma", 0, 0, axis_index_groups=groups)
    own = [frames] + [lax.ppermute(frames, "pb", across(dy, dx, 0)) for dy, dx in SHIFTS]
    own = [jnp.stack(own[:4]), jnp.stack(own[4:])]
    other = [lax.ppermute(part, "pb", across(0, 0, 1)) for part in own]
    far = lax.ppermute(near, "ma", sides)
    near_top = lax.ppermute(near[14:], "pb", [(i, i + 1) for i in range(15)])
    far_top = lax.ppermute(near_top, "ma", sides)
    rows = [v.reshape(-1, depth) for v in (near, far, near_top, far_top)]
    return rows, own + other


def fill_rows(refs, rows_ref):
    at = 0
    for ref in refs:
        rows_ref[at : at + ref.shape[0]] = ref[...]
        at += ref.shape[0]


def products(at_ref, rows_ref, map_refs, begin, width):
    total = None
    for g in range(8):
        one = pl.multiple_of(at_ref[2 * g] * LANES, LANES)
        two = pl.multiple_of(at_ref[2 * g + 1] * LANES, LANES)
        lhs = jnp.concatenate([rows_ref[:, pl.ds(one, LANES)], rows_ref[:, pl.ds(two, LANES)]], axis=1)
        own, other = map_refs[g // 4], map_refs[2 + g // 4]
        rhs = jnp.concatenate([own[g % 4, pl.ds(begin, width)], other[g % 4, pl.ds(begin, width)]], axis=1)
        part = lax.dot_general(lhs, rhs, (((1,), (1,)), ((), ())), preferred_element_type=jnp.float32)
        total = part if total is None else total + part
    return total


def place_rows(side, out_ref, cols, value):
    for r in range(ROWS // 8):
        if r < 32:
            start, far = TOP + 16 * (r % 16), r // 16
        else:
            start, far = 16 * (r % 2), (r - 32) // 2
        start = pl.multiple_of(start + 8 * (side if far == 0 else 1 - side), 8)
        out_ref[pl.ds(start, 8), cols] = value[8 * r : 8 * r + 8]


def edge_kernel(at_ref, *refs):
    row_refs, map_refs, (last_ref, lead_ref, rows_ref) = refs[:4], refs[4:8], refs[8:]
    fill_rows(row_refs, rows_ref)
    side = at_ref[16]
    begin = COLUMNS - LEFT
    for at, width in ((0, 256), (256, 128)):
        value = products(at_ref, rows_ref, map_refs, begin + at, width)
        place_rows(side, last_ref, slice(at, at + width), value)
    place_rows(side, lead_ref, slice(0, LANES), products(at_ref, rows_ref, map_refs, 0, LANES))


def split_tile(split_ref, slot, value):
    for kind, rest in enumerate((value, value * value)):
        for part in range(3):
            piece = rest.astype(jnp.bfloat16)
            split_ref[3 * kind + part, :, tile(slot)] = piece
            if part < 2:
                rest = rest - piece.astype(jnp.float32)


def band_of():
    at_in = lax.broadcasted_iota(jnp.int32, (4 * LANES, 2 * LANES), 0)
    at_out = lax.broadcasted_iota(jnp.int32, (4 * LANES, 2 * LANES), 1) + LANES
    return jnp.where(jnp.abs(at_in - at_out) <= RAD, 1.0, 0.0).astype(jnp.bfloat16)


def contrast_pair(split_ref, slot, band, tiles):
    found = []
    for kind in range(2):
        total = None
        for part in range(3):
            lhs = split_ref[3 * kind + part, :, slot * LANES : (slot + 4) * LANES]
            term = jnp.dot(lhs, band, preferred_element_type=jnp.float32)
            total = term if total is None else total + term
        found.append(total * (1.0 / (2 * RAD + 1)))
    mean, square = found
    scale = lax.rsqrt(square - mean * mean + 1.0)
    return [(v - mean[:, tile(i)]) * scale[:, tile(i)] for i, v in enumerate(tiles)]


def middle_kernel(at_ref, *refs):
    row_refs, map_refs = refs[:4], refs[4:8]
    last_ref, lead_ref, next_ref, inner_ref, rows_ref, mid_ref, split_ref = refs[8:]
    fill_rows(row_refs, rows_ref)
    side = at_ref[16]
    for at in (0, 256):
        value = products(at_ref, rows_ref, map_refs, LANES + at, 256)
        place_rows(side, mid_ref, slice(at, at + 256), value)
    next_ref[...] = mid_ref[:, tile(0)]

    def score(c):
        if c == HALO:
            return lead_ref[...]
        if c < HALO + 5:
            return mid_ref[:, tile(c - HALO - 1)]
        return last_ref[:, tile(c - HALO - 5)]

    for c in range(HALO, TILES):
        split_tile(split_ref, c - HALO, score(c))
    band = band_of()
    for c in range(FIRST, LAST, 2):
        values = contrast_pair(split_ref, c - HALO - 1, band, [score(c), score(c + 1)])
        for half, value in enumerate(values):
            inner_ref[c - FIRST + half] = value


def best_kernel(slopes_ref, left_ref, right_ref, last_ref, lead_ref, next_ref, inner_ref, out_ref, split_ref, x_ref, lag_ref, sum_ref, best_ref):
    first_map = slopes_ref[8] == 0
    empty = jnp.zeros((ROWS, LANES), jnp.bfloat16)
    band = band_of()
    edge = [left_ref[:, tile(c)] for c in range(HALO)] + [lead_ref[...], next_ref[...]]
    for part in range(6):
        split_ref[part, :, tile(0)] = empty
    for c, value in enumerate(edge):
        split_tile(split_ref, c + 1, value)
    for c in (0, 2):
        values = contrast_pair(split_ref, c, band, edge[c : c + 2])
        for half, value in enumerate(values):
            if c + half < HALO:
                value = jnp.where(first_map, 0.0, value)
            x_ref[c + half] = value
    edge = [last_ref[:, tile(1)], last_ref[:, tile(2)], right_ref[...]]
    for part in range(6):
        split_ref[part, :, tile(3)] = empty
    for c, value in enumerate(edge):
        split_tile(split_ref, c, value)
    x_ref[4] = contrast_pair(split_ref, 0, band, edge[1:2])[0]

    def contrast_at(c, row):
        take = pl.ds(row, 8, stride=32)
        if c < FIRST:
            return x_ref[c, take]
        return inner_ref[c - FIRST, take] if c < LAST else x_ref[4, take]

    steps = SEQ - 1 + 32
    zero = jnp.zeros((8, LANES), jnp.float32)
    for t in range(steps):
        for c in range(HALO):
            lag_ref[t, c] = zero
        for c in range(TILES):
            lag_ref[t, c + HALO] = contrast_at(c, t + TOP - SEQ + 1)
    for index in range(8):
        for c in range(TILES):
            sum_ref[index, c] = zero

    lane = lax.broadcasted_iota(jnp.int32, (8, LANES), 1)

    def step(t, begin, drop, emit):
        best = [None] * TILES
        for index in range(8):
            v = slopes_ref[index]
            by = v
            far = SEQ * v
            whole = far // LANES
            far = far % LANES
            before = zero
            old = None

            def dropped(c):
                return pltpu.roll(lag_ref[t - SEQ, c + HALO - whole], far, 1)

            if drop:
                old = dropped(begin - 1)
            for c in range(begin, TILES):
                moved = pltpu.roll(sum_ref[index, c], by, 1)
                total = jnp.where(lane < by, before, moved) + lag_ref[t, c + HALO]
                before = moved
                if drop:
                    gone = dropped(c)
                    total = total - jnp.where(lane < far, old, gone)
                    old = gone
                sum_ref[index, c] = total
                if emit and c >= HALO:
                    best[c] = total if best[c] is None else jnp.maximum(best[c], total)
        if emit:
            for c in range(HALO, TILES):
                best_ref[c - HALO, pl.ds(t - SEQ + 1, 8, stride=32)] = best[c] * (1.0 / math.sqrt(SEQ))

    def phase(first, last, begin, drop, emit):
        def body(t, carry):
            step(t, begin, drop, emit)
            return carry

        lax.fori_loop(first, last, body, 0)

    phase(0, SEQ - 1, 0, False, False)
    step(SEQ - 1, 0, False, True)
    phase(SEQ, 34, 0, True, True)
    phase(34, 43, 1, True, True)
    phase(43, steps, 2, True, True)
    for c in range(COLUMNS // LANES):
        out_ref[:, tile(c)] = best_ref[c]


SMEM = pl.BlockSpec(memory_space=pltpu.SMEM)
VMEM = pl.BlockSpec(memory_space=pltpu.VMEM)
SPLIT = pltpu.VMEM((6, ROWS, 8 * LANES), jnp.bfloat16)


def local(queries, map_descriptors, slopes):
    ma = lax.axis_index("ma")
    pb = lax.axis_index("pb")
    rows, frames = gather(queries[0], map_descriptors)
    y, x, core = pb // 4, pb // 2 % 2, pb % 2
    at = []
    for dy, dx in ((0, 0),) + SHIFTS:
        chip = (y - dy + 4) % 4 * 2 + (x - dx + 2) % 2
        at += [2 * chip + core, 2 * chip + 1 - core]
    at = jnp.stack([jnp.asarray(v, jnp.int32) for v in at + [ma % 2]])
    block = lambda width: jax.ShapeDtypeStruct((ROWS, width), jnp.float32)
    limit = pltpu.CompilerParams(vmem_limit_bytes=40 << 20)
    rows_scratch = pltpu.VMEM((ROWS, 2048), jnp.bfloat16)
    last, lead = pl.pallas_call(
        edge_kernel,
        name="edges",
        out_shape=(block(LEFT), block(LANES)),
        in_specs=[SMEM] + [VMEM] * 8,
        out_specs=(VMEM,) * 2,
        scratch_shapes=[rows_scratch],
        compiler_params=limit,
        cost_estimate=pl.CostEstimate(flops=2 * ROWS * 512 * 2048, bytes_accessed=6 << 20, transcendentals=0),
    )(at, *rows, *frames)
    left = lax.ppermute(last, "ma", [(i, i + 1) for i in range(31)])
    right = lax.ppermute(lead, "ma", [(i + 1, i) for i in range(31)])
    after, inner = pl.pallas_call(
        middle_kernel,
        name="middle",
        out_shape=(block(LANES), jax.ShapeDtypeStruct((LAST - FIRST, ROWS, LANES), jnp.float32)),
        in_specs=[SMEM] + [VMEM] * 10,
        out_specs=(VMEM,) * 2,
        scratch_shapes=[rows_scratch, pltpu.VMEM((ROWS, 512), jnp.float32), SPLIT],
        compiler_params=limit,
        cost_estimate=pl.CostEstimate(flops=8 * ROWS * 512 * 2048, bytes_accessed=16 << 20, transcendentals=0),
    )(at, *rows, *frames, last, lead)
    marks = jnp.concatenate([slopes, ma[None].astype(jnp.int32)])
    best = best_of(marks, left, right, last, lead, after, inner)
    return best[None]


def best_of(marks, left, right, last, lead, after, inner):
    return pl.pallas_call(
        best_kernel,
        name="best",
        out_shape=jax.ShapeDtypeStruct((ROWS - TOP, COLUMNS), jnp.float32),
        in_specs=[SMEM] + [VMEM] * 6,
        out_specs=VMEM,
        scratch_shapes=[
            SPLIT,
            pltpu.VMEM((5, ROWS, LANES), jnp.float32),
            pltpu.VMEM((SEQ + 31, TILES + HALO, 8, LANES), jnp.float32),
            pltpu.VMEM((8, TILES, 8, LANES), jnp.float32),
            pltpu.VMEM((COLUMNS // LANES, ROWS - TOP, LANES), jnp.float32),
        ],
        compiler_params=pltpu.CompilerParams(vmem_limit_bytes=40 << 20),
        cost_estimate=pl.CostEstimate(flops=60 << 20, bytes_accessed=4 << 20, transcendentals=0),
    )(marks, left, right, last, lead, after, inner)


def solution(mesh):
    return jax.shard_map(
        local,
        mesh=mesh,
        in_specs=(P(None, ("pb", "ma"), None), P("ma", "pb"), P()),
        out_specs=P(None, "pb", "ma"),
        check_vma=False,
    )
```

time: 508 us -> 116 us (0.23)
  the two profiles are of different devices: /device:TPU:104 before, /device:TPU:37 now
where the time goes in v3:
time: 116 us; the launch traced here: 115 us
  starting transfers between devices  67 us (58%)
  Pallas kernels  24.7 us (21%)
  waiting for transfers between devices  21.2 us (18%)
  local copies, waits for them, and re-layouts  1.71 us (1%)
    ppermute x7, starting transfers between devices, gather(): lax.ppermute(frames, 'pb', across(dy, dx, 0))  25.6 us
    pallas_call x1, Pallas kernels, best_of(): pl.pallas_call(best_kernel, name='best', out_shape=jax.ShapeDtypeStruct((...  17.6 us
    all_to_all x1, starting transfers between devices, gather(): near = lax.all_to_all(copies, 'ma', 0, 0, axis_index_groups=groups)  14.8 us
    ppermute x2, starting transfers between devices, gather(): other = [lax.ppermute(part, 'pb', across(0, 0, 1)) for part in own]  11.4 us
    ppermute x1, waiting for transfers between devices, gather(): near_top = lax.ppermute(near[14:], 'pb', [(i, i + 1) for i in range(15)])  9.01 us
    ppermute x1, waiting for transfers between devices, local(): right = lax.ppermute(lead, 'ma', [(i + 1, i) for i in range(31)])  7.42 us
    pallas_call x1, Pallas kernels, local(): pl.pallas_call(middle_kernel, name='middle', out_shape=(block(LANES), jax...  4.34 us
    ppermute x1, starting transfers between devices, local(): right = lax.ppermute(lead, 'ma', [(i + 1, i) for i in range(31)])  4.25 us
  transfers between devices with their start and end apart: 15, of which 4 were waited for; matrix products, arithmetic and copies ran while one was open for 0% of the time, Pallas kernels for 4%

profile of v3, /device:TPU:37, one launch (start us, length us, event | category | flops | bytes accessed | tf_op | source)
XLA Modules:
  0.0 115.4 jit_solution(8212519182324306522)
XLA Ops:
  0.0 1.6 %broadcast_in_dim.15 = bf16[16,8,2048]{2,1,0:T(8,128)(2,1)} broadcast(bf16[8,2048]{1,0:T(8,128)(2,1)} %bitcast.48), dimensions={1,2} | broadcast | bytes 557056 | tf_op jit(solution)/shard_map/broadcast_in_dim | solution.py:41
  1.6 0.0 copy-start
  1.6 14.8 %all-to-all-start = ((bf16[16,8,2048]{2,1,0:T(8,128)(2,1)}), bf16[16,8,2048]{2,1,0:T(8,128)(2,1)S(1)}, u32[]{:S(2)}, u32[]{:S(2)}) async-start(bf16[16,8,2048]{2,1,0:T(8,128)(2,1)} %broadcast_in_dim.15), calls=%async_computation | async-start | bytes 1048576 | tf_op jit(solution)/shard_map/all_to_all | solution.py:43
  16.4 0.0 copy-done
  16.4 2.1 %collective-permute-start.5 = (bf16[1024,128]{1,0:T(8,128)(2,1)S(1)}, bf16[1024,128]{1,0:T(8,128)(2,1)S(1)}, u32[]{:S(2)}, u32[]{:S(2)}) collective-permute-start(bf16[1024,128]{1,0:T(8,128)(2,1)S(1)} %copy-done), channel_id=1, source_target_pairs={{0,64},{32,96},{64,0},{96,32},{128,192},{160,224},{192,128},{224,1... | collective-permute-start | bytes 786440 | tf_op jit(solution)/shard_map/ppermute | solution.py:44
  18.5 4.6 %collective-permute-start.4 = (bf16[1024,128]{1,0:T(8,128)(2,1)S(1)}, bf16[1024,128]{1,0:T(8,128)(2,1)S(1)}, u32[]{:S(2)}, u32[]{:S(2)}) collective-permute-start(bf16[1024,128]{1,0:T(8,128)(2,1)S(1)} %copy-done), channel_id=1, source_target_pairs={{0,384},{32,416},{64,448},{96,480},{128,0},{160,32},{192,64},{224,... | collective-permute-start | bytes 786440 | tf_op jit(solution)/shard_map/ppermute | solution.py:44
  23.2 1.9 %collective-permute-start.3 = (bf16[1024,128]{1,0:T(8,128)(2,1)S(1)}, bf16[1024,128]{1,0:T(8,128)(2,1)S(1)}, u32[]{:S(2)}, u32[]{:S(2)}) collective-permute-start(bf16[1024,128]{1,0:T(8,128)(2,1)S(1)} %copy-done), channel_id=1, source_target_pairs={{0,128},{32,160},{64,192},{96,224},{128,256},{160,288},{192,320},{... | collective-permute-start | bytes 786440 | tf_op jit(solution)/shard_map/ppermute | solution.py:44
  25.1 6.0 %collective-permute-start.9 = (bf16[1024,128]{1,0:T(8,128)(2,1)S(1)}, bf16[1024,128]{1,0:T(8,128)(2,1)S(1)}, u32[]{:S(2)}, u32[]{:S(2)}) collective-permute-start(bf16[1024,128]{1,0:T(8,128)(2,1)S(1)} %copy-done), channel_id=1, source_target_pairs={{0,320},{32,352},{64,256},{96,288},{128,448},{160,480},{192,384},{... | collective-permute-start | bytes 786440 | tf_op jit(solution)/shard_map/ppermute | solution.py:44
  31.1 3.2 %collective-permute-start.8 = (bf16[1024,128]{1,0:T(8,128)(2,1)S(1)}, bf16[1024,128]{1,0:T(8,128)(2,1)S(1)}, u32[]{:S(2)}, u32[]{:S(2)}) collective-permute-start(bf16[1024,128]{1,0:T(8,128)(2,1)S(1)} %copy-done), channel_id=1, source_target_pairs={{0,256},{32,288},{64,320},{96,352},{128,384},{160,416},{192,448},{... | collective-permute-start | bytes 786440 | tf_op jit(solution)/shard_map/ppermute | solution.py:44
  34.4 0.0 collective-permute-done.5
  34.4 4.5 %collective-permute-start.7 = (bf16[1024,128]{1,0:T(8,128)(2,1)S(1)}, bf16[1024,128]{1,0:T(8,128)(2,1)S(1)}, u32[]{:S(2)}, u32[]{:S(2)}) collective-permute-start(bf16[1024,128]{1,0:T(8,128)(2,1)S(1)} %copy-done), channel_id=1, source_target_pairs={{0,448},{32,480},{64,384},{96,416},{128,64},{160,96},{192,0},{224,... | collective-permute-start | bytes 786440 | tf_op jit(solution)/shard_map/ppermute | solution.py:44
  38.9 0.0 collective-permute-done.4
  38.9 3.2 %collective-permute-start.6 = (bf16[1024,128]{1,0:T(8,128)(2,1)S(1)}, bf16[1024,128]{1,0:T(8,128)(2,1)S(1)}, u32[]{:S(2)}, u32[]{:S(2)}) collective-permute-start(bf16[1024,128]{1,0:T(8,128)(2,1)S(1)} %copy-done), channel_id=1, source_target_pairs={{0,192},{32,224},{64,128},{96,160},{128,320},{160,352},{192,256},{... | collective-permute-start | bytes 786440 | tf_op jit(solution)/shard_map/ppermute | solution.py:44
  42.1 0.0 collective-permute-done.3
  42.1 0.1 pad_maximum_fusion.refs_4_
  42.3 6.0 %collective-permute-start.10 = (bf16[4,1024,128]{2,1,0:T(8,128)(2,1)S(1)}, bf16[4,1024,128]{2,1,0:T(8,128)(2,1)}, u32[]{:S(2)}, u32[]{:S(2)}) collective-permute-start(bf16[4,1024,128]{2,1,0:T(8,128)(2,1)S(1)} %pad_maximum_fusion.refs_4_), channel_id=1, source_target_pairs={{0,32},{32,0},{64,96},{96,64},{128,160},{160,128},{192,224},{224,1... | collective-permute-start | bytes 3145736 | tf_op jit(solution)/shard_map/ppermute | solution.py:46
  48.3 0.0 collective-permute-done.9
  48.3 0.0 collective-permute-done.8
  48.3 0.0 collective-permute-done.7
  48.3 1.9 %collective-permute-done.6 = bf16[1024,128]{1,0:T(8,128)(2,1)S(1)} collective-permute-done((bf16[1024,128]{1,0:T(8,128)(2,1)S(1)}, bf16[1024,128]{1,0:T(8,128)(2,1)S(1)}, u32[]{:S(2)}, u32[]{:S(2)}) %collective-permute-start.6) | collective-permute-done | bytes 262176 | tf_op jit(solution)/shard_map/ppermute | solution.py:44
  50.3 0.1 pad_maximum_fusion.1.refs_5_
  50.4 5.4 %collective-permute-start.11 = (bf16[4,1024,128]{2,1,0:T(8,128)(2,1)S(1)}, bf16[4,1024,128]{2,1,0:T(8,128)(2,1)}, u32[]{:S(2)}, u32[]{:S(2)}) collective-permute-start(bf16[4,1024,128]{2,1,0:T(8,128)(2,1)S(1)} %pad_maximum_fusion.1.refs_5_), channel_id=1, source_target_pairs={{0,32},{32,0},{64,96},{96,64},{128,160},{160,128},{192,224},{224,1... | collective-permute-start | bytes 3145736 | tf_op jit(solution)/shard_map/ppermute | solution.py:46
  55.8 0.0 all-to-all-done
  55.8 3.7 %collective-permute-start = (bf16[16,8,2048]{2,1,0:T(8,128)(2,1)S(1)}, bf16[16,8,2048]{2,1,0:T(8,128)(2,1)S(1)}, u32[]{:S(2)}, u32[]{:S(2)}) collective-permute-start(bf16[16,8,2048]{2,1,0:T(8,128)(2,1)S(1)} %all-to-all-done), channel_id=1, source_target_pairs={{0,1},{1,0},{2,3},{3,2},{4,5},{5,4},{6,7},{7,6},{8,9},{9,8},{10,11... | collective-permute-start | bytes 1572872 | tf_op jit(solution)/shard_map/ppermute | solution.py:47
  59.5 3.4 %collective-permute-start.1 = (bf16[2,8,2048]{2,1,0:T(8,128)(2,1)S(1)}, bf16[2,8,2048]{2,1,0:T(8,128)(2,1)S(1)}, u32[]{:S(2)}, u32[]{:S(2)}) collective-permute-start(bf16[2,8,2048]{2,1,0:T(8,128)(2,1)S(1)} %slice.4), channel_id=1, source_target_pairs={{0,32},{32,64},{64,96},{96,128},{128,160},{160,192},{192,224},{224... | collective-permute-start | bytes 196616 | tf_op jit(solution)/shard_map/ppermute | solution.py:48
  62.9 9.0 %collective-permute-done.1 = bf16[2,8,2048]{2,1,0:T(8,128)(2,1)S(1)} collective-permute-done((bf16[2,8,2048]{2,1,0:T(8,128)(2,1)S(1)}, bf16[2,8,2048]{2,1,0:T(8,128)(2,1)S(1)}, u32[]{:S(2)}, u32[]{:S(2)}) %collective-permute-start.1) | collective-permute-done | bytes 65568 | tf_op jit(solution)/shard_map/ppermute | solution.py:48
  71.9 1.9 %collective-permute-start.2 = (bf16[2,8,2048]{2,1,0:T(8,128)(2,1)S(1)}, bf16[2,8,2048]{2,1,0:T(8,128)(2,1)S(1)}, u32[]{:S(2)}, u32[]{:S(2)}) collective-permute-start(bf16[2,8,2048]{2,1,0:T(8,128)(2,1)S(1)} %collective-permute-done.1), channel_id=1, source_target_pairs={{0,1},{1,0},{2,3},{3,2},{4,5},{5,4},{6,7},{7,6},{8,9},{9,8},{10,11... | collective-permute-start | bytes 196616 | tf_op jit(solution)/shard_map/ppermute | solution.py:49
  74.0 0.1 stack.101.at_ref
  74.1 0.0 collective-permute-done.10.refs_6_
  74.1 0.0 collective-permute-done.11.refs_7_
  74.1 2.8 %collective-permute-done.2 = bf16[2,8,2048]{2,1,0:T(8,128)(2,1)S(1)} collective-permute-done((bf16[2,8,2048]{2,1,0:T(8,128)(2,1)S(1)}, bf16[2,8,2048]{2,1,0:T(8,128)(2,1)S(1)}, u32[]{:S(2)}, u32[]{:S(2)}) %collective-permute-start.2) | collective-permute-done | bytes 65568 | tf_op jit(solution)/shard_map/ppermute | solution.py:49
  76.9 0.0 collective-permute-done
  76.9 2.8 %edges.1 = (f32[288,384]{1,0:T(8,128)S(1)}, f32[288,128]{1,0:T(8,128)S(1)}) custom-call(s32[17]{0:T(128)S(1)} %stack.101.at_ref, bf16[128,2048]{1,0:T(8,128)(2,1)S(1)} %bitcast.32, bf16[128,2048]{1,0:T(8,128)(2,1)S(1)} %bitcast.34, bf16[16,2048]{1,0:T(8,128)(2,1)S(1)} %bitcast.36, bf16[16,2048]{1,0:T(8,128)(2,1)S(1)} %bitcast.38, ...), custom_call_target="tpu_custom_call" | custom-call | flops 603979776 | bytes 6291456 | tf_op jit(solution)/shard_map/edges/pallas_call | solution.py:256
  79.7 0.0 copy-start.1
  79.7 1.9 %collective-permute-start.12 = (f32[288,384]{1,0:T(8,128)S(1)}, f32[288,384]{1,0:T(8,128)S(1)}, u32[]{:S(2)}, u32[]{:S(2)}) collective-permute-start(f32[288,384]{1,0:T(8,128)S(1)} %get-tuple-element.13.refs_8_.last_ref), channel_id=1, source_target_pairs={{0,1},{1,2},{2,3},{3,4},{4,5},{5,6},{6,7},{7,8},{8,9},{9,10},{10,1... | collective-permute-start | bytes 1327112 | tf_op jit(solution)/shard_map/ppermute | solution.py:266
  81.7 0.0 copy-done.1
  81.7 0.1 pad_add_fusion.slopes_ref
  81.8 4.2 %collective-permute-start.13 = (f32[288,128]{1,0:T(8,128)S(1)}, f32[288,128]{1,0:T(8,128)S(1)}, u32[]{:S(2)}, u32[]{:S(2)}) collective-permute-start(f32[288,128]{1,0:T(8,128)S(1)} %get-tuple-element.14.refs_9_.lead_ref), channel_id=1, source_target_pairs={{1,0},{2,1},{3,2},{4,3},{5,4},{6,5},{7,6},{8,7},{9,8},{10,9},{11,1... | collective-permute-start | bytes 442376 | tf_op jit(solution)/shard_map/ppermute | solution.py:267
  86.0 4.3 %middle.1 = (f32[288,128]{1,0:T(8,128)S(1)}, f32[6,288,128]{2,1,0:T(8,128)S(1)}) custom-call(s32[17]{0:T(128)S(1)} %stack.101.at_ref, bf16[128,2048]{1,0:T(8,128)(2,1)S(1)} %bitcast.33, bf16[128,2048]{1,0:T(8,128)(2,1)S(1)} %bitcast.35, bf16[16,2048]{1,0:T(8,128)(2,1)S(1)} %bitcast.37, bf16[16,2048]{1,0:T(8,128)(2,1)S(1)} %bitcast.39, ...), custom_call_target="tpu_custom_call" | custom-call | flops 2415919104 | bytes 16777216 | tf_op jit(solution)/shard_map/middle/pallas_call | solution.py:268
  90.4 7.4 %collective-permute-done.13.right_ref = f32[288,128]{1,0:T(8,128)S(1)} collective-permute-done((f32[288,128]{1,0:T(8,128)S(1)}, f32[288,128]{1,0:T(8,128)S(1)}, u32[]{:S(2)}, u32[]{:S(2)}) %collective-permute-start.13) | collective-permute-done | bytes 147488 | tf_op jit(solution)/shard_map/ppermute | solution.py:267
  97.8 0.0 collective-permute-done.12.left_ref
  97.8 17.6 %best.1 = f32[256,1024]{1,0:T(8,128)} custom-call(s32[9]{0:T(128)S(1)} %pad_add_fusion.slopes_ref, f32[288,384]{1,0:T(8,128)S(1)} %collective-permute-done.12.left_ref, f32[288,128]{1,0:T(8,128)S(1)} %collective-permute-done.13.right_ref, f32[288,384]{1,0:T(8,128)S(1)} %get-tuple-element.13.refs_8_.last_ref, ...), custom_call_target="tpu_custom_call" | custom-call | flops 62914560 | bytes 4194304 | tf_op jit(solution)/shard_map/best/pallas_call | solution.py:284
  (1 shorter events, 0.0 us)
Async XLA Ops:
  1.6 14.8 %copy-start = (bf16[1024,128]{1,0:T(8,128)(2,1)S(1)}, bf16[1024,128]{1,0:T(8,128)(2,1)}, u32[]{:S(2)}) copy-start(bf16[1024,128]{1,0:T(8,128)(2,1)} %param.4) | copy-start | bytes 786436
  1.6 54.2 %all-to-all-start = ((bf16[16,8,2048]{2,1,0:T(8,128)(2,1)}), bf16[16,8,2048]{2,1,0:T(8,128)(2,1)S(1)}, u32[]{:S(2)}, u32[]{:S(2)}) async-start(bf16[16,8,2048]{2,1,0:T(8,128)(2,1)} %broadcast_in_dim.15), calls=%async_computation | async-start | bytes 1048576 | tf_op jit(solution)/shard_map/all_to_all | solution.py:43
  16.4 18.0 %collective-permute-start.5 = (bf16[1024,128]{1,0:T(8,128)(2,1)S(1)}, bf16[1024,128]{1,0:T(8,128)(2,1)S(1)}, u32[]{:S(2)}, u32[]{:S(2)}) collective-permute-start(bf16[1024,128]{1,0:T(8,128)(2,1)S(1)} %copy-done), channel_id=1, source_target_pairs={{0,64},{32,96},{64,0},{96,32},{128,192},{160,224},{192,128},{224,1... | collective-permute-start | bytes 786440 | tf_op jit(solution)/shard_map/ppermute | solution.py:44
  18.5 20.4 %collective-permute-start.4 = (bf16[1024,128]{1,0:T(8,128)(2,1)S(1)}, bf16[1024,128]{1,0:T(8,128)(2,1)S(1)}, u32[]{:S(2)}, u32[]{:S(2)}) collective-permute-start(bf16[1024,128]{1,0:T(8,128)(2,1)S(1)} %copy-done), channel_id=1, source_target_pairs={{0,384},{32,416},{64,448},{96,480},{128,0},{160,32},{192,64},{224,... | collective-permute-start | bytes 786440 | tf_op jit(solution)/shard_map/ppermute | solution.py:44
  23.2 18.9 %collective-permute-start.3 = (bf16[1024,128]{1,0:T(8,128)(2,1)S(1)}, bf16[1024,128]{1,0:T(8,128)(2,1)S(1)}, u32[]{:S(2)}, u32[]{:S(2)}) collective-permute-start(bf16[1024,128]{1,0:T(8,128)(2,1)S(1)} %copy-done), channel_id=1, source_target_pairs={{0,128},{32,160},{64,192},{96,224},{128,256},{160,288},{192,320},{... | collective-permute-start | bytes 786440 | tf_op jit(solution)/shard_map/ppermute | solution.py:44
  25.1 23.2 %collective-permute-start.9 = (bf16[1024,128]{1,0:T(8,128)(2,1)S(1)}, bf16[1024,128]{1,0:T(8,128)(2,1)S(1)}, u32[]{:S(2)}, u32[]{:S(2)}) collective-permute-start(bf16[1024,128]{1,0:T(8,128)(2,1)S(1)} %copy-done), channel_id=1, source_target_pairs={{0,320},{32,352},{64,256},{96,288},{128,448},{160,480},{192,384},{... | collective-permute-start | bytes 786440 | tf_op jit(solution)/shard_map/ppermute | solution.py:44
  31.1 17.2 %collective-permute-start.8 = (bf16[1024,128]{1,0:T(8,128)(2,1)S(1)}, bf16[1024,128]{1,0:T(8,128)(2,1)S(1)}, u32[]{:S(2)}, u32[]{:S(2)}) collective-permute-start(bf16[1024,128]{1,0:T(8,128)(2,1)S(1)} %copy-done), channel_id=1, source_target_pairs={{0,256},{32,288},{64,320},{96,352},{128,384},{160,416},{192,448},{... | collective-permute-start | bytes 786440 | tf_op jit(solution)/shard_map/ppermute | solution.py:44
  34.4 13.9 %collective-permute-start.7 = (bf16[1024,128]{1,0:T(8,128)(2,1)S(1)}, bf16[1024,128]{1,0:T(8,128)(2,1)S(1)}, u32[]{:S(2)}, u32[]{:S(2)}) collective-permute-start(bf16[1024,128]{1,0:T(8,128)(2,1)S(1)} %copy-done), channel_id=1, source_target_pairs={{0,448},{32,480},{64,384},{96,416},{128,64},{160,96},{192,0},{224,... | collective-permute-start | bytes 786440 | tf_op jit(solution)/shard_map/ppermute | solution.py:44
  38.9 11.3 %collective-permute-start.6 = (bf16[1024,128]{1,0:T(8,128)(2,1)S(1)}, bf16[1024,128]{1,0:T(8,128)(2,1)S(1)}, u32[]{:S(2)}, u32[]{:S(2)}) collective-permute-start(bf16[1024,128]{1,0:T(8,128)(2,1)S(1)} %copy-done), channel_id=1, source_target_pairs={{0,192},{32,224},{64,128},{96,160},{128,320},{160,352},{192,256},{... | collective-permute-start | bytes 786440 | tf_op jit(solution)/shard_map/ppermute | solution.py:44
  42.3 31.8 %collective-permute-start.10 = (bf16[4,1024,128]{2,1,0:T(8,128)(2,1)S(1)}, bf16[4,1024,128]{2,1,0:T(8,128)(2,1)}, u32[]{:S(2)}, u32[]{:S(2)}) collective-permute-start(bf16[4,1024,128]{2,1,0:T(8,128)(2,1)S(1)} %pad_maximum_fusion.refs_4_), channel_id=1, source_target_pairs={{0,32},{32,0},{64,96},{96,64},{128,160},{160,128},{192,224},{224,1... | collective-permute-start | bytes 3145736 | tf_op jit(solution)/shard_map/ppermute | solution.py:46
  50.4 23.7 %collective-permute-start.11 = (bf16[4,1024,128]{2,1,0:T(8,128)(2,1)S(1)}, bf16[4,1024,128]{2,1,0:T(8,128)(2,1)}, u32[]{:S(2)}, u32[]{:S(2)}) collective-permute-start(bf16[4,1024,128]{2,1,0:T(8,128)(2,1)S(1)} %pad_maximum_fusion.1.refs_5_), channel_id=1, source_target_pairs={{0,32},{32,0},{64,96},{96,64},{128,160},{160,128},{192,224},{224,1... | collective-permute-start | bytes 3145736 | tf_op jit(solution)/shard_map/ppermute | solution.py:46
  55.8 21.1 %collective-permute-start = (bf16[16,8,2048]{2,1,0:T(8,128)(2,1)S(1)}, bf16[16,8,2048]{2,1,0:T(8,128)(2,1)S(1)}, u32[]{:S(2)}, u32[]{:S(2)}) collective-permute-start(bf16[16,8,2048]{2,1,0:T(8,128)(2,1)S(1)} %all-to-all-done), channel_id=1, source_target_pairs={{0,1},{1,0},{2,3},{3,2},{4,5},{5,4},{6,7},{7,6},{8,9},{9,8},{10,11... | collective-permute-start | bytes 1572872 | tf_op jit(solution)/shard_map/ppermute | solution.py:47
  59.5 12.4 %collective-permute-start.1 = (bf16[2,8,2048]{2,1,0:T(8,128)(2,1)S(1)}, bf16[2,8,2048]{2,1,0:T(8,128)(2,1)S(1)}, u32[]{:S(2)}, u32[]{:S(2)}) collective-permute-start(bf16[2,8,2048]{2,1,0:T(8,128)(2,1)S(1)} %slice.4), channel_id=1, source_target_pairs={{0,32},{32,64},{64,96},{96,128},{128,160},{160,192},{192,224},{224... | collective-permute-start | bytes 196616 | tf_op jit(solution)/shard_map/ppermute | solution.py:48
  71.9 5.0 %collective-permute-start.2 = (bf16[2,8,2048]{2,1,0:T(8,128)(2,1)S(1)}, bf16[2,8,2048]{2,1,0:T(8,128)(2,1)S(1)}, u32[]{:S(2)}, u32[]{:S(2)}) collective-permute-start(bf16[2,8,2048]{2,1,0:T(8,128)(2,1)S(1)} %collective-permute-done.1), channel_id=1, source_target_pairs={{0,1},{1,0},{2,3},{3,2},{4,5},{5,4},{6,7},{7,6},{8,9},{9,8},{10,11... | collective-permute-start | bytes 196616 | tf_op jit(solution)/shard_map/ppermute | solution.py:49
  79.7 1.9 %copy-start.1 = (s32[8]{0:T(128)S(1)}, s32[8]{0:T(128)}, u32[]{:S(2)}) copy-start(s32[8]{0:T(128)} %param.5) | copy-start | bytes 100
  79.7 18.0 %collective-permute-start.12 = (f32[288,384]{1,0:T(8,128)S(1)}, f32[288,384]{1,0:T(8,128)S(1)}, u32[]{:S(2)}, u32[]{:S(2)}) collective-permute-start(f32[288,384]{1,0:T(8,128)S(1)} %get-tuple-element.13.refs_8_.last_ref), channel_id=1, source_target_pairs={{0,1},{1,2},{2,3},{3,4},{4,5},{5,6},{6,7},{7,8},{8,9},{9,10},{10,1... | collective-permute-start | bytes 1327112 | tf_op jit(solution)/shard_map/ppermute | solution.py:266
  81.8 16.0 %collective-permute-start.13 = (f32[288,128]{1,0:T(8,128)S(1)}, f32[288,128]{1,0:T(8,128)S(1)}, u32[]{:S(2)}, u32[]{:S(2)}) collective-permute-start(f32[288,128]{1,0:T(8,128)S(1)} %get-tuple-element.14.refs_9_.lead_ref), channel_id=1, source_target_pairs={{1,0},{2,1},{3,2},{4,3},{5,4},{6,5},{7,6},{8,7},{9,8},{10,9},{11,1... | collective-permute-start | bytes 442376 | tf_op jit(solution)/shard_map/ppermute | solution.py:267

commit v4 on v3

--- a/solution.py
+++ b/solution.py
@@ -43,10 +43,12 @@
     near = lax.all_to_all(copies, "ma", 0, 0, axis_index_groups=groups)
     own = [frames] + [lax.ppermute(frames, "pb", across(dy, dx, 0)) for dy, dx in SHIFTS]
     own = [jnp.stack(own[:4]), jnp.stack(own[4:])]
+    near_top = lax.ppermute(near[14:], "pb", [(i, i + 1) for i in range(15)])
+    parts = [lax.ppermute(near[8:], "ma", sides), lax.ppermute(near[:8], "ma", sides)]
+    far_top = lax.ppermute(parts[0][6:], "pb", [(i, i + 1) for i in range(15)])
+    own[1], parts[0], near_top = lax.optimization_barrier((own[1], parts[0], near_top))
+    far = jnp.concatenate(parts[::-1])
     other = [lax.ppermute(part, "pb", across(0, 0, 1)) for part in own]
-    far = lax.ppermute(near, "ma", sides)
-    near_top = lax.ppermute(near[14:], "pb", [(i, i + 1) for i in range(15)])
-    far_top = lax.ppermute(near_top, "ma", sides)
     rows = [v.reshape(-1, depth) for v in (near, far, near_top, far_top)]
     return rows, own + other
 
@@ -224,7 +226,7 @@
             step(t, begin, drop, emit)
             return carry
 
-        lax.fori_loop(first, last, body, 0)
+        lax.fori_loop(first, last, body, 0, unroll=2)
 
     phase(0, SEQ - 1, 0, False, False)
     step(SEQ - 1, 0, False, True)

time: 116 us -> 111 us (0.957)
  the two profiles are of different devices: /device:TPU:37 before, /device:TPU:57 now
where the time goes in v4:
time: 111 us; the launch traced here: 110 us
  starting transfers between devices  70.9 us (64%)
  Pallas kernels  22.7 us (20%)
  waiting for transfers between devices  11.2 us (10%)
  other arithmetic  2.53 us (2%)
  local copies, waits for them, and re-layouts  2.44 us (2%)
    ppermute x7, starting transfers between devices, gather(): lax.ppermute(frames, 'pb', across(dy, dx, 0))  26.8 us
    pallas_call x1, Pallas kernels, best_of(): pl.pallas_call(best_kernel, name='best', out_shape=jax.ShapeDtypeStruct((...  15.6 us
    all_to_all x1, starting transfers between devices, gather(): near = lax.all_to_all(copies, 'ma', 0, 0, axis_index_groups=groups)  14.8 us
    ppermute x2, starting transfers between devices, gather(): other = [lax.ppermute(part, 'pb', across(0, 0, 1)) for part in own]  9.94 us
    ppermute x1, waiting for transfers between devices, local(): right = lax.ppermute(lead, 'ma', [(i + 1, i) for i in range(31)])  7.45 us
    pallas_call x1, Pallas kernels, local(): pl.pallas_call(middle_kernel, name='middle', out_shape=(block(LANES), jax...  4.31 us
    ppermute x1, starting transfers between devices, gather(): near_top = lax.ppermute(near[14:], 'pb', [(i, i + 1) for i in range(15)])  4.26 us
    ppermute x1, waiting for transfers between devices, gather(): lax.ppermute(near[:8], 'ma', sides)  3.69 us
  transfers between devices with their start and end apart: 16, of which 2 were waited for; matrix products, arithmetic and copies ran while one was open for 2% of the time, Pallas kernels for 4%

profile of v4, /device:TPU:57, one launch (start us, length us, event | category | flops | bytes accessed | tf_op | source)
XLA Modules:
  0.0 110.2 jit_solution(9762416614801418098)
XLA Ops:
  0.0 1.6 %broadcast_in_dim.15 = bf16[16,8,2048]{2,1,0:T(8,128)(2,1)} broadcast(bf16[8,2048]{1,0:T(8,128)(2,1)} %bitcast.46), dimensions={1,2} | broadcast | bytes 557056 | tf_op jit(solution)/shard_map/broadcast_in_dim | solution.py:41
  1.6 14.8 %all-to-all-start = ((bf16[16,8,2048]{2,1,0:T(8,128)(2,1)}), bf16[16,8,2048]{2,1,0:T(8,128)(2,1)S(1)}, u32[]{:S(2)}, u32[]{:S(2)}) async-start(bf16[16,8,2048]{2,1,0:T(8,128)(2,1)} %broadcast_in_dim.15), calls=%async_computation | async-start | bytes 1048576 | tf_op jit(solution)/shard_map/all_to_all | solution.py:43
  16.4 0.0 copy-done
  16.4 4.7 %collective-permute-start.10 = (bf16[1024,128]{1,0:T(8,128)(2,1)S(1)}, bf16[1024,128]{1,0:T(8,128)(2,1)S(1)}, u32[]{:S(2)}, u32[]{:S(2)}) collective-permute-start(bf16[1024,128]{1,0:T(8,128)(2,1)S(1)} %copy-done), channel_id=1, source_target_pairs={{0,64},{32,96},{64,0},{96,32},{128,192},{160,224},{192,128},{224,1... | collective-permute-start | bytes 786440 | tf_op jit(solution)/shard_map/ppermute | solution.py:44
  21.1 2.4 %collective-permute-start.9 = (bf16[1024,128]{1,0:T(8,128)(2,1)S(1)}, bf16[1024,128]{1,0:T(8,128)(2,1)S(1)}, u32[]{:S(2)}, u32[]{:S(2)}) collective-permute-start(bf16[1024,128]{1,0:T(8,128)(2,1)S(1)} %copy-done), channel_id=1, source_target_pairs={{0,384},{32,416},{64,448},{96,480},{128,0},{160,32},{192,64},{224,... | collective-permute-start | bytes 786440 | tf_op jit(solution)/shard_map/ppermute | solution.py:44
  23.4 4.1 %collective-permute-start.8 = (bf16[1024,128]{1,0:T(8,128)(2,1)S(1)}, bf16[1024,128]{1,0:T(8,128)(2,1)S(1)}, u32[]{:S(2)}, u32[]{:S(2)}) collective-permute-start(bf16[1024,128]{1,0:T(8,128)(2,1)S(1)} %copy-done), channel_id=1, source_target_pairs={{0,128},{32,160},{64,192},{96,224},{128,256},{160,288},{192,320},{... | collective-permute-start | bytes 786440 | tf_op jit(solution)/shard_map/ppermute | solution.py:44
  27.6 1.9 %collective-permute-start.4 = (bf16[1024,128]{1,0:T(8,128)(2,1)S(1)}, bf16[1024,128]{1,0:T(8,128)(2,1)S(1)}, u32[]{:S(2)}, u32[]{:S(2)}) collective-permute-start(bf16[1024,128]{1,0:T(8,128)(2,1)S(1)} %copy-done), channel_id=1, source_target_pairs={{0,320},{32,352},{64,256},{96,288},{128,448},{160,480},{192,384},{... | collective-permute-start | bytes 786440 | tf_op jit(solution)/shard_map/ppermute | solution.py:44
  29.5 4.8 %collective-permute-start.3 = (bf16[1024,128]{1,0:T(8,128)(2,1)S(1)}, bf16[1024,128]{1,0:T(8,128)(2,1)S(1)}, u32[]{:S(2)}, u32[]{:S(2)}) collective-permute-start(bf16[1024,128]{1,0:T(8,128)(2,1)S(1)} %copy-done), channel_id=1, source_target_pairs={{0,256},{32,288},{64,320},{96,352},{128,384},{160,416},{192,448},{... | collective-permute-start | bytes 786440 | tf_op jit(solution)/shard_map/ppermute | solution.py:44
  34.3 0.0 collective-permute-done.10
  34.3 3.6 %collective-permute-start.2 = (bf16[1024,128]{1,0:T(8,128)(2,1)S(1)}, bf16[1024,128]{1,0:T(8,128)(2,1)S(1)}, u32[]{:S(2)}, u32[]{:S(2)}) collective-permute-start(bf16[1024,128]{1,0:T(8,128)(2,1)S(1)} %copy-done), channel_id=1, source_target_pairs={{0,448},{32,480},{64,384},{96,416},{128,64},{160,96},{192,0},{224,... | collective-permute-start | bytes 786440 | tf_op jit(solution)/shard_map/ppermute | solution.py:44
  37.9 0.0 collective-permute-done.9
  38.0 0.0 copy-start.3
  38.0 5.3 %collective-permute-start.1 = (bf16[1024,128]{1,0:T(8,128)(2,1)S(1)}, bf16[1024,128]{1,0:T(8,128)(2,1)}, u32[]{:S(2)}, u32[]{:S(2)}) collective-permute-start(bf16[1024,128]{1,0:T(8,128)(2,1)S(1)} %copy-done), channel_id=1, source_target_pairs={{0,192},{32,224},{64,128},{96,160},{128,320},{160,352},{192,256},{... | collective-permute-start | bytes 786440 | tf_op jit(solution)/shard_map/ppermute | solution.py:44
  43.2 0.0 all-to-all-done
  43.3 0.0 copy-done.3
  43.3 0.0 collective-permute-done.8
  43.3 0.0 copy-start.4
  43.3 3.1 %collective-permute-start.5 = (bf16[8,8,2048]{2,1,0:T(8,128)(2,1)S(1)}, bf16[8,8,2048]{2,1,0:T(8,128)(2,1)S(1)}, u32[]{:S(2)}, u32[]{:S(2)}) collective-permute-start(bf16[8,8,2048]{2,1,0:T(8,128)(2,1)S(1)} %get-tuple-element.24), channel_id=1, source_target_pairs={{0,1},{1,0},{2,3},{3,2},{4,5},{5,4},{6,7},{7,6},{8,9},{9,8},{10,11... | collective-permute-start | bytes 786440 | tf_op jit(solution)/shard_map/ppermute | solution.py:47
  46.5 1.2 %pad_maximum_fusion.1.refs_4_ = bf16[4,1024,128]{2,1,0:T(8,128)(2,1)S(1)} fusion(bf16[1,1024,128]{2,1,0:T(8,128)(2,1)S(1)} %bitcast.43, bf16[1,1024,128]{2,1,0:T(8,128)(2,1)} %bitcast.44, bf16[1,1024,128]{2,1,0:T(8,128)(2,1)} %bitcast.45, bf16[1,1024,128]{2,1,0:T(8,128)(2,1)S(1)} %bitcast.39), kind=kLoop, calls=%fused_computation.1 | loop fusion | flops 1572864 | bytes 2097152 | tf_op jit(solution)/shard_map/stack | solution.py:45
  47.7 0.0 collective-permute-done.4
  47.7 5.4 %collective-permute-start.11 = (bf16[4,1024,128]{2,1,0:T(8,128)(2,1)S(1)}, bf16[4,1024,128]{2,1,0:T(8,128)(2,1)}, u32[]{:S(2)}, u32[]{:S(2)}) collective-permute-start(bf16[4,1024,128]{2,1,0:T(8,128)(2,1)S(1)} %pad_maximum_fusion.1.refs_4_), channel_id=1, source_target_pairs={{0,32},{32,0},{64,96},{96,64},{128,160},{160,128},{192,224},{224,1... | collective-permute-start | bytes 3145736 | tf_op jit(solution)/shard_map/ppermute | solution.py:51
  53.1 0.0 collective-permute-done.3
  53.1 0.0 copy-start.1
  53.1 4.3 %collective-permute-start.6 = (bf16[2,8,2048]{2,1,0:T(8,128)(2,1)S(1)}, bf16[2,8,2048]{2,1,0:T(8,128)(2,1)S(1)}, u32[]{:S(2)}, u32[]{:S(2)}) collective-permute-start(bf16[2,8,2048]{2,1,0:T(8,128)(2,1)S(1)} %slice.18), channel_id=1, source_target_pairs={{0,32},{32,64},{64,96},{96,128},{128,160},{160,192},{192,224},{224... | collective-permute-start | bytes 196616 | tf_op jit(solution)/shard_map/ppermute | solution.py:46
  57.3 0.0 collective-permute-done.2
  57.4 0.0 copy-start.2
  57.4 0.0 collective-permute-done.1
  57.4 0.7 copy-done.2
  58.1 1.2 %pad_maximum_fusion.refs_5_ = bf16[4,1024,128]{2,1,0:T(8,128)(2,1)S(1)} fusion(bf16[1,1024,128]{2,1,0:T(8,128)(2,1)S(1)} %bitcast.40, bf16[1,1024,128]{2,1,0:T(8,128)(2,1)} %bitcast.41, bf16[1,1024,128]{2,1,0:T(8,128)(2,1)} %bitcast.42, bf16[1,1024,128]{2,1,0:T(8,128)(2,1)} %bitcast.20), kind=kLoop, calls=%fused_computation | loop fusion | flops 1572864 | bytes 2097152 | tf_op jit(solution)/shard_map/stack | solution.py:45
  59.3 0.0 collective-permute-done.6
  59.3 0.0 collective-permute-done.5
  59.3 4.6 %collective-permute-start.12 = (bf16[4,1024,128]{2,1,0:T(8,128)(2,1)S(1)}, bf16[4,1024,128]{2,1,0:T(8,128)(2,1)}, u32[]{:S(2)}, u32[]{:S(2)}) collective-permute-start(bf16[4,1024,128]{2,1,0:T(8,128)(2,1)S(1)} %pad_maximum_fusion.refs_5_), channel_id=1, source_target_pairs={{0,32},{32,0},{64,96},{96,64},{128,160},{160,128},{192,224},{224,1... | collective-permute-start | bytes 3145736 | tf_op jit(solution)/shard_map/ppermute | solution.py:51
  63.9 3.0 %collective-permute-start = (bf16[8,8,2048]{2,1,0:T(8,128)(2,1)S(1)}, bf16[8,8,2048]{2,1,0:T(8,128)(2,1)S(1)}, u32[]{:S(2)}, u32[]{:S(2)}) collective-permute-start(bf16[8,8,2048]{2,1,0:T(8,128)(2,1)S(1)} %get-tuple-element.23), channel_id=1, source_target_pairs={{0,1},{1,0},{2,3},{3,2},{4,5},{5,4},{6,7},{7,6},{8,9},{9,8},{10,11... | collective-permute-start | bytes 786440 | tf_op jit(solution)/shard_map/ppermute | solution.py:47
  67.1 0.1 stack.101.at_ref
  67.2 2.8 %collective-permute-start.7 = (bf16[2,8,2048]{2,1,0:T(8,128)(2,1)S(1)}, bf16[2,8,2048]{2,1,0:T(8,128)(2,1)S(1)}, u32[]{:S(2)}, u32[]{:S(2)}) collective-permute-start(bf16[2,8,2048]{2,1,0:T(8,128)(2,1)S(1)} %slice.19), channel_id=1, source_target_pairs={{0,32},{32,64},{64,96},{96,128},{128,160},{160,192},{192,224},{224... | collective-permute-start | bytes 196616 | tf_op jit(solution)/shard_map/ppermute | solution.py:48
  70.0 3.7 %collective-permute-done = bf16[8,8,2048]{2,1,0:T(8,128)(2,1)S(1)} collective-permute-done((bf16[8,8,2048]{2,1,0:T(8,128)(2,1)S(1)}, bf16[8,8,2048]{2,1,0:T(8,128)(2,1)S(1)}, u32[]{:S(2)}, u32[]{:S(2)}) %collective-permute-start) | collective-permute-done | bytes 262176 | tf_op jit(solution)/shard_map/ppermute | solution.py:47
  73.7 0.0 collective-permute-done.11.refs_6_
  73.8 0.0 collective-permute-done.7
  73.8 0.0 collective-permute-done.12.refs_7_
  73.8 2.8 %edges.1 = (f32[288,384]{1,0:T(8,128)S(1)}, f32[288,128]{1,0:T(8,128)S(1)}) custom-call(s32[17]{0:T(128)S(1)} %stack.101.at_ref, bf16[128,2048]{1,0:T(8,128)(2,1)S(1)} %bitcast.33, bf16[128,2048]{1,0:T(8,128)(2,1)S(1)} %maximum_bitcast_fusion.refs_1_, bf16[16,2048]{1,0:T(8,128)(2,1)S(1)} %bitcast.35, bf16[16,2048]{1,0:T(8,128)(2,1)S(1)} %bitcast.37, ...), custom_call_target="tpu_custom_call" | custom-call | flops 603979776 | bytes 6291456 | tf_op jit(solution)/shard_map/edges/pallas_call | solution.py:258
  76.6 0.0 copy-start.5
  76.6 3.0 %collective-permute-start.13 = (f32[288,384]{1,0:T(8,128)S(1)}, f32[288,384]{1,0:T(8,128)S(1)}, u32[]{:S(2)}, u32[]{:S(2)}) collective-permute-start(f32[288,384]{1,0:T(8,128)S(1)} %get-tuple-element.19.refs_8_.last_ref), channel_id=1, source_target_pairs={{0,1},{1,2},{2,3},{3,4},{4,5},{5,6},{6,7},{7,8},{8,9},{9,10},{10,1... | collective-permute-start | bytes 1327112 | tf_op jit(solution)/shard_map/ppermute | solution.py:268
  79.6 0.1 pad_add_fusion.slopes_ref
  79.7 3.1 %collective-permute-start.14 = (f32[288,128]{1,0:T(8,128)S(1)}, f32[288,128]{1,0:T(8,128)S(1)}, u32[]{:S(2)}, u32[]{:S(2)}) collective-permute-start(f32[288,128]{1,0:T(8,128)S(1)} %get-tuple-element.20.refs_9_.lead_ref), channel_id=1, source_target_pairs={{1,0},{2,1},{3,2},{4,3},{5,4},{6,5},{7,6},{8,7},{9,8},{10,9},{11,1... | collective-permute-start | bytes 442376 | tf_op jit(solution)/shard_map/ppermute | solution.py:269
  82.8 4.3 %middle.1 = (f32[288,128]{1,0:T(8,128)S(1)}, f32[6,288,128]{2,1,0:T(8,128)S(1)}) custom-call(s32[17]{0:T(128)S(1)} %stack.101.at_ref, bf16[128,2048]{1,0:T(8,128)(2,1)S(1)} %bitcast.34, bf16[128,2048]{1,0:T(8,128)(2,1)S(1)} %maximum_bitcast_fusion.refs_1_, bf16[16,2048]{1,0:T(8,128)(2,1)S(1)} %bitcast.36, bf16[16,2048]{1,0:T(8,128)(2,1)S(1)} %bitcast.38, ...), custom_call_target="tpu_custom_call" | custom-call | flops 2415919104 | bytes 16777216 | tf_op jit(solution)/shard_map/middle/pallas_call | solution.py:270
  87.2 7.4 %collective-permute-done.14.right_ref = f32[288,128]{1,0:T(8,128)S(1)} collective-permute-done((f32[288,128]{1,0:T(8,128)S(1)}, f32[288,128]{1,0:T(8,128)S(1)}, u32[]{:S(2)}, u32[]{:S(2)}) %collective-permute-start.14) | collective-permute-done | bytes 147488 | tf_op jit(solution)/shard_map/ppermute | solution.py:269
  94.6 0.0 collective-permute-done.13.left_ref
  94.6 15.6 %best.1 = f32[256,1024]{1,0:T(8,128)} custom-call(s32[9]{0:T(128)S(1)} %pad_add_fusion.slopes_ref, f32[288,384]{1,0:T(8,128)S(1)} %collective-permute-done.13.left_ref, f32[288,128]{1,0:T(8,128)S(1)} %collective-permute-done.14.right_ref, f32[288,384]{1,0:T(8,128)S(1)} %get-tuple-element.19.refs_8_.last_ref, ...), custom_call_target="tpu_custom_call" | custom-call | flops 62914560 | bytes 4194304 | tf_op jit(solution)/shard_map/best/pallas_call | solution.py:286
  (8 shorter events, 0.1 us)
Async XLA Ops:
  1.6 14.8 %copy-start = (bf16[1024,128]{1,0:T(8,128)(2,1)S(1)}, bf16[1024,128]{1,0:T(8,128)(2,1)}, u32[]{:S(2)}) copy-start(bf16[1024,128]{1,0:T(8,128)(2,1)} %param.4) | copy-start | bytes 786436
  1.6 41.6 %all-to-all-start = ((bf16[16,8,2048]{2,1,0:T(8,128)(2,1)}), bf16[16,8,2048]{2,1,0:T(8,128)(2,1)S(1)}, u32[]{:S(2)}, u32[]{:S(2)}) async-start(bf16[16,8,2048]{2,1,0:T(8,128)(2,1)} %broadcast_in_dim.15), calls=%async_computation | async-start | bytes 1048576 | tf_op jit(solution)/shard_map/all_to_all | solution.py:43
  16.4 17.9 %collective-permute-start.10 = (bf16[1024,128]{1,0:T(8,128)(2,1)S(1)}, bf16[1024,128]{1,0:T(8,128)(2,1)S(1)}, u32[]{:S(2)}, u32[]{:S(2)}) collective-permute-start(bf16[1024,128]{1,0:T(8,128)(2,1)S(1)} %copy-done), channel_id=1, source_target_pairs={{0,64},{32,96},{64,0},{96,32},{128,192},{160,224},{192,128},{224,1... | collective-permute-start | bytes 786440 | tf_op jit(solution)/shard_map/ppermute | solution.py:44
  21.1 16.9 %collective-permute-start.9 = (bf16[1024,128]{1,0:T(8,128)(2,1)S(1)}, bf16[1024,128]{1,0:T(8,128)(2,1)S(1)}, u32[]{:S(2)}, u32[]{:S(2)}) collective-permute-start(bf16[1024,128]{1,0:T(8,128)(2,1)S(1)} %copy-done), channel_id=1, source_target_pairs={{0,384},{32,416},{64,448},{96,480},{128,0},{160,32},{192,64},{224,... | collective-permute-start | bytes 786440 | tf_op jit(solution)/shard_map/ppermute | solution.py:44
  23.4 19.9 %collective-permute-start.8 = (bf16[1024,128]{1,0:T(8,128)(2,1)S(1)}, bf16[1024,128]{1,0:T(8,128)(2,1)S(1)}, u32[]{:S(2)}, u32[]{:S(2)}) collective-permute-start(bf16[1024,128]{1,0:T(8,128)(2,1)S(1)} %copy-done), channel_id=1, source_target_pairs={{0,128},{32,160},{64,192},{96,224},{128,256},{160,288},{192,320},{... | collective-permute-start | bytes 786440 | tf_op jit(solution)/shard_map/ppermute | solution.py:44
  27.6 20.1 %collective-permute-start.4 = (bf16[1024,128]{1,0:T(8,128)(2,1)S(1)}, bf16[1024,128]{1,0:T(8,128)(2,1)S(1)}, u32[]{:S(2)}, u32[]{:S(2)}) collective-permute-start(bf16[1024,128]{1,0:T(8,128)(2,1)S(1)} %copy-done), channel_id=1, source_target_pairs={{0,320},{32,352},{64,256},{96,288},{128,448},{160,480},{192,384},{... | collective-permute-start | bytes 786440 | tf_op jit(solution)/shard_map/ppermute | solution.py:44
  29.5 23.6 %collective-permute-start.3 = (bf16[1024,128]{1,0:T(8,128)(2,1)S(1)}, bf16[1024,128]{1,0:T(8,128)(2,1)S(1)}, u32[]{:S(2)}, u32[]{:S(2)}) collective-permute-start(bf16[1024,128]{1,0:T(8,128)(2,1)S(1)} %copy-done), channel_id=1, source_target_pairs={{0,256},{32,288},{64,320},{96,352},{128,384},{160,416},{192,448},{... | collective-permute-start | bytes 786440 | tf_op jit(solution)/shard_map/ppermute | solution.py:44
  34.3 23.0 %collective-permute-start.2 = (bf16[1024,128]{1,0:T(8,128)(2,1)S(1)}, bf16[1024,128]{1,0:T(8,128)(2,1)S(1)}, u32[]{:S(2)}, u32[]{:S(2)}) collective-permute-start(bf16[1024,128]{1,0:T(8,128)(2,1)S(1)} %copy-done), channel_id=1, source_target_pairs={{0,448},{32,480},{64,384},{96,416},{128,64},{160,96},{192,0},{224,... | collective-permute-start | bytes 786440 | tf_op jit(solution)/shard_map/ppermute | solution.py:44
  38.0 5.4 %copy-start.3 = (bf16[1024,128]{1,0:T(8,128)(2,1)}, bf16[1024,128]{1,0:T(8,128)(2,1)S(1)}, u32[]{:S(2)}) copy-start(bf16[1024,128]{1,0:T(8,128)(2,1)S(1)} %collective-permute-done.9) | copy-start | bytes 786436
  38.0 19.4 %collective-permute-start.1 = (bf16[1024,128]{1,0:T(8,128)(2,1)S(1)}, bf16[1024,128]{1,0:T(8,128)(2,1)}, u32[]{:S(2)}, u32[]{:S(2)}) collective-permute-start(bf16[1024,128]{1,0:T(8,128)(2,1)S(1)} %copy-done), channel_id=1, source_target_pairs={{0,192},{32,224},{64,128},{96,160},{128,320},{160,352},{192,256},{... | collective-permute-start | bytes 786440 | tf_op jit(solution)/shard_map/ppermute | solution.py:44
  43.3 3.1 %copy-start.4 = (bf16[1024,128]{1,0:T(8,128)(2,1)}, bf16[1024,128]{1,0:T(8,128)(2,1)S(1)}, u32[]{:S(2)}) copy-start(bf16[1024,128]{1,0:T(8,128)(2,1)S(1)} %collective-permute-done.8) | copy-start | bytes 786436
  43.3 16.0 %collective-permute-start.5 = (bf16[8,8,2048]{2,1,0:T(8,128)(2,1)S(1)}, bf16[8,8,2048]{2,1,0:T(8,128)(2,1)S(1)}, u32[]{:S(2)}, u32[]{:S(2)}) collective-permute-start(bf16[8,8,2048]{2,1,0:T(8,128)(2,1)S(1)} %get-tuple-element.24), channel_id=1, source_target_pairs={{0,1},{1,0},{2,3},{3,2},{4,5},{5,4},{6,7},{7,6},{8,9},{9,8},{10,11... | collective-permute-start | bytes 786440 | tf_op jit(solution)/shard_map/ppermute | solution.py:47
  47.7 26.1 %collective-permute-start.11 = (bf16[4,1024,128]{2,1,0:T(8,128)(2,1)S(1)}, bf16[4,1024,128]{2,1,0:T(8,128)(2,1)}, u32[]{:S(2)}, u32[]{:S(2)}) collective-permute-start(bf16[4,1024,128]{2,1,0:T(8,128)(2,1)S(1)} %pad_maximum_fusion.1.refs_4_), channel_id=1, source_target_pairs={{0,32},{32,0},{64,96},{96,64},{128,160},{160,128},{192,224},{224,1... | collective-permute-start | bytes 3145736 | tf_op jit(solution)/shard_map/ppermute | solution.py:51
  53.1 4.3 %copy-start.1 = (bf16[1024,128]{1,0:T(8,128)(2,1)}, bf16[1024,128]{1,0:T(8,128)(2,1)S(1)}, u32[]{:S(2)}) copy-start(bf16[1024,128]{1,0:T(8,128)(2,1)S(1)} %collective-permute-done.3) | copy-start | bytes 786436
  53.1 6.2 %collective-permute-start.6 = (bf16[2,8,2048]{2,1,0:T(8,128)(2,1)S(1)}, bf16[2,8,2048]{2,1,0:T(8,128)(2,1)S(1)}, u32[]{:S(2)}, u32[]{:S(2)}) collective-permute-start(bf16[2,8,2048]{2,1,0:T(8,128)(2,1)S(1)} %slice.18), channel_id=1, source_target_pairs={{0,32},{32,64},{64,96},{96,128},{128,160},{160,192},{192,224},{224... | collective-permute-start | bytes 196616 | tf_op jit(solution)/shard_map/ppermute | solution.py:46
  57.4 0.7 copy-start.2
  59.3 14.5 %collective-permute-start.12 = (bf16[4,1024,128]{2,1,0:T(8,128)(2,1)S(1)}, bf16[4,1024,128]{2,1,0:T(8,128)(2,1)}, u32[]{:S(2)}, u32[]{:S(2)}) collective-permute-start(bf16[4,1024,128]{2,1,0:T(8,128)(2,1)S(1)} %pad_maximum_fusion.refs_5_), channel_id=1, source_target_pairs={{0,32},{32,0},{64,96},{96,64},{128,160},{160,128},{192,224},{224,1... | collective-permute-start | bytes 3145736 | tf_op jit(solution)/shard_map/ppermute | solution.py:51
  63.9 9.8 %collective-permute-start = (bf16[8,8,2048]{2,1,0:T(8,128)(2,1)S(1)}, bf16[8,8,2048]{2,1,0:T(8,128)(2,1)S(1)}, u32[]{:S(2)}, u32[]{:S(2)}) collective-permute-start(bf16[8,8,2048]{2,1,0:T(8,128)(2,1)S(1)} %get-tuple-element.23), channel_id=1, source_target_pairs={{0,1},{1,0},{2,3},{3,2},{4,5},{5,4},{6,7},{7,6},{8,9},{9,8},{10,11... | collective-permute-start | bytes 786440 | tf_op jit(solution)/shard_map/ppermute | solution.py:47
  67.2 6.6 %collective-permute-start.7 = (bf16[2,8,2048]{2,1,0:T(8,128)(2,1)S(1)}, bf16[2,8,2048]{2,1,0:T(8,128)(2,1)S(1)}, u32[]{:S(2)}, u32[]{:S(2)}) collective-permute-start(bf16[2,8,2048]{2,1,0:T(8,128)(2,1)S(1)} %slice.19), channel_id=1, source_target_pairs={{0,32},{32,64},{64,96},{96,128},{128,160},{160,192},{192,224},{224... | collective-permute-start | bytes 196616 | tf_op jit(solution)/shard_map/ppermute | solution.py:48
  76.6 3.1 %copy-start.5 = (s32[8]{0:T(128)S(1)}, s32[8]{0:T(128)}, u32[]{:S(2)}) copy-start(s32[8]{0:T(128)} %param.5) | copy-start | bytes 100
  76.6 18.0 %collective-permute-start.13 = (f32[288,384]{1,0:T(8,128)S(1)}, f32[288,384]{1,0:T(8,128)S(1)}, u32[]{:S(2)}, u32[]{:S(2)}) collective-permute-start(f32[288,384]{1,0:T(8,128)S(1)} %get-tuple-element.19.refs_8_.last_ref), channel_id=1, source_target_pairs={{0,1},{1,2},{2,3},{3,4},{4,5},{5,6},{6,7},{7,8},{8,9},{9,10},{10,1... | collective-permute-start | bytes 1327112 | tf_op jit(solution)/shard_map/ppermute | solution.py:268
  79.7 14.9 %collective-permute-start.14 = (f32[288,128]{1,0:T(8,128)S(1)}, f32[288,128]{1,0:T(8,128)S(1)}, u32[]{:S(2)}, u32[]{:S(2)}) collective-permute-start(f32[288,128]{1,0:T(8,128)S(1)} %get-tuple-element.20.refs_9_.lead_ref), channel_id=1, source_target_pairs={{1,0},{2,1},{3,2},{4,3},{5,4},{6,5},{7,6},{8,7},{9,8},{10,9},{11,1... | collective-permute-start | bytes 442376 | tf_op jit(solution)/shard_map/ppermute | solution.py:269

commit v5 on v4

--- a/solution.py
+++ b/solution.py
@@ -15,10 +15,12 @@
 LANES = 128
 ROWS = TOP + 256
 COLUMNS = 1024
+THIRD = ROWS // 3
+PACK = 40
 HALO = LEFT // LANES
 TILES = HALO + COLUMNS // LANES
 FIRST, LAST = HALO + 1, TILES - 1
-SHIFTS = ((1, 0), (3, 0), (0, 1), (1, 1), (3, 1), (2, 0), (2, 1))
+SHIFTS = ((1, 0), (1, 1), (3, 1), (3, 0), (2, 0), (2, 1), (0, 1))
 
 
 def tile(c):
@@ -83,8 +85,23 @@
         out_ref[pl.ds(start, 8), cols] = value[8 * r : 8 * r + 8]
 
 
+def packed(ref, cols, first):
+    lane = lax.broadcasted_iota(jnp.int32, (THIRD, LANES), 1)
+    parts = [
+        pltpu.roll(ref[g * THIRD : (g + 1) * THIRD, cols], (PACK * g - first) % LANES, 1)
+        for g in range(3)
+    ]
+    return jnp.where(lane < PACK, parts[0], jnp.where(lane < 2 * PACK, parts[1], parts[2]))
+
+
+def unpacked(value, first):
+    parts = [pltpu.roll(value, (first - PACK * g) % LANES, 1) for g in range(3)]
+    return jnp.concatenate(parts)
+
+
 def edge_kernel(at_ref, *refs):
-    row_refs, map_refs, (last_ref, lead_ref, rows_ref) = refs[:4], refs[4:8], refs[8:]
+    row_refs, map_refs = refs[:4], refs[4:8]
+    last_ref, lead_ref, left_ref, right_ref, rows_ref = refs[8:]
     fill_rows(row_refs, rows_ref)
     side = at_ref[16]
     begin = COLUMNS - LEFT
@@ -92,6 +109,10 @@
         value = products(at_ref, rows_ref, map_refs, begin + at, width)
         place_rows(side, last_ref, slice(at, at + width), value)
     place_rows(side, lead_ref, slice(0, LANES), products(at_ref, rows_ref, map_refs, 0, LANES))
+    left_ref[:ROWS] = last_ref[:, tile(1)]
+    left_ref[ROWS : 2 * ROWS] = last_ref[:, tile(2)]
+    left_ref[2 * ROWS :] = packed(last_ref, tile(0), LANES - PACK)
+    right_ref[...] = packed(lead_ref, tile(0), 0)
 
 
 def split_tile(split_ref, slot, value):
@@ -153,7 +174,8 @@
     first_map = slopes_ref[8] == 0
     empty = jnp.zeros((ROWS, LANES), jnp.bfloat16)
     band = band_of()
-    edge = [left_ref[:, tile(c)] for c in range(HALO)] + [lead_ref[...], next_ref[...]]
+    farthest = unpacked(left_ref[2 * ROWS :], LANES - PACK)
+    edge = [farthest, left_ref[:ROWS], left_ref[ROWS : 2 * ROWS], lead_ref[...], next_ref[...]]
     for part in range(6):
         split_ref[part, :, tile(0)] = empty
     for c, value in enumerate(edge):
@@ -164,7 +186,7 @@
             if c + half < HALO:
                 value = jnp.where(first_map, 0.0, value)
             x_ref[c + half] = value
-    edge = [last_ref[:, tile(1)], last_ref[:, tile(2)], right_ref[...]]
+    edge = [last_ref[:, tile(1)], last_ref[:, tile(2)], unpacked(right_ref[...], 0)]
     for part in range(6):
         split_ref[part, :, tile(3)] = empty
     for c, value in enumerate(edge):
@@ -255,18 +277,19 @@
     block = lambda width: jax.ShapeDtypeStruct((ROWS, width), jnp.float32)
     limit = pltpu.CompilerParams(vmem_limit_bytes=40 << 20)
     rows_scratch = pltpu.VMEM((ROWS, 2048), jnp.bfloat16)
-    last, lead = pl.pallas_call(
+    lines = lambda count: jax.ShapeDtypeStruct((count, LANES), jnp.float32)
+    last, lead, left, right = pl.pallas_call(
         edge_kernel,
         name="edges",
-        out_shape=(block(LEFT), block(LANES)),
+        out_shape=(block(LEFT), block(LANES), lines(2 * ROWS + THIRD), lines(THIRD)),
         in_specs=[SMEM] + [VMEM] * 8,
-        out_specs=(VMEM,) * 2,
+        out_specs=(VMEM,) * 4,
         scratch_shapes=[rows_scratch],
         compiler_params=limit,
         cost_estimate=pl.CostEstimate(flops=2 * ROWS * 512 * 2048, bytes_accessed=6 << 20, transcendentals=0),
     )(at, *rows, *frames)
-    left = lax.ppermute(last, "ma", [(i, i + 1) for i in range(31)])
-    right = lax.ppermute(lead, "ma", [(i + 1, i) for i in range(31)])
+    left = lax.ppermute(left, "ma", [(i, i + 1) for i in range(31)])
+    right = lax.ppermute(right, "ma", [(i + 1, i) for i in range(31)])
     after, inner = pl.pallas_call(
         middle_kernel,
         name="middle",

time: 111 us -> 116 us (1.045)
  the two profiles are of different devices: /device:TPU:57 before, /device:TPU:106 now
where the time goes in v5:
time: 116 us; the launch traced here: 115 us
  starting transfers between devices  62.9 us (54%)
  waiting for transfers between devices  23.6 us (20%)
  Pallas kernels  22.7 us (20%)
  other arithmetic  2.61 us (2%)
  local copies, waits for them, and re-layouts  2.54 us (2%)
    ppermute x7, starting transfers between devices, gather(): lax.ppermute(frames, 'pb', across(dy, dx, 0))  26.3 us
    pallas_call x1, Pallas kernels, best_of(): pl.pallas_call(best_kernel, name='best', out_shape=jax.ShapeDtypeStruct((...  15.5 us
    all_to_all x1, starting transfers between devices, gather(): near = lax.all_to_all(copies, 'ma', 0, 0, axis_index_groups=groups)  14.4 us
    ppermute x7, waiting for transfers between devices, gather(): lax.ppermute(frames, 'pb', across(dy, dx, 0))  8.8 us
    ppermute x1, starting transfers between devices, local(): left = lax.ppermute(left, 'ma', [(i, i + 1) for i in range(31)])  5.45 us
    ppermute x1, waiting for transfers between devices, gather(): lax.ppermute(near[:8], 'ma', sides)  5.25 us
    pallas_call x1, Pallas kernels, local(): pl.pallas_call(middle_kernel, name='middle', out_shape=(block(LANES), jax...  4.32 us
    ppermute x2, starting transfers between devices, gather(): other = [lax.ppermute(part, 'pb', across(0, 0, 1)) for part in own]  3.83 us
  transfers between devices with their start and end apart: 16, of which 6 were waited for; matrix products, arithmetic and copies ran while one was open for 2% of the time, Pallas kernels for 4%

profile of v5, /device:TPU:106, one launch (start us, length us, event | category | flops | bytes accessed | tf_op | source)
XLA Modules:
  0.0 114.8 jit_solution(12351634118441466584)
XLA Ops:
  0.0 1.6 %broadcast_in_dim.15 = bf16[16,8,2048]{2,1,0:T(8,128)(2,1)} broadcast(bf16[8,2048]{1,0:T(8,128)(2,1)} %bitcast.47), dimensions={1,2} | broadcast | bytes 557056 | tf_op jit(solution)/shard_map/broadcast_in_dim | solution.py:43
  1.6 14.4 %all-to-all-start = ((bf16[16,8,2048]{2,1,0:T(8,128)(2,1)}), bf16[16,8,2048]{2,1,0:T(8,128)(2,1)S(1)}, u32[]{:S(2)}, u32[]{:S(2)}) async-start(bf16[16,8,2048]{2,1,0:T(8,128)(2,1)} %broadcast_in_dim.15), calls=%async_computation | async-start | bytes 1048576 | tf_op jit(solution)/shard_map/all_to_all | solution.py:45
  16.0 0.0 copy-done
  16.0 3.9 %collective-permute-start.10 = (bf16[1024,128]{1,0:T(8,128)(2,1)S(1)}, bf16[1024,128]{1,0:T(8,128)(2,1)S(1)}, u32[]{:S(2)}, u32[]{:S(2)}) collective-permute-start(bf16[1024,128]{1,0:T(8,128)(2,1)S(1)} %copy-done), channel_id=1, source_target_pairs={{0,448},{32,480},{64,384},{96,416},{128,64},{160,96},{192,0},{224,... | collective-permute-start | bytes 786440 | tf_op jit(solution)/shard_map/ppermute | solution.py:46
  20.0 4.3 %collective-permute-start.9 = (bf16[1024,128]{1,0:T(8,128)(2,1)S(1)}, bf16[1024,128]{1,0:T(8,128)(2,1)S(1)}, u32[]{:S(2)}, u32[]{:S(2)}) collective-permute-start(bf16[1024,128]{1,0:T(8,128)(2,1)S(1)} %copy-done), channel_id=1, source_target_pairs={{0,192},{32,224},{64,128},{96,160},{128,320},{160,352},{192,256},{... | collective-permute-start | bytes 786440 | tf_op jit(solution)/shard_map/ppermute | solution.py:46
  24.3 4.0 %collective-permute-start.4 = (bf16[1024,128]{1,0:T(8,128)(2,1)S(1)}, bf16[1024,128]{1,0:T(8,128)(2,1)S(1)}, u32[]{:S(2)}, u32[]{:S(2)}) collective-permute-start(bf16[1024,128]{1,0:T(8,128)(2,1)S(1)} %copy-done), channel_id=1, source_target_pairs={{0,64},{32,96},{64,0},{96,32},{128,192},{160,224},{192,128},{224,1... | collective-permute-start | bytes 786440 | tf_op jit(solution)/shard_map/ppermute | solution.py:46
  28.3 6.3 %collective-permute-start.3 = (bf16[1024,128]{1,0:T(8,128)(2,1)S(1)}, bf16[1024,128]{1,0:T(8,128)(2,1)S(1)}, u32[]{:S(2)}, u32[]{:S(2)}) collective-permute-start(bf16[1024,128]{1,0:T(8,128)(2,1)S(1)} %copy-done), channel_id=1, source_target_pairs={{0,320},{32,352},{64,256},{96,288},{128,448},{160,480},{192,384},{... | collective-permute-start | bytes 786440 | tf_op jit(solution)/shard_map/ppermute | solution.py:46
  34.6 1.9 %collective-permute-start.2 = (bf16[1024,128]{1,0:T(8,128)(2,1)S(1)}, bf16[1024,128]{1,0:T(8,128)(2,1)S(1)}, u32[]{:S(2)}, u32[]{:S(2)}) collective-permute-start(bf16[1024,128]{1,0:T(8,128)(2,1)S(1)} %copy-done), channel_id=1, source_target_pairs={{0,256},{32,288},{64,320},{96,352},{128,384},{160,416},{192,448},{... | collective-permute-start | bytes 786440 | tf_op jit(solution)/shard_map/ppermute | solution.py:46
  36.5 0.0 collective-permute-done.10
  36.6 0.0 copy-start.4
  36.6 2.5 %collective-permute-start.1 = (bf16[1024,128]{1,0:T(8,128)(2,1)S(1)}, bf16[1024,128]{1,0:T(8,128)(2,1)S(1)}, u32[]{:S(2)}, u32[]{:S(2)}) collective-permute-start(bf16[1024,128]{1,0:T(8,128)(2,1)S(1)} %copy-done), channel_id=1, source_target_pairs={{0,384},{32,416},{64,448},{96,480},{128,0},{160,32},{192,64},{224,... | collective-permute-start | bytes 786440 | tf_op jit(solution)/shard_map/ppermute | solution.py:46
  39.1 0.0 collective-permute-done.9
  39.1 3.3 %collective-permute-start.8 = (bf16[1024,128]{1,0:T(8,128)(2,1)S(1)}, bf16[1024,128]{1,0:T(8,128)(2,1)S(1)}, u32[]{:S(2)}, u32[]{:S(2)}) collective-permute-start(bf16[1024,128]{1,0:T(8,128)(2,1)S(1)} %copy-done), channel_id=1, source_target_pairs={{0,128},{32,160},{64,192},{96,224},{128,256},{160,288},{192,320},{... | collective-permute-start | bytes 786440 | tf_op jit(solution)/shard_map/ppermute | solution.py:46
  42.4 2.0 %all-to-all-done = bf16[16,8,2048]{2,1,0:T(8,128)(2,1)S(1)} async-done(((bf16[16,8,2048]{2,1,0:T(8,128)(2,1)}), bf16[16,8,2048]{2,1,0:T(8,128)(2,1)S(1)}, u32[]{:S(2)}, u32[]{:S(2)}) %all-to-all-start) | async-done | bytes 524320 | tf_op jit(solution)/shard_map/all_to_all | solution.py:45
  44.5 8.8 %collective-permute-done.8 = bf16[1024,128]{1,0:T(8,128)(2,1)S(1)} collective-permute-done((bf16[1024,128]{1,0:T(8,128)(2,1)S(1)}, bf16[1024,128]{1,0:T(8,128)(2,1)S(1)}, u32[]{:S(2)}, u32[]{:S(2)}) %collective-permute-start.8) | collective-permute-done | bytes 262176 | tf_op jit(solution)/shard_map/ppermute | solution.py:46
  53.3 3.1 %collective-permute-start.5 = (bf16[8,8,2048]{2,1,0:T(8,128)(2,1)S(1)}, bf16[8,8,2048]{2,1,0:T(8,128)(2,1)S(1)}, u32[]{:S(2)}, u32[]{:S(2)}) collective-permute-start(bf16[8,8,2048]{2,1,0:T(8,128)(2,1)S(1)} %get-tuple-element.28), channel_id=1, source_target_pairs={{0,1},{1,0},{2,3},{3,2},{4,5},{5,4},{6,7},{7,6},{8,9},{9,8},{10,11... | collective-permute-start | bytes 786440 | tf_op jit(solution)/shard_map/ppermute | solution.py:49
  56.4 1.2 %pad_maximum_fusion.1.refs_4_ = bf16[4,1024,128]{2,1,0:T(8,128)(2,1)S(1)} fusion(bf16[1,1024,128]{2,1,0:T(8,128)(2,1)} %bitcast.44, bf16[1,1024,128]{2,1,0:T(8,128)(2,1)} %bitcast.45, bf16[1,1024,128]{2,1,0:T(8,128)(2,1)} %bitcast.46, bf16[1,1024,128]{2,1,0:T(8,128)(2,1)S(1)} %bitcast.39), kind=kLoop, calls=%fused_computation.1 | loop fusion | flops 1572864 | bytes 2097152 | tf_op jit(solution)/shard_map/stack | solution.py:47
  57.6 0.0 collective-permute-done.4
  57.7 1.9 %collective-permute-start.11 = (bf16[4,1024,128]{2,1,0:T(8,128)(2,1)S(1)}, bf16[4,1024,128]{2,1,0:T(8,128)(2,1)}, u32[]{:S(2)}, u32[]{:S(2)}) collective-permute-start(bf16[4,1024,128]{2,1,0:T(8,128)(2,1)S(1)} %pad_maximum_fusion.1.refs_4_), channel_id=1, source_target_pairs={{0,32},{32,0},{64,96},{96,64},{128,160},{160,128},{192,224},{224,1... | collective-permute-start | bytes 3145736 | tf_op jit(solution)/shard_map/ppermute | solution.py:53
  59.6 0.0 collective-permute-done.3
  59.6 0.0 copy-start.1
  59.6 2.4 %collective-permute-start.6 = (bf16[2,8,2048]{2,1,0:T(8,128)(2,1)S(1)}, bf16[2,8,2048]{2,1,0:T(8,128)(2,1)S(1)}, u32[]{:S(2)}, u32[]{:S(2)}) collective-permute-start(bf16[2,8,2048]{2,1,0:T(8,128)(2,1)S(1)} %slice.18), channel_id=1, source_target_pairs={{0,32},{32,64},{64,96},{96,128},{128,160},{160,192},{192,224},{224... | collective-permute-start | bytes 196616 | tf_op jit(solution)/shard_map/ppermute | solution.py:48
  62.0 0.0 collective-permute-done.2
  62.0 0.0 collective-permute-done.1
  62.1 0.0 copy-start.3
  62.1 0.0 copy-done.1
  62.1 0.7 copy-done.2
  62.7 0.1 copy-done.3
  62.8 1.2 %pad_maximum_fusion.refs_5_ = bf16[4,1024,128]{2,1,0:T(8,128)(2,1)S(1)} fusion(bf16[1,1024,128]{2,1,0:T(8,128)(2,1)S(1)} %bitcast.40, bf16[1,1024,128]{2,1,0:T(8,128)(2,1)} %bitcast.41, bf16[1,1024,128]{2,1,0:T(8,128)(2,1)} %bitcast.42, bf16[1,1024,128]{2,1,0:T(8,128)(2,1)} %bitcast.43), kind=kLoop, calls=%fused_computation | loop fusion | flops 1572864 | bytes 2097152 | tf_op jit(solution)/shard_map/stack | solution.py:47
  64.1 3.5 %collective-permute-done.6 = bf16[2,8,2048]{2,1,0:T(8,128)(2,1)S(1)} collective-permute-done((bf16[2,8,2048]{2,1,0:T(8,128)(2,1)S(1)}, bf16[2,8,2048]{2,1,0:T(8,128)(2,1)S(1)}, u32[]{:S(2)}, u32[]{:S(2)}) %collective-permute-start.6) | collective-permute-done | bytes 65568 | tf_op jit(solution)/shard_map/ppermute | solution.py:48
  67.6 0.0 collective-permute-done.5
  67.6 1.9 %collective-permute-start.12 = (bf16[4,1024,128]{2,1,0:T(8,128)(2,1)S(1)}, bf16[4,1024,128]{2,1,0:T(8,128)(2,1)}, u32[]{:S(2)}, u32[]{:S(2)}) collective-permute-start(bf16[4,1024,128]{2,1,0:T(8,128)(2,1)S(1)} %pad_maximum_fusion.refs_5_), channel_id=1, source_target_pairs={{0,32},{32,0},{64,96},{96,64},{128,160},{160,128},{192,224},{224,1... | collective-permute-start | bytes 3145736 | tf_op jit(solution)/shard_map/ppermute | solution.py:53
  69.5 3.3 %collective-permute-start = (bf16[8,8,2048]{2,1,0:T(8,128)(2,1)S(1)}, bf16[8,8,2048]{2,1,0:T(8,128)(2,1)S(1)}, u32[]{:S(2)}, u32[]{:S(2)}) collective-permute-start(bf16[8,8,2048]{2,1,0:T(8,128)(2,1)S(1)} %get-tuple-element.27), channel_id=1, source_target_pairs={{0,1},{1,0},{2,3},{3,2},{4,5},{5,4},{6,7},{7,6},{8,9},{9,8},{10,11... | collective-permute-start | bytes 786440 | tf_op jit(solution)/shard_map/ppermute | solution.py:49
  73.0 0.1 stack.101.at_ref
  73.1 2.1 %collective-permute-start.7 = (bf16[2,8,2048]{2,1,0:T(8,128)(2,1)S(1)}, bf16[2,8,2048]{2,1,0:T(8,128)(2,1)S(1)}, u32[]{:S(2)}, u32[]{:S(2)}) collective-permute-start(bf16[2,8,2048]{2,1,0:T(8,128)(2,1)S(1)} %slice.19), channel_id=1, source_target_pairs={{0,32},{32,64},{64,96},{96,128},{128,160},{160,192},{192,224},{224... | collective-permute-start | bytes 196616 | tf_op jit(solution)/shard_map/ppermute | solution.py:50
  75.3 5.3 %collective-permute-done = bf16[8,8,2048]{2,1,0:T(8,128)(2,1)S(1)} collective-permute-done((bf16[8,8,2048]{2,1,0:T(8,128)(2,1)S(1)}, bf16[8,8,2048]{2,1,0:T(8,128)(2,1)S(1)}, u32[]{:S(2)}, u32[]{:S(2)}) %collective-permute-start) | collective-permute-done | bytes 262176 | tf_op jit(solution)/shard_map/ppermute | solution.py:49
  80.6 0.0 collective-permute-done.11.refs_6_
  80.6 2.2 %collective-permute-done.7 = bf16[2,8,2048]{2,1,0:T(8,128)(2,1)S(1)} collective-permute-done((bf16[2,8,2048]{2,1,0:T(8,128)(2,1)S(1)}, bf16[2,8,2048]{2,1,0:T(8,128)(2,1)S(1)}, u32[]{:S(2)}, u32[]{:S(2)}) %collective-permute-start.7) | collective-permute-done | bytes 65568 | tf_op jit(solution)/shard_map/ppermute | solution.py:50
  82.8 0.0 collective-permute-done.12.refs_7_
  82.8 2.9 %edges.1 = (f32[288,384]{1,0:T(8,128)S(1)}, f32[288,128]{1,0:T(8,128)S(1)}, f32[672,128]{1,0:T(8,128)S(1)}, f32[96,128]{1,0:T(8,128)S(1)}) custom-call(s32[17]{0:T(128)S(1)} %stack.101.at_ref, bf16[128,2048]{1,0:T(8,128)(2,1)S(1)} %bitcast.33, bf16[128,2048]{1,0:T(8,128)(2,1)S(1)} %maximum_bitcast_fusion.refs_1_, bf16[16,2048]{1,0:T(8,128)(2,1)S(1)} %bitcast.35, ...), custom_call_target="tpu_custom_call" | custom-call | flops 603979776 | bytes 6291456 | tf_op jit(solution)/shard_map/edges/pallas_call | solution.py:281
  85.6 0.0 copy-start.7
  85.7 5.5 %collective-permute-start.13 = (f32[672,128]{1,0:T(8,128)S(1)}, f32[672,128]{1,0:T(8,128)S(1)}, u32[]{:S(2)}, u32[]{:S(2)}) collective-permute-start(f32[672,128]{1,0:T(8,128)S(1)} %get-tuple-element.21), channel_id=1, source_target_pairs={{0,1},{1,2},{2,3},{3,4},{4,5},{5,6},{6,7},{7,8},{8,9},{9,10},{10,1... | collective-permute-start | bytes 1032200 | tf_op jit(solution)/shard_map/ppermute | solution.py:291
  91.1 0.1 pad_add_fusion.slopes_ref
  91.2 1.9 %collective-permute-start.14 = (f32[96,128]{1,0:T(8,128)S(1)}, f32[96,128]{1,0:T(8,128)S(1)}, u32[]{:S(2)}, u32[]{:S(2)}) collective-permute-start(f32[96,128]{1,0:T(8,128)S(1)} %get-tuple-element.22), channel_id=1, source_target_pairs={{1,0},{2,1},{3,2},{4,3},{5,4},{6,5},{7,6},{8,7},{9,8},{10,9},{11,1... | collective-permute-start | bytes 147464 | tf_op jit(solution)/shard_map/ppermute | solution.py:292
  93.1 4.3 %middle.1 = (f32[288,128]{1,0:T(8,128)S(1)}, f32[6,288,128]{2,1,0:T(8,128)S(1)}) custom-call(s32[17]{0:T(128)S(1)} %stack.101.at_ref, bf16[128,2048]{1,0:T(8,128)(2,1)S(1)} %bitcast.34, bf16[128,2048]{1,0:T(8,128)(2,1)S(1)} %maximum_bitcast_fusion.refs_1_, bf16[16,2048]{1,0:T(8,128)(2,1)S(1)} %bitcast.36, bf16[16,2048]{1,0:T(8,128)(2,1)S(1)} %bitcast.38, ...), custom_call_target="tpu_custom_call" | custom-call | flops 2415919104 | bytes 16777216 | tf_op jit(solution)/shard_map/middle/pallas_call | solution.py:293
  97.4 1.8 %collective-permute-done.14.right_ref = f32[96,128]{1,0:T(8,128)S(1)} collective-permute-done((f32[96,128]{1,0:T(8,128)S(1)}, f32[96,128]{1,0:T(8,128)S(1)}, u32[]{:S(2)}, u32[]{:S(2)}) %collective-permute-start.14) | collective-permute-done | bytes 49184 | tf_op jit(solution)/shard_map/ppermute | solution.py:292
  99.3 0.0 collective-permute-done.13.left_ref
  99.3 15.5 %best.1 = f32[256,1024]{1,0:T(8,128)} custom-call(s32[9]{0:T(128)S(1)} %pad_add_fusion.slopes_ref, f32[672,128]{1,0:T(8,128)S(1)} %collective-permute-done.13.left_ref, f32[96,128]{1,0:T(8,128)S(1)} %collective-permute-done.14.right_ref, f32[288,384]{1,0:T(8,128)S(1)} %get-tuple-element.23.refs_8_.last_ref, ...), custom_call_target="tpu_custom_call" | custom-call | flops 62914560 | bytes 4194304 | tf_op jit(solution)/shard_map/best/pallas_call | solution.py:309
  (12 shorter events, 0.1 us)
Async XLA Ops:
  1.6 14.4 %copy-start = (bf16[1024,128]{1,0:T(8,128)(2,1)S(1)}, bf16[1024,128]{1,0:T(8,128)(2,1)}, u32[]{:S(2)}) copy-start(bf16[1024,128]{1,0:T(8,128)(2,1)} %param.4) | copy-start | bytes 786436
  1.6 42.8 %all-to-all-start = ((bf16[16,8,2048]{2,1,0:T(8,128)(2,1)}), bf16[16,8,2048]{2,1,0:T(8,128)(2,1)S(1)}, u32[]{:S(2)}, u32[]{:S(2)}) async-start(bf16[16,8,2048]{2,1,0:T(8,128)(2,1)} %broadcast_in_dim.15), calls=%async_computation | async-start | bytes 1048576 | tf_op jit(solution)/shard_map/all_to_all | solution.py:45
  16.0 20.5 %collective-permute-start.10 = (bf16[1024,128]{1,0:T(8,128)(2,1)S(1)}, bf16[1024,128]{1,0:T(8,128)(2,1)S(1)}, u32[]{:S(2)}, u32[]{:S(2)}) collective-permute-start(bf16[1024,128]{1,0:T(8,128)(2,1)S(1)} %copy-done), channel_id=1, source_target_pairs={{0,448},{32,480},{64,384},{96,416},{128,64},{160,96},{192,0},{224,... | collective-permute-start | bytes 786440 | tf_op jit(solution)/shard_map/ppermute | solution.py:46
  20.0 19.1 %collective-permute-start.9 = (bf16[1024,128]{1,0:T(8,128)(2,1)S(1)}, bf16[1024,128]{1,0:T(8,128)(2,1)S(1)}, u32[]{:S(2)}, u32[]{:S(2)}) collective-permute-start(bf16[1024,128]{1,0:T(8,128)(2,1)S(1)} %copy-done), channel_id=1, source_target_pairs={{0,192},{32,224},{64,128},{96,160},{128,320},{160,352},{192,256},{... | collective-permute-start | bytes 786440 | tf_op jit(solution)/shard_map/ppermute | solution.py:46
  24.3 33.3 %collective-permute-start.4 = (bf16[1024,128]{1,0:T(8,128)(2,1)S(1)}, bf16[1024,128]{1,0:T(8,128)(2,1)S(1)}, u32[]{:S(2)}, u32[]{:S(2)}) collective-permute-start(bf16[1024,128]{1,0:T(8,128)(2,1)S(1)} %copy-done), channel_id=1, source_target_pairs={{0,64},{32,96},{64,0},{96,32},{128,192},{160,224},{192,128},{224,1... | collective-permute-start | bytes 786440 | tf_op jit(solution)/shard_map/ppermute | solution.py:46
  28.3 31.2 %collective-permute-start.3 = (bf16[1024,128]{1,0:T(8,128)(2,1)S(1)}, bf16[1024,128]{1,0:T(8,128)(2,1)S(1)}, u32[]{:S(2)}, u32[]{:S(2)}) collective-permute-start(bf16[1024,128]{1,0:T(8,128)(2,1)S(1)} %copy-done), channel_id=1, source_target_pairs={{0,320},{32,352},{64,256},{96,288},{128,448},{160,480},{192,384},{... | collective-permute-start | bytes 786440 | tf_op jit(solution)/shard_map/ppermute | solution.py:46
  34.6 27.4 %collective-permute-start.2 = (bf16[1024,128]{1,0:T(8,128)(2,1)S(1)}, bf16[1024,128]{1,0:T(8,128)(2,1)S(1)}, u32[]{:S(2)}, u32[]{:S(2)}) collective-permute-start(bf16[1024,128]{1,0:T(8,128)(2,1)S(1)} %copy-done), channel_id=1, source_target_pairs={{0,256},{32,288},{64,320},{96,352},{128,384},{160,416},{192,448},{... | collective-permute-start | bytes 786440 | tf_op jit(solution)/shard_map/ppermute | solution.py:46
  36.6 7.9 %copy-start.4 = (bf16[1024,128]{1,0:T(8,128)(2,1)}, bf16[1024,128]{1,0:T(8,128)(2,1)S(1)}, u32[]{:S(2)}) copy-start(bf16[1024,128]{1,0:T(8,128)(2,1)S(1)} %collective-permute-done.10) | copy-start | bytes 786436
  36.6 25.5 %collective-permute-start.1 = (bf16[1024,128]{1,0:T(8,128)(2,1)S(1)}, bf16[1024,128]{1,0:T(8,128)(2,1)S(1)}, u32[]{:S(2)}, u32[]{:S(2)}) collective-permute-start(bf16[1024,128]{1,0:T(8,128)(2,1)S(1)} %copy-done), channel_id=1, source_target_pairs={{0,384},{32,416},{64,448},{96,480},{128,0},{160,32},{192,64},{224,... | collective-permute-start | bytes 786440 | tf_op jit(solution)/shard_map/ppermute | solution.py:46
  39.1 5.4 %copy-start.5 = (bf16[1024,128]{1,0:T(8,128)(2,1)}, bf16[1024,128]{1,0:T(8,128)(2,1)S(1)}, u32[]{:S(2)}) copy-start(bf16[1024,128]{1,0:T(8,128)(2,1)S(1)} %collective-permute-done.9) | copy-start | bytes 786436
  39.1 14.2 %collective-permute-start.8 = (bf16[1024,128]{1,0:T(8,128)(2,1)S(1)}, bf16[1024,128]{1,0:T(8,128)(2,1)S(1)}, u32[]{:S(2)}, u32[]{:S(2)}) collective-permute-start(bf16[1024,128]{1,0:T(8,128)(2,1)S(1)} %copy-done), channel_id=1, source_target_pairs={{0,128},{32,160},{64,192},{96,224},{128,256},{160,288},{192,320},{... | collective-permute-start | bytes 786440 | tf_op jit(solution)/shard_map/ppermute | solution.py:46
  53.3 3.1 %copy-start.6 = (bf16[1024,128]{1,0:T(8,128)(2,1)}, bf16[1024,128]{1,0:T(8,128)(2,1)S(1)}, u32[]{:S(2)}) copy-start(bf16[1024,128]{1,0:T(8,128)(2,1)S(1)} %collective-permute-done.8) | copy-start | bytes 786436
  53.3 14.3 %collective-permute-start.5 = (bf16[8,8,2048]{2,1,0:T(8,128)(2,1)S(1)}, bf16[8,8,2048]{2,1,0:T(8,128)(2,1)S(1)}, u32[]{:S(2)}, u32[]{:S(2)}) collective-permute-start(bf16[8,8,2048]{2,1,0:T(8,128)(2,1)S(1)} %get-tuple-element.28), channel_id=1, source_target_pairs={{0,1},{1,0},{2,3},{3,2},{4,5},{5,4},{6,7},{7,6},{8,9},{9,8},{10,11... | collective-permute-start | bytes 786440 | tf_op jit(solution)/shard_map/ppermute | solution.py:49
  57.7 22.9 %collective-permute-start.11 = (bf16[4,1024,128]{2,1,0:T(8,128)(2,1)S(1)}, bf16[4,1024,128]{2,1,0:T(8,128)(2,1)}, u32[]{:S(2)}, u32[]{:S(2)}) collective-permute-start(bf16[4,1024,128]{2,1,0:T(8,128)(2,1)S(1)} %pad_maximum_fusion.1.refs_4_), channel_id=1, source_target_pairs={{0,32},{32,0},{64,96},{96,64},{128,160},{160,128},{192,224},{224,1... | collective-permute-start | bytes 3145736 | tf_op jit(solution)/shard_map/ppermute | solution.py:53
  59.6 2.5 %copy-start.1 = (bf16[1024,128]{1,0:T(8,128)(2,1)}, bf16[1024,128]{1,0:T(8,128)(2,1)S(1)}, u32[]{:S(2)}) copy-start(bf16[1024,128]{1,0:T(8,128)(2,1)S(1)} %collective-permute-done.3) | copy-start | bytes 786436
  59.6 8.0 %collective-permute-start.6 = (bf16[2,8,2048]{2,1,0:T(8,128)(2,1)S(1)}, bf16[2,8,2048]{2,1,0:T(8,128)(2,1)S(1)}, u32[]{:S(2)}, u32[]{:S(2)}) collective-permute-start(bf16[2,8,2048]{2,1,0:T(8,128)(2,1)S(1)} %slice.18), channel_id=1, source_target_pairs={{0,32},{32,64},{64,96},{96,128},{128,160},{160,192},{192,224},{224... | collective-permute-start | bytes 196616 | tf_op jit(solution)/shard_map/ppermute | solution.py:48
  62.0 0.7 copy-start.2
  62.1 0.8 copy-start.3
  67.6 15.2 %collective-permute-start.12 = (bf16[4,1024,128]{2,1,0:T(8,128)(2,1)S(1)}, bf16[4,1024,128]{2,1,0:T(8,128)(2,1)}, u32[]{:S(2)}, u32[]{:S(2)}) collective-permute-start(bf16[4,1024,128]{2,1,0:T(8,128)(2,1)S(1)} %pad_maximum_fusion.refs_5_), channel_id=1, source_target_pairs={{0,32},{32,0},{64,96},{96,64},{128,160},{160,128},{192,224},{224,1... | collective-permute-start | bytes 3145736 | tf_op jit(solution)/shard_map/ppermute | solution.py:53
  69.5 11.0 %collective-permute-start = (bf16[8,8,2048]{2,1,0:T(8,128)(2,1)S(1)}, bf16[8,8,2048]{2,1,0:T(8,128)(2,1)S(1)}, u32[]{:S(2)}, u32[]{:S(2)}) collective-permute-start(bf16[8,8,2048]{2,1,0:T(8,128)(2,1)S(1)} %get-tuple-element.27), channel_id=1, source_target_pairs={{0,1},{1,0},{2,3},{3,2},{4,5},{5,4},{6,7},{7,6},{8,9},{9,8},{10,11... | collective-permute-start | bytes 786440 | tf_op jit(solution)/shard_map/ppermute | solution.py:49
  73.1 9.6 %collective-permute-start.7 = (bf16[2,8,2048]{2,1,0:T(8,128)(2,1)S(1)}, bf16[2,8,2048]{2,1,0:T(8,128)(2,1)S(1)}, u32[]{:S(2)}, u32[]{:S(2)}) collective-permute-start(bf16[2,8,2048]{2,1,0:T(8,128)(2,1)S(1)} %slice.19), channel_id=1, source_target_pairs={{0,32},{32,64},{64,96},{96,128},{128,160},{160,192},{192,224},{224... | collective-permute-start | bytes 196616 | tf_op jit(solution)/shard_map/ppermute | solution.py:50
  85.6 5.5 %copy-start.7 = (s32[8]{0:T(128)S(1)}, s32[8]{0:T(128)}, u32[]{:S(2)}) copy-start(s32[8]{0:T(128)} %param.5) | copy-start | bytes 100
  85.7 13.6 %collective-permute-start.13 = (f32[672,128]{1,0:T(8,128)S(1)}, f32[672,128]{1,0:T(8,128)S(1)}, u32[]{:S(2)}, u32[]{:S(2)}) collective-permute-start(f32[672,128]{1,0:T(8,128)S(1)} %get-tuple-element.21), channel_id=1, source_target_pairs={{0,1},{1,2},{2,3},{3,4},{4,5},{5,6},{6,7},{7,8},{8,9},{9,10},{10,1... | collective-permute-start | bytes 1032200 | tf_op jit(solution)/shard_map/ppermute | solution.py:291
  91.2 8.1 %collective-permute-start.14 = (f32[96,128]{1,0:T(8,128)S(1)}, f32[96,128]{1,0:T(8,128)S(1)}, u32[]{:S(2)}, u32[]{:S(2)}) collective-permute-start(f32[96,128]{1,0:T(8,128)S(1)} %get-tuple-element.22), channel_id=1, source_target_pairs={{1,0},{2,1},{3,2},{4,3},{5,4},{6,5},{7,6},{8,7},{9,8},{10,9},{11,1... | collective-permute-start | bytes 147464 | tf_op jit(solution)/shard_map/ppermute | solution.py:292

commit v6 on v5

--- a/solution.py
+++ b/solution.py
@@ -20,7 +20,7 @@
 HALO = LEFT // LANES
 TILES = HALO + COLUMNS // LANES
 FIRST, LAST = HALO + 1, TILES - 1
-SHIFTS = ((1, 0), (1, 1), (3, 1), (3, 0), (2, 0), (2, 1), (0, 1))
+SHIFTS = ((1, 0), (3, 0), (0, 1), (1, 1), (3, 1), (2, 0), (2, 1))
 
 
 def tile(c):

time: 116 us -> 117 us (level)
  the two profiles are of different devices: /device:TPU:106 before, /device:TPU:57 now
where the time goes in v6:
time: 117 us; the launch traced here: 116 us
  starting transfers between devices  70.8 us (61%)
  Pallas kernels  22.7 us (19%)
  waiting for transfers between devices  16.6 us (14%)
  other arithmetic  2.61 us (2%)
  local copies, waits for them, and re-layouts  2.54 us (2%)
    ppermute x7, starting transfers between devices, gather(): lax.ppermute(frames, 'pb', across(dy, dx, 0))  25.6 us
    pallas_call x1, Pallas kernels, best_of(): pl.pallas_call(best_kernel, name='best', out_shape=jax.ShapeDtypeStruct((...  15.5 us
    all_to_all x1, starting transfers between devices, gather(): near = lax.all_to_all(copies, 'ma', 0, 0, axis_index_groups=groups)  14.8 us
    ppermute x2, starting transfers between devices, gather(): other = [lax.ppermute(part, 'pb', across(0, 0, 1)) for part in own]  13.1 us
    ppermute x7, waiting for transfers between devices, gather(): lax.ppermute(frames, 'pb', across(dy, dx, 0))  8.82 us
    ppermute x1, waiting for transfers between devices, gather(): lax.ppermute(near[:8], 'ma', sides)  4.56 us
    pallas_call x1, Pallas kernels, local(): pl.pallas_call(middle_kernel, name='middle', out_shape=(block(LANES), jax...  4.32 us
    ppermute x1, starting transfers between devices, gather(): near_top = lax.ppermute(near[14:], 'pb', [(i, i + 1) for i in range(15)])  3.54 us
  transfers between devices with their start and end apart: 16, of which 3 were waited for; matrix products, arithmetic and copies ran while one was open for 2% of the time, Pallas kernels for 4%

profile of v6, /device:TPU:57, one launch (start us, length us, event | category | flops | bytes accessed | tf_op | source)
XLA Modules:
  0.0 115.7 jit_solution(13464862009881211475)
XLA Ops:
  0.0 1.6 %broadcast_in_dim.15 = bf16[16,8,2048]{2,1,0:T(8,128)(2,1)} broadcast(bf16[8,2048]{1,0:T(8,128)(2,1)} %bitcast.47), dimensions={1,2} | broadcast | bytes 557056 | tf_op jit(solution)/shard_map/broadcast_in_dim | solution.py:43
  1.6 14.8 %all-to-all-start = ((bf16[16,8,2048]{2,1,0:T(8,128)(2,1)}), bf16[16,8,2048]{2,1,0:T(8,128)(2,1)S(1)}, u32[]{:S(2)}, u32[]{:S(2)}) async-start(bf16[16,8,2048]{2,1,0:T(8,128)(2,1)} %broadcast_in_dim.15), calls=%async_computation | async-start | bytes 1048576 | tf_op jit(solution)/shard_map/all_to_all | solution.py:45
  16.4 0.0 copy-done
  16.4 4.7 %collective-permute-start.10 = (bf16[1024,128]{1,0:T(8,128)(2,1)S(1)}, bf16[1024,128]{1,0:T(8,128)(2,1)S(1)}, u32[]{:S(2)}, u32[]{:S(2)}) collective-permute-start(bf16[1024,128]{1,0:T(8,128)(2,1)S(1)} %copy-done), channel_id=1, source_target_pairs={{0,64},{32,96},{64,0},{96,32},{128,192},{160,224},{192,128},{224,1... | collective-permute-start | bytes 786440 | tf_op jit(solution)/shard_map/ppermute | solution.py:46
  21.1 2.4 %collective-permute-start.9 = (bf16[1024,128]{1,0:T(8,128)(2,1)S(1)}, bf16[1024,128]{1,0:T(8,128)(2,1)S(1)}, u32[]{:S(2)}, u32[]{:S(2)}) collective-permute-start(bf16[1024,128]{1,0:T(8,128)(2,1)S(1)} %copy-done), channel_id=1, source_target_pairs={{0,384},{32,416},{64,448},{96,480},{128,0},{160,32},{192,64},{224,... | collective-permute-start | bytes 786440 | tf_op jit(solution)/shard_map/ppermute | solution.py:46
  23.4 2.5 %collective-permute-start.4 = (bf16[1024,128]{1,0:T(8,128)(2,1)S(1)}, bf16[1024,128]{1,0:T(8,128)(2,1)S(1)}, u32[]{:S(2)}, u32[]{:S(2)}) collective-permute-start(bf16[1024,128]{1,0:T(8,128)(2,1)S(1)} %copy-done), channel_id=1, source_target_pairs={{0,320},{32,352},{64,256},{96,288},{128,448},{160,480},{192,384},{... | collective-permute-start | bytes 786440 | tf_op jit(solution)/shard_map/ppermute | solution.py:46
  26.0 4.2 %collective-permute-start.3 = (bf16[1024,128]{1,0:T(8,128)(2,1)S(1)}, bf16[1024,128]{1,0:T(8,128)(2,1)S(1)}, u32[]{:S(2)}, u32[]{:S(2)}) collective-permute-start(bf16[1024,128]{1,0:T(8,128)(2,1)S(1)} %copy-done), channel_id=1, source_target_pairs={{0,256},{32,288},{64,320},{96,352},{128,384},{160,416},{192,448},{... | collective-permute-start | bytes 786440 | tf_op jit(solution)/shard_map/ppermute | solution.py:46
  30.2 4.5 %collective-permute-start.2 = (bf16[1024,128]{1,0:T(8,128)(2,1)S(1)}, bf16[1024,128]{1,0:T(8,128)(2,1)S(1)}, u32[]{:S(2)}, u32[]{:S(2)}) collective-permute-start(bf16[1024,128]{1,0:T(8,128)(2,1)S(1)} %copy-done), channel_id=1, source_target_pairs={{0,448},{32,480},{64,384},{96,416},{128,64},{160,96},{192,0},{224,... | collective-permute-start | bytes 786440 | tf_op jit(solution)/shard_map/ppermute | solution.py:46
  34.7 0.0 collective-permute-done.10
  34.7 0.0 copy-start.4
  34.7 4.4 %collective-permute-start.1 = (bf16[1024,128]{1,0:T(8,128)(2,1)S(1)}, bf16[1024,128]{1,0:T(8,128)(2,1)S(1)}, u32[]{:S(2)}, u32[]{:S(2)}) collective-permute-start(bf16[1024,128]{1,0:T(8,128)(2,1)S(1)} %copy-done), channel_id=1, source_target_pairs={{0,192},{32,224},{64,128},{96,160},{128,320},{160,352},{192,256},{... | collective-permute-start | bytes 786440 | tf_op jit(solution)/shard_map/ppermute | solution.py:46
  39.1 0.0 collective-permute-done.9
  39.1 2.9 %collective-permute-start.8 = (bf16[1024,128]{1,0:T(8,128)(2,1)S(1)}, bf16[1024,128]{1,0:T(8,128)(2,1)S(1)}, u32[]{:S(2)}, u32[]{:S(2)}) collective-permute-start(bf16[1024,128]{1,0:T(8,128)(2,1)S(1)} %copy-done), channel_id=1, source_target_pairs={{0,128},{32,160},{64,192},{96,224},{128,256},{160,288},{192,320},{... | collective-permute-start | bytes 786440 | tf_op jit(solution)/shard_map/ppermute | solution.py:46
  42.0 0.0 all-to-all-done
  42.1 8.8 %collective-permute-done.8 = bf16[1024,128]{1,0:T(8,128)(2,1)S(1)} collective-permute-done((bf16[1024,128]{1,0:T(8,128)(2,1)S(1)}, bf16[1024,128]{1,0:T(8,128)(2,1)S(1)}, u32[]{:S(2)}, u32[]{:S(2)}) %collective-permute-start.8) | collective-permute-done | bytes 262176 | tf_op jit(solution)/shard_map/ppermute | solution.py:46
  50.9 2.7 %collective-permute-start.5 = (bf16[8,8,2048]{2,1,0:T(8,128)(2,1)S(1)}, bf16[8,8,2048]{2,1,0:T(8,128)(2,1)S(1)}, u32[]{:S(2)}, u32[]{:S(2)}) collective-permute-start(bf16[8,8,2048]{2,1,0:T(8,128)(2,1)S(1)} %get-tuple-element.28), channel_id=1, source_target_pairs={{0,1},{1,0},{2,3},{3,2},{4,5},{5,4},{6,7},{7,6},{8,9},{9,8},{10,11... | collective-permute-start | bytes 786440 | tf_op jit(solution)/shard_map/ppermute | solution.py:49
  53.6 1.2 %pad_maximum_fusion.1.refs_4_ = bf16[4,1024,128]{2,1,0:T(8,128)(2,1)S(1)} fusion(bf16[1,1024,128]{2,1,0:T(8,128)(2,1)} %bitcast.44, bf16[1,1024,128]{2,1,0:T(8,128)(2,1)} %bitcast.45, bf16[1,1024,128]{2,1,0:T(8,128)(2,1)} %bitcast.46, bf16[1,1024,128]{2,1,0:T(8,128)(2,1)S(1)} %bitcast.39), kind=kLoop, calls=%fused_computation.1 | loop fusion | flops 1572864 | bytes 2097152 | tf_op jit(solution)/shard_map/stack | solution.py:47
  54.9 0.0 collective-permute-done.4
  54.9 8.8 %collective-permute-start.11 = (bf16[4,1024,128]{2,1,0:T(8,128)(2,1)S(1)}, bf16[4,1024,128]{2,1,0:T(8,128)(2,1)}, u32[]{:S(2)}, u32[]{:S(2)}) collective-permute-start(bf16[4,1024,128]{2,1,0:T(8,128)(2,1)S(1)} %pad_maximum_fusion.1.refs_4_), channel_id=1, source_target_pairs={{0,32},{32,0},{64,96},{96,64},{128,160},{160,128},{192,224},{224,1... | collective-permute-start | bytes 3145736 | tf_op jit(solution)/shard_map/ppermute | solution.py:53
  63.7 0.0 collective-permute-done.3
  63.7 0.0 copy-start.1
  63.7 3.5 %collective-permute-start.6 = (bf16[2,8,2048]{2,1,0:T(8,128)(2,1)S(1)}, bf16[2,8,2048]{2,1,0:T(8,128)(2,1)S(1)}, u32[]{:S(2)}, u32[]{:S(2)}) collective-permute-start(bf16[2,8,2048]{2,1,0:T(8,128)(2,1)S(1)} %slice.18), channel_id=1, source_target_pairs={{0,32},{32,64},{64,96},{96,128},{128,160},{160,192},{192,224},{224... | collective-permute-start | bytes 196616 | tf_op jit(solution)/shard_map/ppermute | solution.py:48
  67.3 0.0 collective-permute-done.2
  67.3 0.0 copy-start.2
  67.3 0.0 collective-permute-done.1
  67.3 0.7 copy-done.2
  68.0 0.1 copy-done.3
  68.1 1.2 %pad_maximum_fusion.refs_5_ = bf16[4,1024,128]{2,1,0:T(8,128)(2,1)S(1)} fusion(bf16[1,1024,128]{2,1,0:T(8,128)(2,1)S(1)} %bitcast.40, bf16[1,1024,128]{2,1,0:T(8,128)(2,1)} %bitcast.41, bf16[1,1024,128]{2,1,0:T(8,128)(2,1)} %bitcast.42, bf16[1,1024,128]{2,1,0:T(8,128)(2,1)} %bitcast.43), kind=kLoop, calls=%fused_computation | loop fusion | flops 1572864 | bytes 2097152 | tf_op jit(solution)/shard_map/stack | solution.py:47
  69.3 0.0 collective-permute-done.6
  69.3 0.0 collective-permute-done.5
  69.3 4.3 %collective-permute-start.12 = (bf16[4,1024,128]{2,1,0:T(8,128)(2,1)S(1)}, bf16[4,1024,128]{2,1,0:T(8,128)(2,1)}, u32[]{:S(2)}, u32[]{:S(2)}) collective-permute-start(bf16[4,1024,128]{2,1,0:T(8,128)(2,1)S(1)} %pad_maximum_fusion.refs_5_), channel_id=1, source_target_pairs={{0,32},{32,0},{64,96},{96,64},{128,160},{160,128},{192,224},{224,1... | collective-permute-start | bytes 3145736 | tf_op jit(solution)/shard_map/ppermute | solution.py:53
  73.6 3.1 %collective-permute-start = (bf16[8,8,2048]{2,1,0:T(8,128)(2,1)S(1)}, bf16[8,8,2048]{2,1,0:T(8,128)(2,1)S(1)}, u32[]{:S(2)}, u32[]{:S(2)}) collective-permute-start(bf16[8,8,2048]{2,1,0:T(8,128)(2,1)S(1)} %get-tuple-element.27), channel_id=1, source_target_pairs={{0,1},{1,0},{2,3},{3,2},{4,5},{5,4},{6,7},{7,6},{8,9},{9,8},{10,11... | collective-permute-start | bytes 786440 | tf_op jit(solution)/shard_map/ppermute | solution.py:49
  76.8 0.1 stack.101.at_ref
  76.9 1.9 %collective-permute-start.7 = (bf16[2,8,2048]{2,1,0:T(8,128)(2,1)S(1)}, bf16[2,8,2048]{2,1,0:T(8,128)(2,1)S(1)}, u32[]{:S(2)}, u32[]{:S(2)}) collective-permute-start(bf16[2,8,2048]{2,1,0:T(8,128)(2,1)S(1)} %slice.19), channel_id=1, source_target_pairs={{0,32},{32,64},{64,96},{96,128},{128,160},{160,192},{192,224},{224... | collective-permute-start | bytes 196616 | tf_op jit(solution)/shard_map/ppermute | solution.py:50
  78.9 4.6 %collective-permute-done = bf16[8,8,2048]{2,1,0:T(8,128)(2,1)S(1)} collective-permute-done((bf16[8,8,2048]{2,1,0:T(8,128)(2,1)S(1)}, bf16[8,8,2048]{2,1,0:T(8,128)(2,1)S(1)}, u32[]{:S(2)}, u32[]{:S(2)}) %collective-permute-start) | collective-permute-done | bytes 262176 | tf_op jit(solution)/shard_map/ppermute | solution.py:49
  83.5 0.0 collective-permute-done.11.refs_6_
  83.5 0.0 collective-permute-done.7
  83.5 0.0 collective-permute-done.12.refs_7_
  83.5 2.9 %edges.1 = (f32[288,384]{1,0:T(8,128)S(1)}, f32[288,128]{1,0:T(8,128)S(1)}, f32[672,128]{1,0:T(8,128)S(1)}, f32[96,128]{1,0:T(8,128)S(1)}) custom-call(s32[17]{0:T(128)S(1)} %stack.101.at_ref, bf16[128,2048]{1,0:T(8,128)(2,1)S(1)} %bitcast.33, bf16[128,2048]{1,0:T(8,128)(2,1)S(1)} %maximum_bitcast_fusion.refs_1_, bf16[16,2048]{1,0:T(8,128)(2,1)S(1)} %bitcast.35, ...), custom_call_target="tpu_custom_call" | custom-call | flops 603979776 | bytes 6291456 | tf_op jit(solution)/shard_map/edges/pallas_call | solution.py:281
  86.4 0.0 copy-start.7
  86.4 3.1 %collective-permute-start.13 = (f32[672,128]{1,0:T(8,128)S(1)}, f32[672,128]{1,0:T(8,128)S(1)}, u32[]{:S(2)}, u32[]{:S(2)}) collective-permute-start(f32[672,128]{1,0:T(8,128)S(1)} %get-tuple-element.21), channel_id=1, source_target_pairs={{0,1},{1,2},{2,3},{3,4},{4,5},{5,6},{6,7},{7,8},{8,9},{9,10},{10,1... | collective-permute-start | bytes 1032200 | tf_op jit(solution)/shard_map/ppermute | solution.py:291
  89.5 0.0 copy-done.7
  89.5 0.1 pad_add_fusion.slopes_ref
  89.6 3.1 %collective-permute-start.14 = (f32[96,128]{1,0:T(8,128)S(1)}, f32[96,128]{1,0:T(8,128)S(1)}, u32[]{:S(2)}, u32[]{:S(2)}) collective-permute-start(f32[96,128]{1,0:T(8,128)S(1)} %get-tuple-element.22), channel_id=1, source_target_pairs={{1,0},{2,1},{3,2},{4,3},{5,4},{6,5},{7,6},{8,7},{9,8},{10,9},{11,1... | collective-permute-start | bytes 147464 | tf_op jit(solution)/shard_map/ppermute | solution.py:292
  92.7 4.3 %middle.1 = (f32[288,128]{1,0:T(8,128)S(1)}, f32[6,288,128]{2,1,0:T(8,128)S(1)}) custom-call(s32[17]{0:T(128)S(1)} %stack.101.at_ref, bf16[128,2048]{1,0:T(8,128)(2,1)S(1)} %bitcast.34, bf16[128,2048]{1,0:T(8,128)(2,1)S(1)} %maximum_bitcast_fusion.refs_1_, bf16[16,2048]{1,0:T(8,128)(2,1)S(1)} %bitcast.36, bf16[16,2048]{1,0:T(8,128)(2,1)S(1)} %bitcast.38, ...), custom_call_target="tpu_custom_call" | custom-call | flops 2415919104 | bytes 16777216 | tf_op jit(solution)/shard_map/middle/pallas_call | solution.py:293
  97.0 3.2 %collective-permute-done.14.right_ref = f32[96,128]{1,0:T(8,128)S(1)} collective-permute-done((f32[96,128]{1,0:T(8,128)S(1)}, f32[96,128]{1,0:T(8,128)S(1)}, u32[]{:S(2)}, u32[]{:S(2)}) %collective-permute-start.14) | collective-permute-done | bytes 49184 | tf_op jit(solution)/shard_map/ppermute | solution.py:292
  100.2 0.0 collective-permute-done.13.left_ref
  100.2 15.5 %best.1 = f32[256,1024]{1,0:T(8,128)} custom-call(s32[9]{0:T(128)S(1)} %pad_add_fusion.slopes_ref, f32[672,128]{1,0:T(8,128)S(1)} %collective-permute-done.13.left_ref, f32[96,128]{1,0:T(8,128)S(1)} %collective-permute-done.14.right_ref, f32[288,384]{1,0:T(8,128)S(1)} %get-tuple-element.23.refs_8_.last_ref, ...), custom_call_target="tpu_custom_call" | custom-call | flops 62914560 | bytes 4194304 | tf_op jit(solution)/shard_map/best/pallas_call | solution.py:309
  (12 shorter events, 0.1 us)
Async XLA Ops:
  1.6 14.8 %copy-start = (bf16[1024,128]{1,0:T(8,128)(2,1)S(1)}, bf16[1024,128]{1,0:T(8,128)(2,1)}, u32[]{:S(2)}) copy-start(bf16[1024,128]{1,0:T(8,128)(2,1)} %param.4) | copy-start | bytes 786436
  1.6 40.4 %all-to-all-start = ((bf16[16,8,2048]{2,1,0:T(8,128)(2,1)}), bf16[16,8,2048]{2,1,0:T(8,128)(2,1)S(1)}, u32[]{:S(2)}, u32[]{:S(2)}) async-start(bf16[16,8,2048]{2,1,0:T(8,128)(2,1)} %broadcast_in_dim.15), calls=%async_computation | async-start | bytes 1048576 | tf_op jit(solution)/shard_map/all_to_all | solution.py:45
  16.4 18.3 %collective-permute-start.10 = (bf16[1024,128]{1,0:T(8,128)(2,1)S(1)}, bf16[1024,128]{1,0:T(8,128)(2,1)S(1)}, u32[]{:S(2)}, u32[]{:S(2)}) collective-permute-start(bf16[1024,128]{1,0:T(8,128)(2,1)S(1)} %copy-done), channel_id=1, source_target_pairs={{0,64},{32,96},{64,0},{96,32},{128,192},{160,224},{192,128},{224,1... | collective-permute-start | bytes 786440 | tf_op jit(solution)/shard_map/ppermute | solution.py:46
  21.1 18.1 %collective-permute-start.9 = (bf16[1024,128]{1,0:T(8,128)(2,1)S(1)}, bf16[1024,128]{1,0:T(8,128)(2,1)S(1)}, u32[]{:S(2)}, u32[]{:S(2)}) collective-permute-start(bf16[1024,128]{1,0:T(8,128)(2,1)S(1)} %copy-done), channel_id=1, source_target_pairs={{0,384},{32,416},{64,448},{96,480},{128,0},{160,32},{192,64},{224,... | collective-permute-start | bytes 786440 | tf_op jit(solution)/shard_map/ppermute | solution.py:46
  23.4 31.4 %collective-permute-start.4 = (bf16[1024,128]{1,0:T(8,128)(2,1)S(1)}, bf16[1024,128]{1,0:T(8,128)(2,1)S(1)}, u32[]{:S(2)}, u32[]{:S(2)}) collective-permute-start(bf16[1024,128]{1,0:T(8,128)(2,1)S(1)} %copy-done), channel_id=1, source_target_pairs={{0,320},{32,352},{64,256},{96,288},{128,448},{160,480},{192,384},{... | collective-permute-start | bytes 786440 | tf_op jit(solution)/shard_map/ppermute | solution.py:46
  26.0 37.7 %collective-permute-start.3 = (bf16[1024,128]{1,0:T(8,128)(2,1)S(1)}, bf16[1024,128]{1,0:T(8,128)(2,1)S(1)}, u32[]{:S(2)}, u32[]{:S(2)}) collective-permute-start(bf16[1024,128]{1,0:T(8,128)(2,1)S(1)} %copy-done), channel_id=1, source_target_pairs={{0,256},{32,288},{64,320},{96,352},{128,384},{160,416},{192,448},{... | collective-permute-start | bytes 786440 | tf_op jit(solution)/shard_map/ppermute | solution.py:46
  30.2 37.1 %collective-permute-start.2 = (bf16[1024,128]{1,0:T(8,128)(2,1)S(1)}, bf16[1024,128]{1,0:T(8,128)(2,1)S(1)}, u32[]{:S(2)}, u32[]{:S(2)}) collective-permute-start(bf16[1024,128]{1,0:T(8,128)(2,1)S(1)} %copy-done), channel_id=1, source_target_pairs={{0,448},{32,480},{64,384},{96,416},{128,64},{160,96},{192,0},{224,... | collective-permute-start | bytes 786440 | tf_op jit(solution)/shard_map/ppermute | solution.py:46
  34.7 7.4 %copy-start.4 = (bf16[1024,128]{1,0:T(8,128)(2,1)}, bf16[1024,128]{1,0:T(8,128)(2,1)S(1)}, u32[]{:S(2)}) copy-start(bf16[1024,128]{1,0:T(8,128)(2,1)S(1)} %collective-permute-done.10) | copy-start | bytes 786436
  34.7 32.5 %collective-permute-start.1 = (bf16[1024,128]{1,0:T(8,128)(2,1)S(1)}, bf16[1024,128]{1,0:T(8,128)(2,1)S(1)}, u32[]{:S(2)}, u32[]{:S(2)}) collective-permute-start(bf16[1024,128]{1,0:T(8,128)(2,1)S(1)} %copy-done), channel_id=1, source_target_pairs={{0,192},{32,224},{64,128},{96,160},{128,320},{160,352},{192,256},{... | collective-permute-start | bytes 786440 | tf_op jit(solution)/shard_map/ppermute | solution.py:46
  39.1 3.0 %copy-start.5 = (bf16[1024,128]{1,0:T(8,128)(2,1)}, bf16[1024,128]{1,0:T(8,128)(2,1)S(1)}, u32[]{:S(2)}) copy-start(bf16[1024,128]{1,0:T(8,128)(2,1)S(1)} %collective-permute-done.9) | copy-start | bytes 786436
  39.1 11.8 %collective-permute-start.8 = (bf16[1024,128]{1,0:T(8,128)(2,1)S(1)}, bf16[1024,128]{1,0:T(8,128)(2,1)S(1)}, u32[]{:S(2)}, u32[]{:S(2)}) collective-permute-start(bf16[1024,128]{1,0:T(8,128)(2,1)S(1)} %copy-done), channel_id=1, source_target_pairs={{0,128},{32,160},{64,192},{96,224},{128,256},{160,288},{192,320},{... | collective-permute-start | bytes 786440 | tf_op jit(solution)/shard_map/ppermute | solution.py:46
  50.9 2.7 %copy-start.6 = (bf16[1024,128]{1,0:T(8,128)(2,1)}, bf16[1024,128]{1,0:T(8,128)(2,1)S(1)}, u32[]{:S(2)}) copy-start(bf16[1024,128]{1,0:T(8,128)(2,1)S(1)} %collective-permute-done.8) | copy-start | bytes 786436
  50.9 18.4 %collective-permute-start.5 = (bf16[8,8,2048]{2,1,0:T(8,128)(2,1)S(1)}, bf16[8,8,2048]{2,1,0:T(8,128)(2,1)S(1)}, u32[]{:S(2)}, u32[]{:S(2)}) collective-permute-start(bf16[8,8,2048]{2,1,0:T(8,128)(2,1)S(1)} %get-tuple-element.28), channel_id=1, source_target_pairs={{0,1},{1,0},{2,3},{3,2},{4,5},{5,4},{6,7},{7,6},{8,9},{9,8},{10,11... | collective-permute-start | bytes 786440 | tf_op jit(solution)/shard_map/ppermute | solution.py:49
  54.9 28.6 %collective-permute-start.11 = (bf16[4,1024,128]{2,1,0:T(8,128)(2,1)S(1)}, bf16[4,1024,128]{2,1,0:T(8,128)(2,1)}, u32[]{:S(2)}, u32[]{:S(2)}) collective-permute-start(bf16[4,1024,128]{2,1,0:T(8,128)(2,1)S(1)} %pad_maximum_fusion.1.refs_4_), channel_id=1, source_target_pairs={{0,32},{32,0},{64,96},{96,64},{128,160},{160,128},{192,224},{224,1... | collective-permute-start | bytes 3145736 | tf_op jit(solution)/shard_map/ppermute | solution.py:53
  63.7 3.6 %copy-start.1 = (bf16[1024,128]{1,0:T(8,128)(2,1)}, bf16[1024,128]{1,0:T(8,128)(2,1)S(1)}, u32[]{:S(2)}) copy-start(bf16[1024,128]{1,0:T(8,128)(2,1)S(1)} %collective-permute-done.3) | copy-start | bytes 786436
  63.7 5.6 %collective-permute-start.6 = (bf16[2,8,2048]{2,1,0:T(8,128)(2,1)S(1)}, bf16[2,8,2048]{2,1,0:T(8,128)(2,1)S(1)}, u32[]{:S(2)}, u32[]{:S(2)}) collective-permute-start(bf16[2,8,2048]{2,1,0:T(8,128)(2,1)S(1)} %slice.18), channel_id=1, source_target_pairs={{0,32},{32,64},{64,96},{96,128},{128,160},{160,192},{192,224},{224... | collective-permute-start | bytes 196616 | tf_op jit(solution)/shard_map/ppermute | solution.py:48
  67.3 0.7 copy-start.2
  67.3 0.8 copy-start.3
  69.3 14.2 %collective-permute-start.12 = (bf16[4,1024,128]{2,1,0:T(8,128)(2,1)S(1)}, bf16[4,1024,128]{2,1,0:T(8,128)(2,1)}, u32[]{:S(2)}, u32[]{:S(2)}) collective-permute-start(bf16[4,1024,128]{2,1,0:T(8,128)(2,1)S(1)} %pad_maximum_fusion.refs_5_), channel_id=1, source_target_pairs={{0,32},{32,0},{64,96},{96,64},{128,160},{160,128},{192,224},{224,1... | collective-permute-start | bytes 3145736 | tf_op jit(solution)/shard_map/ppermute | solution.py:53
  73.6 9.8 %collective-permute-start = (bf16[8,8,2048]{2,1,0:T(8,128)(2,1)S(1)}, bf16[8,8,2048]{2,1,0:T(8,128)(2,1)S(1)}, u32[]{:S(2)}, u32[]{:S(2)}) collective-permute-start(bf16[8,8,2048]{2,1,0:T(8,128)(2,1)S(1)} %get-tuple-element.27), channel_id=1, source_target_pairs={{0,1},{1,0},{2,3},{3,2},{4,5},{5,4},{6,7},{7,6},{8,9},{9,8},{10,11... | collective-permute-start | bytes 786440 | tf_op jit(solution)/shard_map/ppermute | solution.py:49
  76.9 6.6 %collective-permute-start.7 = (bf16[2,8,2048]{2,1,0:T(8,128)(2,1)S(1)}, bf16[2,8,2048]{2,1,0:T(8,128)(2,1)S(1)}, u32[]{:S(2)}, u32[]{:S(2)}) collective-permute-start(bf16[2,8,2048]{2,1,0:T(8,128)(2,1)S(1)} %slice.19), channel_id=1, source_target_pairs={{0,32},{32,64},{64,96},{96,128},{128,160},{160,192},{192,224},{224... | collective-permute-start | bytes 196616 | tf_op jit(solution)/shard_map/ppermute | solution.py:50
  86.4 3.1 %copy-start.7 = (s32[8]{0:T(128)S(1)}, s32[8]{0:T(128)}, u32[]{:S(2)}) copy-start(s32[8]{0:T(128)} %param.5) | copy-start | bytes 100
  86.4 13.8 %collective-permute-start.13 = (f32[672,128]{1,0:T(8,128)S(1)}, f32[672,128]{1,0:T(8,128)S(1)}, u32[]{:S(2)}, u32[]{:S(2)}) collective-permute-start(f32[672,128]{1,0:T(8,128)S(1)} %get-tuple-element.21), channel_id=1, source_target_pairs={{0,1},{1,2},{2,3},{3,4},{4,5},{5,6},{6,7},{7,8},{8,9},{9,10},{10,1... | collective-permute-start | bytes 1032200 | tf_op jit(solution)/shard_map/ppermute | solution.py:291
  89.6 10.7 %collective-permute-start.14 = (f32[96,128]{1,0:T(8,128)S(1)}, f32[96,128]{1,0:T(8,128)S(1)}, u32[]{:S(2)}, u32[]{:S(2)}) collective-permute-start(f32[96,128]{1,0:T(8,128)S(1)} %get-tuple-element.22), channel_id=1, source_target_pairs={{1,0},{2,1},{3,2},{4,3},{5,4},{6,5},{7,6},{8,7},{9,8},{10,9},{11,1... | collective-permute-start | bytes 147464 | tf_op jit(solution)/shard_map/ppermute | solution.py:292

commit v7 on v6

--- a/solution.py
+++ b/solution.py
@@ -101,7 +101,7 @@
 
 def edge_kernel(at_ref, *refs):
     row_refs, map_refs = refs[:4], refs[4:8]
-    last_ref, lead_ref, left_ref, right_ref, rows_ref = refs[8:]
+    last_ref, lead_ref, left_ref, rows_ref = refs[8:]
     fill_rows(row_refs, rows_ref)
     side = at_ref[16]
     begin = COLUMNS - LEFT
@@ -112,7 +112,6 @@
     left_ref[:ROWS] = last_ref[:, tile(1)]
     left_ref[ROWS : 2 * ROWS] = last_ref[:, tile(2)]
     left_ref[2 * ROWS :] = packed(last_ref, tile(0), LANES - PACK)
-    right_ref[...] = packed(lead_ref, tile(0), 0)
 
 
 def split_tile(split_ref, slot, value):
@@ -186,7 +185,7 @@
             if c + half < HALO:
                 value = jnp.where(first_map, 0.0, value)
             x_ref[c + half] = value
-    edge = [last_ref[:, tile(1)], last_ref[:, tile(2)], unpacked(right_ref[...], 0)]
+    edge = [last_ref[:, tile(1)], last_ref[:, tile(2)], right_ref[...]]
     for part in range(6):
         split_ref[part, :, tile(3)] = empty
     for c, value in enumerate(edge):
@@ -278,18 +277,18 @@
     limit = pltpu.CompilerParams(vmem_limit_bytes=40 << 20)
     rows_scratch = pltpu.VMEM((ROWS, 2048), jnp.bfloat16)
     lines = lambda count: jax.ShapeDtypeStruct((count, LANES), jnp.float32)
-    last, lead, left, right = pl.pallas_call(
+    last, lead, left = pl.pallas_call(
         edge_kernel,
         name="edges",
-        out_shape=(block(LEFT), block(LANES), lines(2 * ROWS + THIRD), lines(THIRD)),
+        out_shape=(block(LEFT), block(LANES), lines(2 * ROWS + THIRD)),
         in_specs=[SMEM] + [VMEM] * 8,
-        out_specs=(VMEM,) * 4,
+        out_specs=(VMEM,) * 3,
         scratch_shapes=[rows_scratch],
         compiler_params=limit,
         cost_estimate=pl.CostEstimate(flops=2 * ROWS * 512 * 2048, bytes_accessed=6 << 20, transcendentals=0),
     )(at, *rows, *frames)
     left = lax.ppermute(left, "ma", [(i, i + 1) for i in range(31)])
-    right = lax.ppermute(right, "ma", [(i + 1, i) for i in range(31)])
+    right = lax.ppermute(lead, "ma", [(i + 1, i) for i in range(31)])
     after, inner = pl.pallas_call(
         middle_kernel,
         name="middle",

time: 117 us -> 109 us (0.932)
  waiting for transfers between devices: 16.6 us -> 9.06 us
    ppermute x7, waiting for transfers between devices: 8.82 us -> 0.02 us  [gather(): lax.ppermute(frames, 'pb', across(dy, dx, 0))]
    ppermute x2, starting transfers between devices: 13.1 us -> 9.94 us  [gather(): other = [lax.ppermute(part, 'pb', across(0, 0, 1)) for part in own]]
    ppermute x1, waiting for transfers between devices: 3.23 us -> 5.34 us  [local(): right = lax.ppermute(lead, 'ma', [(i + 1, i) for i in range(31)])]
    ppermute x7, starting transfers between devices: 25.6 us -> 26.8 us  [gather(): lax.ppermute(frames, 'pb', across(dy, dx, 0))]
  transfers between devices with their start and end apart: 16 -> 16, of which waited for: 3 -> 2; matrix products, arithmetic and copies ran while one was open for 2% -> 2% of each run, Pallas kernels for 4% -> 4%
where the time goes in v7:
time: 109 us; the launch traced here: 108 us
  starting transfers between devices  70.9 us (65%)
  Pallas kernels  22.7 us (21%)
  waiting for transfers between devices  9.06 us (8%)
  other arithmetic  2.53 us (2%)
  local copies, waits for them, and re-layouts  2.44 us (2%)
    ppermute x7, starting transfers between devices, gather(): lax.ppermute(frames, 'pb', across(dy, dx, 0))  26.8 us
    pallas_call x1, Pallas kernels, best_of(): pl.pallas_call(best_kernel, name='best', out_shape=jax.ShapeDtypeStruct((...  15.5 us
    all_to_all x1, starting transfers between devices, gather(): near = lax.all_to_all(copies, 'ma', 0, 0, axis_index_groups=groups)  14.8 us
    ppermute x2, starting transfers between devices, gather(): other = [lax.ppermute(part, 'pb', across(0, 0, 1)) for part in own]  9.94 us
    ppermute x1, waiting for transfers between devices, local(): right = lax.ppermute(lead, 'ma', [(i + 1, i) for i in range(31)])  5.34 us
    pallas_call x1, Pallas kernels, local(): pl.pallas_call(middle_kernel, name='middle', out_shape=(block(LANES), jax...  4.32 us
    ppermute x1, starting transfers between devices, gather(): near_top = lax.ppermute(near[14:], 'pb', [(i, i + 1) for i in range(15)])  4.26 us
    ppermute x1, waiting for transfers between devices, gather(): lax.ppermute(near[:8], 'ma', sides)  3.69 us
  transfers between devices with their start and end apart: 16, of which 2 were waited for; matrix products, arithmetic and copies ran while one was open for 2% of the time, Pallas kernels for 4%

profile of v7, /device:TPU:57, one launch (start us, length us, event | category | flops | bytes accessed | tf_op | source)
XLA Modules:
  0.0 108.1 jit_solution(15285962917613960717)
XLA Ops:
  0.0 1.6 %broadcast_in_dim.15 = bf16[16,8,2048]{2,1,0:T(8,128)(2,1)} broadcast(bf16[8,2048]{1,0:T(8,128)(2,1)} %bitcast.46), dimensions={1,2} | broadcast | bytes 557056 | tf_op jit(solution)/shard_map/broadcast_in_dim | solution.py:43
  1.6 14.8 %all-to-all-start = ((bf16[16,8,2048]{2,1,0:T(8,128)(2,1)}), bf16[16,8,2048]{2,1,0:T(8,128)(2,1)S(1)}, u32[]{:S(2)}, u32[]{:S(2)}) async-start(bf16[16,8,2048]{2,1,0:T(8,128)(2,1)} %broadcast_in_dim.15), calls=%async_computation | async-start | bytes 1048576 | tf_op jit(solution)/shard_map/all_to_all | solution.py:45
  16.4 0.0 copy-done
  16.4 4.7 %collective-permute-start.10 = (bf16[1024,128]{1,0:T(8,128)(2,1)S(1)}, bf16[1024,128]{1,0:T(8,128)(2,1)S(1)}, u32[]{:S(2)}, u32[]{:S(2)}) collective-permute-start(bf16[1024,128]{1,0:T(8,128)(2,1)S(1)} %copy-done), channel_id=1, source_target_pairs={{0,64},{32,96},{64,0},{96,32},{128,192},{160,224},{192,128},{224,1... | collective-permute-start | bytes 786440 | tf_op jit(solution)/shard_map/ppermute | solution.py:46
  21.1 2.4 %collective-permute-start.9 = (bf16[1024,128]{1,0:T(8,128)(2,1)S(1)}, bf16[1024,128]{1,0:T(8,128)(2,1)S(1)}, u32[]{:S(2)}, u32[]{:S(2)}) collective-permute-start(bf16[1024,128]{1,0:T(8,128)(2,1)S(1)} %copy-done), channel_id=1, source_target_pairs={{0,384},{32,416},{64,448},{96,480},{128,0},{160,32},{192,64},{224,... | collective-permute-start | bytes 786440 | tf_op jit(solution)/shard_map/ppermute | solution.py:46
  23.4 4.1 %collective-permute-start.8 = (bf16[1024,128]{1,0:T(8,128)(2,1)S(1)}, bf16[1024,128]{1,0:T(8,128)(2,1)S(1)}, u32[]{:S(2)}, u32[]{:S(2)}) collective-permute-start(bf16[1024,128]{1,0:T(8,128)(2,1)S(1)} %copy-done), channel_id=1, source_target_pairs={{0,128},{32,160},{64,192},{96,224},{128,256},{160,288},{192,320},{... | collective-permute-start | bytes 786440 | tf_op jit(solution)/shard_map/ppermute | solution.py:46
  27.6 1.9 %collective-permute-start.4 = (bf16[1024,128]{1,0:T(8,128)(2,1)S(1)}, bf16[1024,128]{1,0:T(8,128)(2,1)S(1)}, u32[]{:S(2)}, u32[]{:S(2)}) collective-permute-start(bf16[1024,128]{1,0:T(8,128)(2,1)S(1)} %copy-done), channel_id=1, source_target_pairs={{0,320},{32,352},{64,256},{96,288},{128,448},{160,480},{192,384},{... | collective-permute-start | bytes 786440 | tf_op jit(solution)/shard_map/ppermute | solution.py:46
  29.5 4.8 %collective-permute-start.3 = (bf16[1024,128]{1,0:T(8,128)(2,1)S(1)}, bf16[1024,128]{1,0:T(8,128)(2,1)S(1)}, u32[]{:S(2)}, u32[]{:S(2)}) collective-permute-start(bf16[1024,128]{1,0:T(8,128)(2,1)S(1)} %copy-done), channel_id=1, source_target_pairs={{0,256},{32,288},{64,320},{96,352},{128,384},{160,416},{192,448},{... | collective-permute-start | bytes 786440 | tf_op jit(solution)/shard_map/ppermute | solution.py:46
  34.3 0.0 collective-permute-done.10
  34.3 3.6 %collective-permute-start.2 = (bf16[1024,128]{1,0:T(8,128)(2,1)S(1)}, bf16[1024,128]{1,0:T(8,128)(2,1)S(1)}, u32[]{:S(2)}, u32[]{:S(2)}) collective-permute-start(bf16[1024,128]{1,0:T(8,128)(2,1)S(1)} %copy-done), channel_id=1, source_target_pairs={{0,448},{32,480},{64,384},{96,416},{128,64},{160,96},{192,0},{224,... | collective-permute-start | bytes 786440 | tf_op jit(solution)/shard_map/ppermute | solution.py:46
  37.9 0.0 collective-permute-done.9
  38.0 0.0 copy-start.3
  38.0 5.3 %collective-permute-start.1 = (bf16[1024,128]{1,0:T(8,128)(2,1)S(1)}, bf16[1024,128]{1,0:T(8,128)(2,1)}, u32[]{:S(2)}, u32[]{:S(2)}) collective-permute-start(bf16[1024,128]{1,0:T(8,128)(2,1)S(1)} %copy-done), channel_id=1, source_target_pairs={{0,192},{32,224},{64,128},{96,160},{128,320},{160,352},{192,256},{... | collective-permute-start | bytes 786440 | tf_op jit(solution)/shard_map/ppermute | solution.py:46
  43.2 0.0 all-to-all-done
  43.3 0.0 copy-done.3
  43.3 0.0 collective-permute-done.8
  43.3 0.0 copy-start.4
  43.3 3.1 %collective-permute-start.5 = (bf16[8,8,2048]{2,1,0:T(8,128)(2,1)S(1)}, bf16[8,8,2048]{2,1,0:T(8,128)(2,1)S(1)}, u32[]{:S(2)}, u32[]{:S(2)}) collective-permute-start(bf16[8,8,2048]{2,1,0:T(8,128)(2,1)S(1)} %get-tuple-element.26), channel_id=1, source_target_pairs={{0,1},{1,0},{2,3},{3,2},{4,5},{5,4},{6,7},{7,6},{8,9},{9,8},{10,11... | collective-permute-start | bytes 786440 | tf_op jit(solution)/shard_map/ppermute | solution.py:49
  46.5 0.0 copy-done.4
  46.5 1.2 %pad_maximum_fusion.1.refs_4_ = bf16[4,1024,128]{2,1,0:T(8,128)(2,1)S(1)} fusion(bf16[1,1024,128]{2,1,0:T(8,128)(2,1)S(1)} %bitcast.43, bf16[1,1024,128]{2,1,0:T(8,128)(2,1)} %bitcast.44, bf16[1,1024,128]{2,1,0:T(8,128)(2,1)} %bitcast.45, bf16[1,1024,128]{2,1,0:T(8,128)(2,1)S(1)} %bitcast.39), kind=kLoop, calls=%fused_computation.1 | loop fusion | flops 1572864 | bytes 2097152 | tf_op jit(solution)/shard_map/stack | solution.py:47
  47.7 0.0 collective-permute-done.4
  47.7 5.4 %collective-permute-start.11 = (bf16[4,1024,128]{2,1,0:T(8,128)(2,1)S(1)}, bf16[4,1024,128]{2,1,0:T(8,128)(2,1)}, u32[]{:S(2)}, u32[]{:S(2)}) collective-permute-start(bf16[4,1024,128]{2,1,0:T(8,128)(2,1)S(1)} %pad_maximum_fusion.1.refs_4_), channel_id=1, source_target_pairs={{0,32},{32,0},{64,96},{96,64},{128,160},{160,128},{192,224},{224,1... | collective-permute-start | bytes 3145736 | tf_op jit(solution)/shard_map/ppermute | solution.py:53
  53.1 0.0 collective-permute-done.3
  53.1 0.0 copy-start.1
  53.1 4.3 %collective-permute-start.6 = (bf16[2,8,2048]{2,1,0:T(8,128)(2,1)S(1)}, bf16[2,8,2048]{2,1,0:T(8,128)(2,1)S(1)}, u32[]{:S(2)}, u32[]{:S(2)}) collective-permute-start(bf16[2,8,2048]{2,1,0:T(8,128)(2,1)S(1)} %slice.18), channel_id=1, source_target_pairs={{0,32},{32,64},{64,96},{96,128},{128,160},{160,192},{192,224},{224... | collective-permute-start | bytes 196616 | tf_op jit(solution)/shard_map/ppermute | solution.py:48
  57.3 0.0 collective-permute-done.2
  57.4 0.0 collective-permute-done.1
  57.4 0.7 copy-done.2
  58.1 1.2 %pad_maximum_fusion.refs_5_ = bf16[4,1024,128]{2,1,0:T(8,128)(2,1)S(1)} fusion(bf16[1,1024,128]{2,1,0:T(8,128)(2,1)S(1)} %bitcast.40, bf16[1,1024,128]{2,1,0:T(8,128)(2,1)} %bitcast.41, bf16[1,1024,128]{2,1,0:T(8,128)(2,1)} %bitcast.42, bf16[1,1024,128]{2,1,0:T(8,128)(2,1)} %bitcast.20), kind=kLoop, calls=%fused_computation | loop fusion | flops 1572864 | bytes 2097152 | tf_op jit(solution)/shard_map/stack | solution.py:47
  59.3 0.0 collective-permute-done.6
  59.3 0.0 collective-permute-done.5
  59.3 4.6 %collective-permute-start.12 = (bf16[4,1024,128]{2,1,0:T(8,128)(2,1)S(1)}, bf16[4,1024,128]{2,1,0:T(8,128)(2,1)}, u32[]{:S(2)}, u32[]{:S(2)}) collective-permute-start(bf16[4,1024,128]{2,1,0:T(8,128)(2,1)S(1)} %pad_maximum_fusion.refs_5_), channel_id=1, source_target_pairs={{0,32},{32,0},{64,96},{96,64},{128,160},{160,128},{192,224},{224,1... | collective-permute-start | bytes 3145736 | tf_op jit(solution)/shard_map/ppermute | solution.py:53
  63.9 3.0 %collective-permute-start = (bf16[8,8,2048]{2,1,0:T(8,128)(2,1)S(1)}, bf16[8,8,2048]{2,1,0:T(8,128)(2,1)S(1)}, u32[]{:S(2)}, u32[]{:S(2)}) collective-permute-start(bf16[8,8,2048]{2,1,0:T(8,128)(2,1)S(1)} %get-tuple-element.25), channel_id=1, source_target_pairs={{0,1},{1,0},{2,3},{3,2},{4,5},{5,4},{6,7},{7,6},{8,9},{9,8},{10,11... | collective-permute-start | bytes 786440 | tf_op jit(solution)/shard_map/ppermute | solution.py:49
  67.1 0.1 stack.101.at_ref
  67.2 2.8 %collective-permute-start.7 = (bf16[2,8,2048]{2,1,0:T(8,128)(2,1)S(1)}, bf16[2,8,2048]{2,1,0:T(8,128)(2,1)S(1)}, u32[]{:S(2)}, u32[]{:S(2)}) collective-permute-start(bf16[2,8,2048]{2,1,0:T(8,128)(2,1)S(1)} %slice.19), channel_id=1, source_target_pairs={{0,32},{32,64},{64,96},{96,128},{128,160},{160,192},{192,224},{224... | collective-permute-start | bytes 196616 | tf_op jit(solution)/shard_map/ppermute | solution.py:50
  70.0 3.7 %collective-permute-done = bf16[8,8,2048]{2,1,0:T(8,128)(2,1)S(1)} collective-permute-done((bf16[8,8,2048]{2,1,0:T(8,128)(2,1)S(1)}, bf16[8,8,2048]{2,1,0:T(8,128)(2,1)S(1)}, u32[]{:S(2)}, u32[]{:S(2)}) %collective-permute-start) | collective-permute-done | bytes 262176 | tf_op jit(solution)/shard_map/ppermute | solution.py:49
  73.7 0.0 collective-permute-done.11.refs_6_
  73.8 0.0 collective-permute-done.7
  73.8 0.0 collective-permute-done.12.refs_7_
  73.8 2.8 %edges.1 = (f32[288,384]{1,0:T(8,128)S(1)}, f32[288,128]{1,0:T(8,128)S(1)}, f32[672,128]{1,0:T(8,128)S(1)}) custom-call(s32[17]{0:T(128)S(1)} %stack.101.at_ref, bf16[128,2048]{1,0:T(8,128)(2,1)S(1)} %bitcast.33, bf16[128,2048]{1,0:T(8,128)(2,1)S(1)} %maximum_bitcast_fusion.refs_1_, bf16[16,2048]{1,0:T(8,128)(2,1)S(1)} %bitcast.35, ...), custom_call_target="tpu_custom_call" | custom-call | flops 603979776 | bytes 6291456 | tf_op jit(solution)/shard_map/edges/pallas_call | solution.py:280
  76.6 0.0 copy-start.5
  76.6 3.0 %collective-permute-start.13 = (f32[672,128]{1,0:T(8,128)S(1)}, f32[672,128]{1,0:T(8,128)S(1)}, u32[]{:S(2)}, u32[]{:S(2)}) collective-permute-start(f32[672,128]{1,0:T(8,128)S(1)} %get-tuple-element.20), channel_id=1, source_target_pairs={{0,1},{1,2},{2,3},{3,4},{4,5},{5,6},{6,7},{7,8},{8,9},{9,10},{10,1... | collective-permute-start | bytes 1032200 | tf_op jit(solution)/shard_map/ppermute | solution.py:290
  79.7 0.1 pad_add_fusion.slopes_ref
  79.8 3.1 %collective-permute-start.14 = (f32[288,128]{1,0:T(8,128)S(1)}, f32[288,128]{1,0:T(8,128)S(1)}, u32[]{:S(2)}, u32[]{:S(2)}) collective-permute-start(f32[288,128]{1,0:T(8,128)S(1)} %get-tuple-element.21.refs_9_.lead_ref), channel_id=1, source_target_pairs={{1,0},{2,1},{3,2},{4,3},{5,4},{6,5},{7,6},{8,7},{9,8},{10,9},{11,1... | collective-permute-start | bytes 442376 | tf_op jit(solution)/shard_map/ppermute | solution.py:291
  82.9 4.3 %middle.1 = (f32[288,128]{1,0:T(8,128)S(1)}, f32[6,288,128]{2,1,0:T(8,128)S(1)}) custom-call(s32[17]{0:T(128)S(1)} %stack.101.at_ref, bf16[128,2048]{1,0:T(8,128)(2,1)S(1)} %bitcast.34, bf16[128,2048]{1,0:T(8,128)(2,1)S(1)} %maximum_bitcast_fusion.refs_1_, bf16[16,2048]{1,0:T(8,128)(2,1)S(1)} %bitcast.36, bf16[16,2048]{1,0:T(8,128)(2,1)S(1)} %bitcast.38, ...), custom_call_target="tpu_custom_call" | custom-call | flops 2415919104 | bytes 16777216 | tf_op jit(solution)/shard_map/middle/pallas_call | solution.py:292
  87.2 5.3 %collective-permute-done.14.right_ref = f32[288,128]{1,0:T(8,128)S(1)} collective-permute-done((f32[288,128]{1,0:T(8,128)S(1)}, f32[288,128]{1,0:T(8,128)S(1)}, u32[]{:S(2)}, u32[]{:S(2)}) %collective-permute-start.14) | collective-permute-done | bytes 147488 | tf_op jit(solution)/shard_map/ppermute | solution.py:291
  92.6 0.0 collective-permute-done.13.left_ref
  92.6 15.5 %best.1 = f32[256,1024]{1,0:T(8,128)} custom-call(s32[9]{0:T(128)S(1)} %pad_add_fusion.slopes_ref, f32[672,128]{1,0:T(8,128)S(1)} %collective-permute-done.13.left_ref, f32[288,128]{1,0:T(8,128)S(1)} %collective-permute-done.14.right_ref, f32[288,384]{1,0:T(8,128)S(1)} %get-tuple-element.22.refs_8_.last_ref, ...), custom_call_target="tpu_custom_call" | custom-call | flops 62914560 | bytes 4194304 | tf_op jit(solution)/shard_map/best/pallas_call | solution.py:308
  (8 shorter events, 0.1 us)
Async XLA Ops:
  1.6 14.8 %copy-start = (bf16[1024,128]{1,0:T(8,128)(2,1)S(1)}, bf16[1024,128]{1,0:T(8,128)(2,1)}, u32[]{:S(2)}) copy-start(bf16[1024,128]{1,0:T(8,128)(2,1)} %param.4) | copy-start | bytes 786436
  1.6 41.6 %all-to-all-start = ((bf16[16,8,2048]{2,1,0:T(8,128)(2,1)}), bf16[16,8,2048]{2,1,0:T(8,128)(2,1)S(1)}, u32[]{:S(2)}, u32[]{:S(2)}) async-start(bf16[16,8,2048]{2,1,0:T(8,128)(2,1)} %broadcast_in_dim.15), calls=%async_computation | async-start | bytes 1048576 | tf_op jit(solution)/shard_map/all_to_all | solution.py:45
  16.4 17.9 %collective-permute-start.10 = (bf16[1024,128]{1,0:T(8,128)(2,1)S(1)}, bf16[1024,128]{1,0:T(8,128)(2,1)S(1)}, u32[]{:S(2)}, u32[]{:S(2)}) collective-permute-start(bf16[1024,128]{1,0:T(8,128)(2,1)S(1)} %copy-done), channel_id=1, source_target_pairs={{0,64},{32,96},{64,0},{96,32},{128,192},{160,224},{192,128},{224,1... | collective-permute-start | bytes 786440 | tf_op jit(solution)/shard_map/ppermute | solution.py:46
  21.1 16.9 %collective-permute-start.9 = (bf16[1024,128]{1,0:T(8,128)(2,1)S(1)}, bf16[1024,128]{1,0:T(8,128)(2,1)S(1)}, u32[]{:S(2)}, u32[]{:S(2)}) collective-permute-start(bf16[1024,128]{1,0:T(8,128)(2,1)S(1)} %copy-done), channel_id=1, source_target_pairs={{0,384},{32,416},{64,448},{96,480},{128,0},{160,32},{192,64},{224,... | collective-permute-start | bytes 786440 | tf_op jit(solution)/shard_map/ppermute | solution.py:46
  23.4 19.9 %collective-permute-start.8 = (bf16[1024,128]{1,0:T(8,128)(2,1)S(1)}, bf16[1024,128]{1,0:T(8,128)(2,1)S(1)}, u32[]{:S(2)}, u32[]{:S(2)}) collective-permute-start(bf16[1024,128]{1,0:T(8,128)(2,1)S(1)} %copy-done), channel_id=1, source_target_pairs={{0,128},{32,160},{64,192},{96,224},{128,256},{160,288},{192,320},{... | collective-permute-start | bytes 786440 | tf_op jit(solution)/shard_map/ppermute | solution.py:46
  27.6 20.1 %collective-permute-start.4 = (bf16[1024,128]{1,0:T(8,128)(2,1)S(1)}, bf16[1024,128]{1,0:T(8,128)(2,1)S(1)}, u32[]{:S(2)}, u32[]{:S(2)}) collective-permute-start(bf16[1024,128]{1,0:T(8,128)(2,1)S(1)} %copy-done), channel_id=1, source_target_pairs={{0,320},{32,352},{64,256},{96,288},{128,448},{160,480},{192,384},{... | collective-permute-start | bytes 786440 | tf_op jit(solution)/shard_map/ppermute | solution.py:46
  29.5 23.6 %collective-permute-start.3 = (bf16[1024,128]{1,0:T(8,128)(2,1)S(1)}, bf16[1024,128]{1,0:T(8,128)(2,1)S(1)}, u32[]{:S(2)}, u32[]{:S(2)}) collective-permute-start(bf16[1024,128]{1,0:T(8,128)(2,1)S(1)} %copy-done), channel_id=1, source_target_pairs={{0,256},{32,288},{64,320},{96,352},{128,384},{160,416},{192,448},{... | collective-permute-start | bytes 786440 | tf_op jit(solution)/shard_map/ppermute | solution.py:46
  34.3 23.0 %collective-permute-start.2 = (bf16[1024,128]{1,0:T(8,128)(2,1)S(1)}, bf16[1024,128]{1,0:T(8,128)(2,1)S(1)}, u32[]{:S(2)}, u32[]{:S(2)}) collective-permute-start(bf16[1024,128]{1,0:T(8,128)(2,1)S(1)} %copy-done), channel_id=1, source_target_pairs={{0,448},{32,480},{64,384},{96,416},{128,64},{160,96},{192,0},{224,... | collective-permute-start | bytes 786440 | tf_op jit(solution)/shard_map/ppermute | solution.py:46
  38.0 5.4 %copy-start.3 = (bf16[1024,128]{1,0:T(8,128)(2,1)}, bf16[1024,128]{1,0:T(8,128)(2,1)S(1)}, u32[]{:S(2)}) copy-start(bf16[1024,128]{1,0:T(8,128)(2,1)S(1)} %collective-permute-done.9) | copy-start | bytes 786436
  38.0 19.4 %collective-permute-start.1 = (bf16[1024,128]{1,0:T(8,128)(2,1)S(1)}, bf16[1024,128]{1,0:T(8,128)(2,1)}, u32[]{:S(2)}, u32[]{:S(2)}) collective-permute-start(bf16[1024,128]{1,0:T(8,128)(2,1)S(1)} %copy-done), channel_id=1, source_target_pairs={{0,192},{32,224},{64,128},{96,160},{128,320},{160,352},{192,256},{... | collective-permute-start | bytes 786440 | tf_op jit(solution)/shard_map/ppermute | solution.py:46
  43.3 3.1 %copy-start.4 = (bf16[1024,128]{1,0:T(8,128)(2,1)}, bf16[1024,128]{1,0:T(8,128)(2,1)S(1)}, u32[]{:S(2)}) copy-start(bf16[1024,128]{1,0:T(8,128)(2,1)S(1)} %collective-permute-done.8) | copy-start | bytes 786436
  43.3 16.0 %collective-permute-start.5 = (bf16[8,8,2048]{2,1,0:T(8,128)(2,1)S(1)}, bf16[8,8,2048]{2,1,0:T(8,128)(2,1)S(1)}, u32[]{:S(2)}, u32[]{:S(2)}) collective-permute-start(bf16[8,8,2048]{2,1,0:T(8,128)(2,1)S(1)} %get-tuple-element.26), channel_id=1, source_target_pairs={{0,1},{1,0},{2,3},{3,2},{4,5},{5,4},{6,7},{7,6},{8,9},{9,8},{10,11... | collective-permute-start | bytes 786440 | tf_op jit(solution)/shard_map/ppermute | solution.py:49
  47.7 26.1 %collective-permute-start.11 = (bf16[4,1024,128]{2,1,0:T(8,128)(2,1)S(1)}, bf16[4,1024,128]{2,1,0:T(8,128)(2,1)}, u32[]{:S(2)}, u32[]{:S(2)}) collective-permute-start(bf16[4,1024,128]{2,1,0:T(8,128)(2,1)S(1)} %pad_maximum_fusion.1.refs_4_), channel_id=1, source_target_pairs={{0,32},{32,0},{64,96},{96,64},{128,160},{160,128},{192,224},{224,1... | collective-permute-start | bytes 3145736 | tf_op jit(solution)/shard_map/ppermute | solution.py:53
  53.1 4.3 %copy-start.1 = (bf16[1024,128]{1,0:T(8,128)(2,1)}, bf16[1024,128]{1,0:T(8,128)(2,1)S(1)}, u32[]{:S(2)}) copy-start(bf16[1024,128]{1,0:T(8,128)(2,1)S(1)} %collective-permute-done.3) | copy-start | bytes 786436
  53.1 6.2 %collective-permute-start.6 = (bf16[2,8,2048]{2,1,0:T(8,128)(2,1)S(1)}, bf16[2,8,2048]{2,1,0:T(8,128)(2,1)S(1)}, u32[]{:S(2)}, u32[]{:S(2)}) collective-permute-start(bf16[2,8,2048]{2,1,0:T(8,128)(2,1)S(1)} %slice.18), channel_id=1, source_target_pairs={{0,32},{32,64},{64,96},{96,128},{128,160},{160,192},{192,224},{224... | collective-permute-start | bytes 196616 | tf_op jit(solution)/shard_map/ppermute | solution.py:48
  57.4 0.7 copy-start.2
  59.3 14.5 %collective-permute-start.12 = (bf16[4,1024,128]{2,1,0:T(8,128)(2,1)S(1)}, bf16[4,1024,128]{2,1,0:T(8,128)(2,1)}, u32[]{:S(2)}, u32[]{:S(2)}) collective-permute-start(bf16[4,1024,128]{2,1,0:T(8,128)(2,1)S(1)} %pad_maximum_fusion.refs_5_), channel_id=1, source_target_pairs={{0,32},{32,0},{64,96},{96,64},{128,160},{160,128},{192,224},{224,1... | collective-permute-start | bytes 3145736 | tf_op jit(solution)/shard_map/ppermute | solution.py:53
  63.9 9.8 %collective-permute-start = (bf16[8,8,2048]{2,1,0:T(8,128)(2,1)S(1)}, bf16[8,8,2048]{2,1,0:T(8,128)(2,1)S(1)}, u32[]{:S(2)}, u32[]{:S(2)}) collective-permute-start(bf16[8,8,2048]{2,1,0:T(8,128)(2,1)S(1)} %get-tuple-element.25), channel_id=1, source_target_pairs={{0,1},{1,0},{2,3},{3,2},{4,5},{5,4},{6,7},{7,6},{8,9},{9,8},{10,11... | collective-permute-start | bytes 786440 | tf_op jit(solution)/shard_map/ppermute | solution.py:49
  67.2 6.6 %collective-permute-start.7 = (bf16[2,8,2048]{2,1,0:T(8,128)(2,1)S(1)}, bf16[2,8,2048]{2,1,0:T(8,128)(2,1)S(1)}, u32[]{:S(2)}, u32[]{:S(2)}) collective-permute-start(bf16[2,8,2048]{2,1,0:T(8,128)(2,1)S(1)} %slice.19), channel_id=1, source_target_pairs={{0,32},{32,64},{64,96},{96,128},{128,160},{160,192},{192,224},{224... | collective-permute-start | bytes 196616 | tf_op jit(solution)/shard_map/ppermute | solution.py:50
  76.6 3.1 %copy-start.5 = (s32[8]{0:T(128)S(1)}, s32[8]{0:T(128)}, u32[]{:S(2)}) copy-start(s32[8]{0:T(128)} %param.5) | copy-start | bytes 100
  76.6 15.9 %collective-permute-start.13 = (f32[672,128]{1,0:T(8,128)S(1)}, f32[672,128]{1,0:T(8,128)S(1)}, u32[]{:S(2)}, u32[]{:S(2)}) collective-permute-start(f32[672,128]{1,0:T(8,128)S(1)} %get-tuple-element.20), channel_id=1, source_target_pairs={{0,1},{1,2},{2,3},{3,4},{4,5},{5,6},{6,7},{7,8},{8,9},{9,10},{10,1... | collective-permute-start | bytes 1032200 | tf_op jit(solution)/shard_map/ppermute | solution.py:290
  79.8 12.8 %collective-permute-start.14 = (f32[288,128]{1,0:T(8,128)S(1)}, f32[288,128]{1,0:T(8,128)S(1)}, u32[]{:S(2)}, u32[]{:S(2)}) collective-permute-start(f32[288,128]{1,0:T(8,128)S(1)} %get-tuple-element.21.refs_9_.lead_ref), channel_id=1, source_target_pairs={{1,0},{2,1},{3,2},{4,3},{5,4},{6,5},{7,6},{8,7},{9,8},{10,9},{11,1... | collective-permute-start | bytes 442376 | tf_op jit(solution)/shard_map/ppermute | solution.py:291
